TPU v7x, 32 devices: a whole 2x2x4 slice. The times are simulated.
32 devices in a mesh: stack: 2 (over x), lat: 16 (over z, y, core).
Axes of the slice: x: 2, y: 2, z: 4, core: 2. Of those that a mesh axis runs over, the one named last changes fastest.
Arguments:
- solution: float32 [8, 1024, 1024], P('stack', 'lat'), parts along dimension 0, may hold values from -10 to 10
- residual: float32 [8, 1024, 1024], P('stack', 'lat'), parts along dimension 0, may hold values from -10 to 10
- gradient: float32 [8, 1024, 1024], P('stack', 'lat'), parts along dimension 0, may hold values from -10 to 10
- direction: float32 [8, 1024, 1024], P('stack', 'lat'), parts along dimension 0, may hold values from -10 to 10
- row_taps: float32 [4, 4, 31], replicated, may hold values from -0.5 to 0.5
- col_taps: float32 [4, 4, 31], replicated, may hold values from -1 to 1
- damping: float32 [1], replicated, may hold values from 0.3 to 3
Outputs:
- new_solution: float32 [8, 1024, 1024], P('stack', 'lat'), parts along dimension 0
- new_residual: float32 [8, 1024, 1024], P('stack', 'lat'), parts along dimension 0
- new_gradient: float32 [8, 1024, 1024], P('stack', 'lat'), parts along dimension 0
- new_direction: float32 [8, 1024, 1024], P('stack', 'lat'), parts along dimension 0
There are 2 independent parts, one for each index of `stack`. A program takes and returns all parts, laid end to end along the dimension named above; an argument that names none is the same for every part. Nothing has to cross between parts.
All inputs are finite; a program needn't handle non-finite values.
Results may differ from a plain program's by a relative error of at most 0.000094.
Values sent between devices are 32-bit elements; how exact they have to be, the bound alone decides.
No kernel may reach another device: no remote copies, remote signals or barrier semaphores. Data moves between devices by JAX's collectives and lax.ppermute only.
A program may use at most 64 MiB of HBM per device.

v0:
```python
import jax
import jax.numpy as jnp
from jax import lax
from jax.sharding import PartitionSpec as P


def padded_2(shard, sides, width):
    for axis, dim in sides:
        peers, length = (lax.axis_size(axis), shard.shape[dim])
        up = [(i, (i + 1) % peers) for i in range(peers - 1)]
        down = [(j, i) for i, j in up]
        last = lax.slice_in_dim(shard, length - width, length, axis=dim)
        first = lax.slice_in_dim(shard, 0, width, axis=dim)
        before = lax.ppermute(last, axis, up)
        after = lax.ppermute(first, axis, down)
        shard = jnp.concatenate([before, shard, after], axis=dim)
    return shard


def operate(padded, row_kernel, col_kernel):
    depth = padded.shape[0]
    taps_count = row_kernel.shape[2]
    border = taps_count // 2
    out_rows = padded.shape[1] - (taps_count - 1)
    columns = padded.shape[2]

    def one_source(source, running):
        source_plane = lax.dynamic_index_in_dim(padded, source, 0, keepdims=False)
        widened = jnp.pad(source_plane, ((0, 0), (border, border)))
        row_now = lax.dynamic_index_in_dim(row_kernel, source, 1, keepdims=False)
        col_now = lax.dynamic_index_in_dim(col_kernel, source, 1, keepdims=False)
        along_cols = jnp.zeros((depth, source_plane.shape[0], columns), jnp.float32)
        for offset in range(taps_count):
            along_cols = (
                along_cols
                + col_now[:, offset][:, None, None] * widened[None, :, offset : offset + columns]
            )
        for offset in range(taps_count):
            running = (
                running
                + row_now[:, offset][:, None, None] * along_cols[:, offset : offset + out_rows, :]
            )
        return running

    initial = jnp.zeros((depth, out_rows, columns), jnp.float32)
    return lax.fori_loop(0, depth, one_source, initial)


def body(solution, residual, gradient, direction, row_taps, col_taps, damping):
    border = row_taps.shape[2] // 2
    row_adjoint = jnp.transpose(row_taps, (1, 0, 2))[:, :, ::-1]
    col_adjoint = jnp.transpose(col_taps, (1, 0, 2))[:, :, ::-1]
    damping_value = damping[0]
    gradient_local = jnp.sum(gradient * gradient)
    norm_before = lax.psum(gradient_local, "lat")
    padded_direction = padded_2(direction, (("lat", 1),), border)
    forward_image = operate(padded_direction, row_taps, col_taps)
    image_local = jnp.sum(forward_image * forward_image)
    direction_local = jnp.sum(direction * direction)
    image_total, direction_total = lax.psum((image_local, direction_local), "lat")
    curvature = image_total + damping_value * direction_total
    step_size = norm_before / curvature
    new_solution = solution + step_size * direction
    new_residual = residual - step_size * forward_image
    padded_new = padded_2(new_residual, (("lat", 1),), border)
    new_gradient = operate(padded_new, row_adjoint, col_adjoint) - damping_value * new_solution
    norm_after = lax.psum(jnp.sum(new_gradient * new_gradient), "lat")
    new_direction = new_gradient + norm_after / norm_before * direction
    return (new_solution, new_residual, new_gradient, new_direction)


def solution(mesh):
    placed = (
        P("stack", "lat", None),
        P("stack", "lat", None),
        P("stack", "lat", None),
        P("stack", "lat", None),
        P(),
        P(),
        P(),
    )
    return jax.shard_map(
        body,
        mesh=mesh,
        in_specs=placed,
        out_specs=(
            P("stack", "lat", None),
            P("stack", "lat", None),
            P("stack", "lat", None),
            P("stack", "lat", None),
        ),
        check_vma=False,
    )
```

profile of v0, /device:TPU:0, one launch (start us, length us, event | category | flops | bytes accessed | tf_op | source)
XLA Modules:
  0.0 213.0 jit_solution(11517978408396874967)
XLA Ops:
  1.8 2.4 %collective-permute-start = (f32[4,15,1024]{2,1,0:T(8,128)S(1)}, f32[4,15,1024]{2,1,0:T(8,128)S(1)}, u32[]{:S(2)}, u32[]{:S(2)}) collective-permute-start(f32[4,15,1024]{2,1,0:T(8,128)S(1)} %get-tuple-element.532), channel_id=1, source_target_pairs={{0,1},{1,2},{2,3},{3,4},{4,5},{5,6},{6,7},{7,8},{8,9},{9,10},{10,1... | collective-permute-start | bytes 737288 | tf_op jit(solution)/shard_map/ppermute | solution.py:14
  7.0 2.7 %collective-permute-done.1 = f32[4,15,1024]{2,1,0:T(8,128)S(1)} collective-permute-done((f32[4,15,1024]{2,1,0:T(8,128)S(1)}, f32[4,15,1024]{2,1,0:T(8,128)S(1)}, u32[]{:S(2)}, u32[]{:S(2)}) %collective-permute-start.1) | collective-permute-done | bytes 245792 | tf_op jit(solution)/shard_map/ppermute | solution.py:15
  11.1 58.6 %while.32 = (s32[]{:T(128)}, f32[4,64,1024]{2,1,0:T(8,128)S(1)}, f32[4,4,31]{2,1,0:T(4,128)S(1)}, f32[4,4,31]{2,1,0:T(4,128)S(1)}, f32[4,94,1024]{2,1,0:T(8,128)}, /*index=5*/s32[]{:T(128)}, s32[]{:T(128)}) while((s32[]{:T(128)}, f32[4,64,1024]{2,1,0:T(8,128)S(1)}, f32[4,4,31]{2,1,0:T(4,128)S(1)}, f32[4,4,31]{2,1,0:T(4,128)S(1)}, ...), condition=%wide.region_3.4_spmd.clone, body=%wide.region_2.3_spmd.clone.sunk | while | flops 40001536 | bytes 61174716 | solution.py:46
  12.6 2.0 pad_slice_fusion.65
  16.2 4.3 %multiply_add_fusion.7 = f32[4,94,1024]{2,1,0:T(8,128)S(1)} fusion(f32[94,1024]{1,0:T(8,128)S(1)} %get-tuple-element.781, f32[4]{0:T(128)S(1)} %get-tuple-element.783, f32[94,1024]{1,0:T(8,128)S(1)} %get-tuple-element.784, f32[4]{0:T(128)S(1)} %get-tuple-element.785, f32[94,1024]{1,0:T(8,128)S(1)} %get-tuple-element.786, f32[4]{0:T(128)S(1)} %get-tuple-element.787, ...), kind=kLoop, calls=%fused_computation.clone.1 | loop fusion | flops 23486464 | bytes 13476336 | tf_op jit(solution)/shard_map/while/body/eval_jaxpr/add | solution.py:35
  21.3 4.4 %fusion.66 = f32[4,64,1024]{2,1,0:T(8,128)S(1)} fusion(f32[4,94,1024]{2,1,0:T(8,128)S(1)} %multiply_add_fusion.7, f32[4,64,1024]{2,1,0:T(8,128)S(1)} %get-tuple-element.982, f32[4]{0:T(128)S(1)} %get-tuple-element.844, f32[4]{0:T(128)S(1)} %get-tuple-element.845, f32[4]{0:T(128)S(1)} %get-tuple-element.846, f32[4]{0:T(128)S(1)} %get-tuple-element.847, ...), kind=kLoop, calls=%fused_computation.2.clone.1 | loop fusion | flops 16515072 | bytes 34603504 | tf_op jit(solution)/shard_map/while/body/eval_jaxpr/add | solution.py:40
  27.3 2.0 pad_slice_fusion.65
  30.8 4.3 %multiply_add_fusion.7 = f32[4,94,1024]{2,1,0:T(8,128)S(1)} fusion(f32[94,1024]{1,0:T(8,128)S(1)} %get-tuple-element.781, f32[4]{0:T(128)S(1)} %get-tuple-element.783, f32[94,1024]{1,0:T(8,128)S(1)} %get-tuple-element.784, f32[4]{0:T(128)S(1)} %get-tuple-element.785, f32[94,1024]{1,0:T(8,128)S(1)} %get-tuple-element.786, f32[4]{0:T(128)S(1)} %get-tuple-element.787, ...), kind=kLoop, calls=%fused_computation.clone.1 | loop fusion | flops 23486464 | bytes 13476336 | tf_op jit(solution)/shard_map/while/body/eval_jaxpr/add | solution.py:35
  36.0 4.4 %fusion.66 = f32[4,64,1024]{2,1,0:T(8,128)S(1)} fusion(f32[4,94,1024]{2,1,0:T(8,128)S(1)} %multiply_add_fusion.7, f32[4,64,1024]{2,1,0:T(8,128)S(1)} %get-tuple-element.982, f32[4]{0:T(128)S(1)} %get-tuple-element.844, f32[4]{0:T(128)S(1)} %get-tuple-element.845, f32[4]{0:T(128)S(1)} %get-tuple-element.846, f32[4]{0:T(128)S(1)} %get-tuple-element.847, ...), kind=kLoop, calls=%fused_computation.2.clone.1 | loop fusion | flops 16515072 | bytes 34603504 | tf_op jit(solution)/shard_map/while/body/eval_jaxpr/add | solution.py:40
  41.9 2.0 pad_slice_fusion.65
  45.5 4.3 %multiply_add_fusion.7 = f32[4,94,1024]{2,1,0:T(8,128)S(1)} fusion(f32[94,1024]{1,0:T(8,128)S(1)} %get-tuple-element.781, f32[4]{0:T(128)S(1)} %get-tuple-element.783, f32[94,1024]{1,0:T(8,128)S(1)} %get-tuple-element.784, f32[4]{0:T(128)S(1)} %get-tuple-element.785, f32[94,1024]{1,0:T(8,128)S(1)} %get-tuple-element.786, f32[4]{0:T(128)S(1)} %get-tuple-element.787, ...), kind=kLoop, calls=%fused_computation.clone.1 | loop fusion | flops 23486464 | bytes 13476336 | tf_op jit(solution)/shard_map/while/body/eval_jaxpr/add | solution.py:35
  50.6 4.4 %fusion.66 = f32[4,64,1024]{2,1,0:T(8,128)S(1)} fusion(f32[4,94,1024]{2,1,0:T(8,128)S(1)} %multiply_add_fusion.7, f32[4,64,1024]{2,1,0:T(8,128)S(1)} %get-tuple-element.982, f32[4]{0:T(128)S(1)} %get-tuple-element.844, f32[4]{0:T(128)S(1)} %get-tuple-element.845, f32[4]{0:T(128)S(1)} %get-tuple-element.846, f32[4]{0:T(128)S(1)} %get-tuple-element.847, ...), kind=kLoop, calls=%fused_computation.2.clone.1 | loop fusion | flops 16515072 | bytes 34603504 | tf_op jit(solution)/shard_map/while/body/eval_jaxpr/add | solution.py:40
  56.6 2.0 pad_slice_fusion.65
  60.1 4.3 %multiply_add_fusion.7 = f32[4,94,1024]{2,1,0:T(8,128)S(1)} fusion(f32[94,1024]{1,0:T(8,128)S(1)} %get-tuple-element.781, f32[4]{0:T(128)S(1)} %get-tuple-element.783, f32[94,1024]{1,0:T(8,128)S(1)} %get-tuple-element.784, f32[4]{0:T(128)S(1)} %get-tuple-element.785, f32[94,1024]{1,0:T(8,128)S(1)} %get-tuple-element.786, f32[4]{0:T(128)S(1)} %get-tuple-element.787, ...), kind=kLoop, calls=%fused_computation.clone.1 | loop fusion | flops 23486464 | bytes 13476336 | tf_op jit(solution)/shard_map/while/body/eval_jaxpr/add | solution.py:35
  65.3 4.4 %fusion.66 = f32[4,64,1024]{2,1,0:T(8,128)S(1)} fusion(f32[4,94,1024]{2,1,0:T(8,128)S(1)} %multiply_add_fusion.7, f32[4,64,1024]{2,1,0:T(8,128)S(1)} %get-tuple-element.982, f32[4]{0:T(128)S(1)} %get-tuple-element.844, f32[4]{0:T(128)S(1)} %get-tuple-element.845, f32[4]{0:T(128)S(1)} %get-tuple-element.846, f32[4]{0:T(128)S(1)} %get-tuple-element.847, ...), kind=kLoop, calls=%fused_computation.2.clone.1 | loop fusion | flops 16515072 | bytes 34603504 | tf_op jit(solution)/shard_map/while/body/eval_jaxpr/add | solution.py:40
  69.7 2.2 %multiply_reduce_fusion.2 = (f32[]{:T(128)}, f32[]{:T(128)}) fusion(f32[4,64,1024]{2,1,0:T(8,128)S(1)} %get-tuple-element.268, f32[4,64,1024]{2,1,0:T(8,128)} %param.13), kind=kLoop, calls=%fused_computation.324 | loop fusion | flops 1048574 | bytes 2097160 | tf_op jit(solution)/shard_map/reduce_sum | solution.py:58
  71.9 34.9 %all-reduce.2 = (f32[]{:T(128)}, f32[]{:T(128)}, f32[]{:T(128)}) all-reduce(f32[]{:T(128)} %get-tuple-element.535, f32[]{:T(128)} %get-tuple-element.534, f32[]{:T(128)} %multiply_reduce_fusion.1), channel_id=1, replica_groups=mesh['stack'=2,'lat'=16] {'lat'}, use_global_device_ids=true, to_apply=%region_1.0 | all-reduce | flops 3 | bytes 24 | tf_op jit(solution)/shard_map/psum | solution.py:55
  115.1 58.6 %while.33 = (s32[]{:T(128)}, f32[4,64,1024]{2,1,0:T(8,128)S(1)}, f32[4,4,31]{2,0,1:T(4,128)S(1)}, f32[4,4,31]{2,0,1:T(4,128)S(1)}, f32[4,94,1024]{2,1,0:T(8,128)}, /*index=5*/s32[]{:T(128)}, s32[]{:T(128)}) while((s32[]{:T(128)}, f32[4,64,1024]{2,1,0:T(8,128)S(1)}, f32[4,4,31]{2,0,1:T(4,128)S(1)}, f32[4,4,31]{2,0,1:T(4,128)S(1)}, ...), condition=%wide.region_9.10_spmd.clone, body=%wide.region_8.9_spmd.clone.sunk | while | flops 40001536 | bytes 61174716 | solution.py:46
  116.7 2.0 pad_slice_fusion.67
  120.2 4.3 %multiply_add_fusion.8 = f32[4,94,1024]{2,1,0:T(8,128)S(1)} fusion(f32[94,1024]{1,0:T(8,128)S(1)} %get-tuple-element.880, f32[4]{0:T(128)S(1)} %get-tuple-element.882, f32[94,1024]{1,0:T(8,128)S(1)} %get-tuple-element.883, f32[4]{0:T(128)S(1)} %get-tuple-element.884, f32[94,1024]{1,0:T(8,128)S(1)} %get-tuple-element.885, ...), kind=kLoop, calls=%fused_computation.158.clone.1 | loop fusion | flops 23486464 | bytes 13476336 | tf_op jit(solution)/shard_map/while/body/eval_jaxpr/add | solution.py:35
  125.4 4.4 %fusion.67 = f32[4,64,1024]{2,1,0:T(8,128)S(1)} fusion(f32[4,94,1024]{2,1,0:T(8,128)S(1)} %multiply_add_fusion.8, f32[4,64,1024]{2,1,0:T(8,128)S(1)} %get-tuple-element.1003, f32[4]{0:T(128)S(1)} %get-tuple-element.943, f32[4]{0:T(128)S(1)} %get-tuple-element.944, f32[4]{0:T(128)S(1)} %get-tuple-element.945, f32[4]{0:T(128)S(1)} %get-tuple-element.946, ...), kind=kLoop, calls=%fused_computation.160.clone.1 | loop fusion | flops 16515072 | bytes 34603504 | tf_op jit(solution)/shard_map/while/body/eval_jaxpr/add | solution.py:40
  131.3 2.0 pad_slice_fusion.67
  134.8 4.3 %multiply_add_fusion.8 = f32[4,94,1024]{2,1,0:T(8,128)S(1)} fusion(f32[94,1024]{1,0:T(8,128)S(1)} %get-tuple-element.880, f32[4]{0:T(128)S(1)} %get-tuple-element.882, f32[94,1024]{1,0:T(8,128)S(1)} %get-tuple-element.883, f32[4]{0:T(128)S(1)} %get-tuple-element.884, f32[94,1024]{1,0:T(8,128)S(1)} %get-tuple-element.885, ...), kind=kLoop, calls=%fused_computation.158.clone.1 | loop fusion | flops 23486464 | bytes 13476336 | tf_op jit(solution)/shard_map/while/body/eval_jaxpr/add | solution.py:35
  140.0 4.4 %fusion.67 = f32[4,64,1024]{2,1,0:T(8,128)S(1)} fusion(f32[4,94,1024]{2,1,0:T(8,128)S(1)} %multiply_add_fusion.8, f32[4,64,1024]{2,1,0:T(8,128)S(1)} %get-tuple-element.1003, f32[4]{0:T(128)S(1)} %get-tuple-element.943, f32[4]{0:T(128)S(1)} %get-tuple-element.944, f32[4]{0:T(128)S(1)} %get-tuple-element.945, f32[4]{0:T(128)S(1)} %get-tuple-element.946, ...), kind=kLoop, calls=%fused_computation.160.clone.1 | loop fusion | flops 16515072 | bytes 34603504 | tf_op jit(solution)/shard_map/while/body/eval_jaxpr/add | solution.py:40
  145.9 2.0 pad_slice_fusion.67
  149.5 4.3 %multiply_add_fusion.8 = f32[4,94,1024]{2,1,0:T(8,128)S(1)} fusion(f32[94,1024]{1,0:T(8,128)S(1)} %get-tuple-element.880, f32[4]{0:T(128)S(1)} %get-tuple-element.882, f32[94,1024]{1,0:T(8,128)S(1)} %get-tuple-element.883, f32[4]{0:T(128)S(1)} %get-tuple-element.884, f32[94,1024]{1,0:T(8,128)S(1)} %get-tuple-element.885, ...), kind=kLoop, calls=%fused_computation.158.clone.1 | loop fusion | flops 23486464 | bytes 13476336 | tf_op jit(solution)/shard_map/while/body/eval_jaxpr/add | solution.py:35
  154.7 4.4 %fusion.67 = f32[4,64,1024]{2,1,0:T(8,128)S(1)} fusion(f32[4,94,1024]{2,1,0:T(8,128)S(1)} %multiply_add_fusion.8, f32[4,64,1024]{2,1,0:T(8,128)S(1)} %get-tuple-element.1003, f32[4]{0:T(128)S(1)} %get-tuple-element.943, f32[4]{0:T(128)S(1)} %get-tuple-element.944, f32[4]{0:T(128)S(1)} %get-tuple-element.945, f32[4]{0:T(128)S(1)} %get-tuple-element.946, ...), kind=kLoop, calls=%fused_computation.160.clone.1 | loop fusion | flops 16515072 | bytes 34603504 | tf_op jit(solution)/shard_map/while/body/eval_jaxpr/add | solution.py:40
  160.6 2.0 pad_slice_fusion.67
  164.1 4.3 %multiply_add_fusion.8 = f32[4,94,1024]{2,1,0:T(8,128)S(1)} fusion(f32[94,1024]{1,0:T(8,128)S(1)} %get-tuple-element.880, f32[4]{0:T(128)S(1)} %get-tuple-element.882, f32[94,1024]{1,0:T(8,128)S(1)} %get-tuple-element.883, f32[4]{0:T(128)S(1)} %get-tuple-element.884, f32[94,1024]{1,0:T(8,128)S(1)} %get-tuple-element.885, ...), kind=kLoop, calls=%fused_computation.158.clone.1 | loop fusion | flops 23486464 | bytes 13476336 | tf_op jit(solution)/shard_map/while/body/eval_jaxpr/add | solution.py:35
  169.3 4.4 %fusion.67 = f32[4,64,1024]{2,1,0:T(8,128)S(1)} fusion(f32[4,94,1024]{2,1,0:T(8,128)S(1)} %multiply_add_fusion.8, f32[4,64,1024]{2,1,0:T(8,128)S(1)} %get-tuple-element.1003, f32[4]{0:T(128)S(1)} %get-tuple-element.943, f32[4]{0:T(128)S(1)} %get-tuple-element.944, f32[4]{0:T(128)S(1)} %get-tuple-element.945, f32[4]{0:T(128)S(1)} %get-tuple-element.946, ...), kind=kLoop, calls=%fused_computation.160.clone.1 | loop fusion | flops 16515072 | bytes 34603504 | tf_op jit(solution)/shard_map/while/body/eval_jaxpr/add | solution.py:40
  173.7 3.5 %multiply_reduce_fusion = (f32[]{:T(128)}, f32[4,64,1024]{2,1,0:T(8,128)S(1)}, f32[4,64,1024]{2,1,0:T(8,128)}) fusion(f32[4,64,1024]{2,1,0:T(8,128)S(1)} %get-tuple-element.269, f32[]{:T(128)} %bitcast.28, f32[4,64,1024]{2,1,0:T(8,128)} %param.11, f32[4,64,1024]{2,1,0:T(8,128)} %param.14, f32[]{:T(128)S(6)} %div.6), kind=kLoop, calls=%fused_computation.319 | loop fusion | flops 1572863 | bytes 5242892 | tf_op jit(solution)/shard_map/reduce_sum | solution.py:67
  177.3 33.3 %psum.31 = f32[]{:T(128)} all-reduce(f32[]{:T(128)} %get-tuple-element.463), channel_id=1, replica_groups=mesh['stack'=2,'lat'=16] {'lat'}, use_global_device_ids=true, to_apply=%region_11.12 | all-reduce | flops 1 | bytes 8 | tf_op jit(solution)/shard_map/psum | solution.py:67
  (87 shorter events, 43.3 us)
Async XLA Ops:
  0.6 5.5 %copy-start = (f32[4,64,1024]{2,1,0:T(8,128)S(1)}, f32[4,64,1024]{2,1,0:T(8,128)}, u32[]{:S(2)}) copy-start(f32[4,64,1024]{2,1,0:T(8,128)} %param.14) | copy-start | bytes 3145732
  1.8 5.2 %collective-permute-start = (f32[4,15,1024]{2,1,0:T(8,128)S(1)}, f32[4,15,1024]{2,1,0:T(8,128)S(1)}, u32[]{:S(2)}, u32[]{:S(2)}) collective-permute-start(f32[4,15,1024]{2,1,0:T(8,128)S(1)} %get-tuple-element.532), channel_id=1, source_target_pairs={{0,1},{1,2},{2,3},{3,4},{4,5},{5,6},{6,7},{7,8},{8,9},{9,10},{10,1... | collective-permute-start | bytes 737288 | tf_op jit(solution)/shard_map/ppermute | solution.py:14
  4.2 5.5 %collective-permute-start.1 = (f32[4,15,1024]{2,1,0:T(8,128)S(1)}, f32[4,15,1024]{2,1,0:T(8,128)S(1)}, u32[]{:S(2)}, u32[]{:S(2)}) collective-permute-start(f32[4,15,1024]{2,1,0:T(8,128)S(1)} %get-tuple-element.533), channel_id=1, source_target_pairs={{1,0},{2,1},{3,2},{4,3},{5,4},{6,5},{7,6},{8,7},{9,8},{10,9},{11,1... | collective-permute-start | bytes 737288 | tf_op jit(solution)/shard_map/ppermute | solution.py:15
  7.0 4.1 %copy-start.5 = (f32[4,4,31]{2,1,0:T(4,128)S(1)}, f32[4,4,31]{2,1,0:T(4,128)}, u32[]{:S(2)}) copy-start(f32[4,4,31]{2,1,0:T(4,128)} %param.15) | copy-start | bytes 5956
  7.0 4.1 %copy-start.6 = (f32[4,4,31]{2,1,0:T(4,128)S(1)}, f32[4,4,31]{2,1,0:T(4,128)}, u32[]{:S(2)}) copy-start(f32[4,4,31]{2,1,0:T(4,128)} %param.16) | copy-start | bytes 5956
  69.7 39.1 %copy-start.4 = (f32[4,64,1024]{2,1,0:T(8,128)S(1)}, f32[4,64,1024]{2,1,0:T(8,128)}, u32[]{:S(2)}) copy-start(f32[4,64,1024]{2,1,0:T(8,128)} %param.12) | copy-start | bytes 3145732
  109.0 6.2 %copy-start.2 = (f32[4,64,1024]{2,1,0:T(8,128)}, f32[4,64,1024]{2,1,0:T(8,128)S(1)}, u32[]{:S(2)}) copy-start(f32[4,64,1024]{2,1,0:T(8,128)S(1)} %multiply_subtract_fusion.1) | copy-start | bytes 3145732
  109.1 3.0 %collective-permute-start.2 = (f32[4,15,1024]{2,1,0:T(8,128)S(1)}, f32[4,15,1024]{2,1,0:T(8,128)S(1)}, u32[]{:S(2)}, u32[]{:S(2)}) collective-permute-start(f32[4,15,1024]{2,1,0:T(8,128)S(1)} %get-tuple-element.530), channel_id=1, source_target_pairs={{0,1},{1,2},{2,3},{3,4},{4,5},{5,6},{6,7},{7,8},{8,9},{9,10},{10,1... | collective-permute-start | bytes 737288 | tf_op jit(solution)/shard_map/ppermute | solution.py:14
  110.4 3.4 %collective-permute-start.3 = (f32[4,15,1024]{2,1,0:T(8,128)S(1)}, f32[4,15,1024]{2,1,0:T(8,128)S(1)}, u32[]{:S(2)}, u32[]{:S(2)}) collective-permute-start(f32[4,15,1024]{2,1,0:T(8,128)S(1)} %get-tuple-element.531), channel_id=1, source_target_pairs={{1,0},{2,1},{3,2},{4,3},{5,4},{6,5},{7,6},{8,7},{9,8},{10,9},{11,1... | collective-permute-start | bytes 737288 | tf_op jit(solution)/shard_map/ppermute | solution.py:15
  173.7 38.1 %copy-start.1 = (f32[4,64,1024]{2,1,0:T(8,128)S(1)}, f32[4,64,1024]{2,1,0:T(8,128)}, u32[]{:S(2)}) copy-start(f32[4,64,1024]{2,1,0:T(8,128)} %param.14) | copy-start | bytes 3145732
  177.3 35.8 %copy-start.3 = (f32[4,64,1024]{2,1,0:T(8,128)}, f32[4,64,1024]{2,1,0:T(8,128)S(1)}, u32[]{:S(2)}) copy-start(f32[4,64,1024]{2,1,0:T(8,128)S(1)} %get-tuple-element.464) | copy-start | bytes 3145732
where the time goes:
time: 214 us; the launch traced here: 213 us
  other arithmetic  80.3 us (38%)
  blocking collectives  68.2 us (32%)
  local copies, waits for them, and re-layouts  48.5 us (23%)
  starting transfers between devices  6.44 us (3%)
  between operations  4.7 us (2%)
  waiting for transfers between devices  4.46 us (2%)
    add x8, other arithmetic, one_source(): running + row_now[:, offset][:, None, None] * along_cols[:, offset:offset...  35.2 us
    psum x1, blocking collectives, body(): norm_before = lax.psum(gradient_local, 'lat')  34.9 us
    add x8, other arithmetic, one_source(): along_cols + col_now[:, offset][:, None, None] * widened[None, :, offset:...  34.5 us
    psum x1, blocking collectives, body(): norm_after = lax.psum(jnp.sum(new_gradient * new_gradient), 'lat')  33.3 us
    slice x16, local copies, waits for them, and re-layouts, one_source(): widened[None, :, offset:offset + columns]  25.4 us
    squeeze x8, local copies, waits for them, and re-layouts, one_source(): source_plane = lax.dynamic_index_in_dim(padded, source, 0, keepdims=False)  8.23 us
    slice x16, local copies, waits for them, and re-layouts, one_source(): row_now[:, offset][:, None, None]  6.72 us
    slice x16, local copies, waits for them, and re-layouts, one_source(): col_now[:, offset][:, None, None]  6.69 us
  transfers between devices with their start and end apart: 4, of which 2 were waited for; matrix products, arithmetic and copies ran while one was open for 0% of the time, Pallas kernels for 0%

commit v1 on v0

v1 whole, which is shorter than its diff:
```python
import functools

import jax
import jax.numpy as jnp
from jax import lax
from jax.experimental import pallas as pl
from jax.experimental.pallas import tpu as pltpu
from jax.sharding import PartitionSpec as P

F32 = jnp.float32
BF16 = jnp.bfloat16
EDGE = 16
LANE = 128
PAD = 128
VM = pl.BlockSpec(memory_space=pltpu.VMEM)
SM = pl.BlockSpec(memory_space=pltpu.SMEM)
LIMIT = 40 * 2**20


def split(x):
    hi = x.astype(BF16)
    return hi, (x - hi.astype(F32)).astype(BF16)


def params():
    return pltpu.CompilerParams(vmem_limit_bytes=LIMIT)


def cost(flops, moved):
    return pl.CostEstimate(flops=int(flops), bytes_accessed=int(moved), transcendentals=0)


def row_base(taps, gap):
    hi = lax.reduce_precision(taps, 8, 7)
    lo = taps - hi
    place = lambda t, at: jnp.pad(t, ((0, 0), (0, 0), (at, 256 - at - t.shape[2])))
    return place(hi, 0) + place(hi, gap) + place(lo, 2 * gap)


def col_base(taps):
    hi = lax.reduce_precision(taps, 8, 7)
    lo = taps - hi
    count = taps.shape[2]

    def place(t):
        wide = jnp.pad(t[:, :, ::-1], ((0, 0), (0, 0), (0, 256 - count)))
        return jnp.roll(wide, 1 - count, axis=2)

    return place(hi), jnp.roll(place(lo), LANE, axis=2)


def prep_kernel(depth, inner, taps_e, taps_l, col_hi, col_lo, r_early, r_late, c_out):
    window = 160
    lane = lax.broadcasted_iota(jnp.int32, (window, 256), 1)
    for o in range(depth):
        for s in range(depth):
            base = jnp.broadcast_to(taps_e[o, pl.ds(s, 1), :], (inner, 256))
            rolled = pltpu.roll(base, 1, 1, stride=1, stride_axis=0)
            r_early[s, o * inner:(o + 1) * inner, :] = rolled.astype(BF16)
            base = jnp.broadcast_to(taps_l[o, pl.ds(s, 1), :], (EDGE, 256))
            rolled = pltpu.roll(base, 1, 1, stride=1, stride_axis=0)
            r_late[s, o * EDGE:(o + 1) * EDGE, :] = rolled.astype(BF16)
            hi = jnp.broadcast_to(col_hi[o, pl.ds(s, 1), :], (window, 256))
            lo = jnp.broadcast_to(col_lo[o, pl.ds(s, 1), :], (window, 256))
            hi = pltpu.roll(hi, 0, 1, stride=1, stride_axis=0)
            lo = pltpu.roll(lo, 0, 1, stride=1, stride_axis=0)
            c_out[o, s * 256:s * 256 + window, :] = jnp.where(lane < LANE, hi, lo).astype(BF16)
            c_out[o, s * 256 + window:(s + 1) * 256, :] = jnp.zeros((256 - window, 256), BF16)


def prep(row, col, inner):
    depth = row.shape[0]
    hi, lo = col_base(col)
    return pl.pallas_call(
        functools.partial(prep_kernel, depth, inner),
        out_shape=(
            jax.ShapeDtypeStruct((depth, depth * inner, 256), BF16),
            jax.ShapeDtypeStruct((depth, depth * EDGE, 256), BF16),
            jax.ShapeDtypeStruct((depth, depth * 256, 256), BF16),
        ),
        in_specs=[VM] * 4,
        out_specs=[VM] * 3,
        compiler_params=params(),
        name="prep",
    )(row_base(row, inner + 2 * EDGE), row_base(row, 3 * EDGE), hi, lo)


def shifted(x, border):
    wide = jnp.concatenate([x, jnp.zeros((x.shape[0], PAD), F32)], axis=1)
    return split(pltpu.roll(wide, border, 1))


def put(win, at, group, hi, lo):
    rows = hi.shape[0]
    for g, part in enumerate((hi, lo, hi)):
        win[pl.ds(pl.multiple_of(at + g * group, EDGE), rows), :] = part


def along_columns(v_hi, v_lo, c_ref, o, rows, columns, depth):
    tall = []
    for part in (v_hi, v_lo):
        for n in range(columns // LANE):
            tall.append(jnp.concatenate(
                [part[s, o * rows:(o + 1) * rows, n * LANE:n * LANE + 256] for s in range(depth)], axis=1))
    got = jnp.dot(jnp.concatenate(tall, axis=0), c_ref[o], preferred_element_type=F32)
    blocks = columns // LANE
    out = []
    for n in range(blocks):
        top = got[n * rows:(n + 1) * rows]
        low = got[(blocks + n) * rows:(blocks + n + 1) * rows]
        out.append(top[:, :LANE] + (top[:, LANE:] + low[:, :LANE]))
    return jnp.concatenate(out, axis=1)


def early_kernel(border, odd_ref, v_ref, near_ref, r_ref, c_ref, out_ref, win, v_hi, v_lo):
    depth, rows, columns = v_ref.shape
    inner = rows - EDGE
    group = rows + EDGE
    odd = odd_ref[0]
    for s in range(depth):
        win[s, 3 * group:, :] = jnp.zeros((256 - 3 * group, columns + PAD), BF16)
        put(win.at[s], odd * EDGE, group, *shifted(v_ref[s], border))
        put(win.at[s], (1 - odd) * rows, group, *shifted(near_ref[s], border))
        got = jnp.dot(r_ref[s], win[s], preferred_element_type=F32)
        hi, lo = split(got)
        v_hi[s], v_lo[s] = hi, lo
    for o in range(depth):
        out_ref[o] = along_columns(v_hi, v_lo, c_ref, o, inner, columns, depth)


def early(odd, v, near, r, c, border):
    depth, rows, columns = v.shape
    inner = rows - EDGE
    wide = columns + PAD
    return pl.pallas_call(
        functools.partial(early_kernel, border),
        out_shape=jax.ShapeDtypeStruct((depth, inner, columns), F32),
        in_specs=[SM, VM, VM, VM, VM],
        out_specs=VM,
        scratch_shapes=[
            pltpu.VMEM((depth, 256, wide), BF16),
            pltpu.VMEM((depth, depth * inner, wide), BF16),
            pltpu.VMEM((depth, depth * inner, wide), BF16),
        ],
        compiler_params=params(),
        cost_estimate=cost(2 * depth * depth * 2 * inner * 8 * 256 * 256, 8 * 2**20),
        name="early",
    )(odd, v, near, r, c)


def late_kernel(border, odd_ref, v_ref, far_ref, r_ref, c_ref, out_ref, win, v_hi, v_lo):
    depth, rows, columns = v_ref.shape
    group = 3 * EDGE
    odd = odd_ref[0]
    start = pl.multiple_of(odd * (rows - 2 * EDGE), EDGE)
    for s in range(depth):
        win[s, 3 * group:, :] = jnp.zeros((256 - 3 * group, columns + PAD), BF16)
        put(win.at[s], (1 - odd) * EDGE, group, *shifted(v_ref[s, pl.ds(start, 2 * EDGE), :], border))
        put(win.at[s], odd * 2 * EDGE, group, *shifted(far_ref[s], border))
        got = jnp.dot(r_ref[s], win[s], preferred_element_type=F32)
        hi, lo = split(got)
        v_hi[s], v_lo[s] = hi, lo
    for o in range(depth):
        out_ref[o] = along_columns(v_hi, v_lo, c_ref, o, EDGE, columns, depth)


def late(odd, v, far, r, c, border):
    depth, rows, columns = v.shape
    wide = columns + PAD
    return pl.pallas_call(
        functools.partial(late_kernel, border),
        out_shape=jax.ShapeDtypeStruct((depth, EDGE, columns), F32),
        in_specs=[SM, VM, VM, VM, VM],
        out_specs=VM,
        scratch_shapes=[
            pltpu.VMEM((depth, 256, wide), BF16),
            pltpu.VMEM((depth, depth * EDGE, wide), BF16),
            pltpu.VMEM((depth, depth * EDGE, wide), BF16),
        ],
        compiler_params=params(),
        cost_estimate=cost(2 * depth * depth * 2 * EDGE * 8 * 256 * 256, 4 * 2**20),
        name="late",
    )(odd, v, far, r, c)


def total(axis, values):
    peers = lax.axis_size(axis)
    step = 1
    while step < peers:
        values = values + lax.ppermute(values, axis, [(i, i ^ step) for i in range(peers)])
        step *= 2
    return values


def body(solution, residual, gradient, direction, row_taps, col_taps, damping):
    border = row_taps.shape[2] // 2
    depth, rows, columns = direction.shape
    inner = rows - EDGE
    peers = lax.axis_size("lat")
    odd = lax.axis_index("lat") % 2
    odd_arr = jnp.full((1,), odd, jnp.int32)
    near_pairs = [(i, i ^ 1) for i in range(peers)]
    far_pairs = [p for a in range(1, peers - 1, 2) for p in ((a, a + 1), (a + 1, a))]

    def near_far(v):
        far = lax.dynamic_slice_in_dim(v, odd * inner, EDGE, axis=1)
        near = lax.dynamic_slice_in_dim(v, (1 - odd) * inner, EDGE, axis=1)
        return lax.ppermute(near, "lat", near_pairs), lax.ppermute(far, "lat", far_pairs)

    def whole(a, b):
        return jnp.where(odd == 1, jnp.concatenate([a, b], axis=1), jnp.concatenate([b, a], axis=1))

    row_adjoint = jnp.transpose(row_taps, (1, 0, 2))[:, :, ::-1]
    col_adjoint = jnp.transpose(col_taps, (1, 0, 2))[:, :, ::-1]
    damp = damping[0]

    p_near, p_far = near_far(direction)
    r_near, r_far = near_far(residual)
    re, rl, c = prep(row_taps, col_taps, inner)
    rae, ral, ca = prep(row_adjoint, col_adjoint, inner)

    image_in = early(odd_arr, direction, p_near, re, c, border)
    image_out = late(odd_arr, direction, p_far, rl, c, border)
    image = whole(image_in, image_out)
    f_near, f_far = near_far(image)
    g_in = early(odd_arr, residual, r_near, rae, ca, border)
    g_out = late(odd_arr, residual, r_far, ral, ca, border)
    back_r = whole(g_in, g_out) - damp * solution
    h_in = early(odd_arr, image, f_near, rae, ca, border)
    h_out = late(odd_arr, image, f_far, ral, ca, border)
    back_f = whole(h_in, h_out) + damp * direction

    sums = jnp.stack([
        jnp.sum(gradient * gradient),
        jnp.sum(image * image),
        jnp.sum(direction * direction),
        jnp.sum(back_r * back_r),
        jnp.sum(back_r * back_f),
        jnp.sum(back_f * back_f),
    ])
    sums = total("lat", sums)
    norm_before, image_total, direction_total, rr, rf, ff = (sums[k] for k in range(6))
    curvature = image_total + damp * direction_total
    step = norm_before / curvature
    norm_after = rr - step * (2.0 * rf - step * ff)
    new_solution = solution + step * direction
    new_residual = residual - step * image
    new_gradient = back_r - step * back_f
    new_direction = new_gradient + norm_after / norm_before * direction
    return (new_solution, new_residual, new_gradient, new_direction)


def solution(mesh):
    split_rows = P("stack", "lat", None)
    return jax.shard_map(
        body,
        mesh=mesh,
        in_specs=(split_rows,) * 4 + (P(),) * 3,
        out_specs=(split_rows,) * 4,
        check_vma=False,
    )
```

time: 214 us -> 69.8 us (0.33)
  other arithmetic: 80.3 us -> 10 us
  blocking collectives: 68.2 us -> 0 us
  local copies, waits for them, and re-layouts: 48.5 us -> 9.31 us
  Pallas kernels: 0 us -> 14.7 us
  starting transfers between devices: 6.44 us -> 21 us
  waiting for transfers between devices: 4.46 us -> 8.38 us
    add x16 -> x6, other arithmetic: 69.7 us -> 0.23 us  [the longest x2 0.21 us: row_base(): return place(hi, 0) + place(hi, gap) + place(lo, 2 * gap)]
    psum x2 -> x0, blocking collectives: 68.2 us -> none  [the longest x1 34.9 us: body(): norm_before = lax.psum(gradient_local, 'lat')]
    slice x50 -> x15, local copies, waits for them, and re-layouts: 40 us -> 1.78 us  [the longest x12 0.97 us: place(): return jnp.roll(wide, 1 - count, axis=2)]
    pallas_call x0 -> x8, Pallas kernels: none -> 14.7 us  [the longest x3 9.2 us: early(): pl.pallas_call(functools.partial(early_kernel, border), out_shape=jax.Sha...]
    ppermute x4 -> x10, starting transfers between devices: 6.44 us -> 21 us  [the longest x3 14.6 us: near_far(): lax.ppermute(near, 'lat', near_pairs)]
    squeeze x12 -> x0, local copies, waits for them, and re-layouts: 8.25 us -> none  [the longest x8 8.23 us: one_source(): source_plane = lax.dynamic_index_in_dim(padded, source, 0, keepdims=False)]
    ppermute x4 -> x10, waiting for transfers between devices: 4.46 us -> 8.38 us  [the longest x4 8.37 us: total(): lax.ppermute(values, axis, [(i, i ^ step) for i in range(peers)])]
    another operation x0 -> x1, local copies, waits for them, and re-layouts: none -> 3.79 us  [body(): jnp.stack([jnp.sum(gradient * gradient), jnp.sum(image * image), jnp.sum(...]
  transfers between devices with their start and end apart: 4 -> 10, of which waited for: 2 -> 4; matrix products, arithmetic and copies ran while one was open for 0% -> 7% of each run, Pallas kernels for 0% -> 17%
where the time goes in v1:
time: 69.8 us; the launch traced here: 69.4 us
  starting transfers between devices  21 us (30%)
  Pallas kernels  14.7 us (21%)
  other arithmetic  10 us (14%)
  local copies, waits for them, and re-layouts  9.31 us (13%)
  waiting for transfers between devices  8.38 us (12%)
  between operations  5.99 us (9%)
    ppermute x3, starting transfers between devices, near_far(): lax.ppermute(near, 'lat', near_pairs)  14.6 us
    pallas_call x3, Pallas kernels, early(): pl.pallas_call(functools.partial(early_kernel, border), out_shape=jax.Sha...  9.2 us
    ppermute x4, waiting for transfers between devices, total(): lax.ppermute(values, axis, [(i, i ^ step) for i in range(peers)])  8.37 us
    ppermute x4, starting transfers between devices, total(): lax.ppermute(values, axis, [(i, i ^ step) for i in range(peers)])  4.28 us
    add x1, other arithmetic, body(): new_direction = new_gradient + norm_after / norm_before * direction  4.02 us
    pallas_call x3, Pallas kernels, late(): pl.pallas_call(functools.partial(late_kernel, border), out_shape=jax.Shap...  3.96 us
    another operation x1, local copies, waits for them, and re-layouts, body(): jnp.stack([jnp.sum(gradient * gradient), jnp.sum(image * image), jnp.sum(...  3.79 us
    dynamic_slice x3, local copies, waits for them, and re-layouts, near_far(): far = lax.dynamic_slice_in_dim(v, odd * inner, EDGE, axis=1)  3.12 us
  transfers between devices with their start and end apart: 10, of which 4 were waited for; matrix products, arithmetic and copies ran while one was open for 7% of the time, Pallas kernels for 17%

profile of v1, /device:TPU:0, one launch (start us, length us, event | category | flops | bytes accessed | tf_op | source)
XLA Modules:
  0.0 69.4 jit_solution(500826432435368146)
XLA Ops:
  0.7 2.0 %constant_dynamic-slice_fusion.2 = (f32[4,16,1024]{2,1,0:T(8,128)}, f32[4,16,1024]{2,1,0:T(8,128)}) fusion(f32[4,64,1024]{2,1,0:T(8,128)} %v_ref.7, s32[]{:T(128)S(6)} %select_n.36, s32[]{:T(128)S(6)} %select_n.35), kind=kLoop, calls=%fused_computation.43 | loop fusion | bytes 1048584 | tf_op jit(solution)/shard_map/dynamic_slice | solution.py:206
  2.7 0.7 collective-permute-start.3
  3.4 4.4 %collective-permute-start.2 = (f32[4,16,1024]{2,1,0:T(8,128)}, f32[4,16,1024]{2,1,0:T(8,128)}, u32[]{:S(2)}, u32[]{:S(2)}) collective-permute-start(f32[4,16,1024]{2,1,0:T(8,128)} %get-tuple-element.30), channel_id=1, source_target_pairs={{0,1},{1,0},{2,3},{3,2},{4,5},{5,4},{6,7},{7,6},{8,9},{9,8},{10,11... | collective-permute-start | bytes 786440 | tf_op jit(solution)/shard_map/ppermute | solution.py:208
  7.8 1.1 %constant_dynamic-slice_fusion.4 = (f32[4,16,1024]{2,1,0:T(8,128)S(1)}, f32[4,16,1024]{2,1,0:T(8,128)S(1)}) fusion(f32[4,64,1024]{2,1,0:T(8,128)} %v_ref.5, s32[]{:T(128)S(6)} %select_n.36, s32[]{:T(128)S(6)} %select_n.35), kind=kLoop, calls=%fused_computation.45 | loop fusion | bytes 1048584 | tf_op jit(solution)/shard_map/dynamic_slice | solution.py:206
  8.8 0.7 collective-permute-start.1
  9.5 2.9 %collective-permute-start = (f32[4,16,1024]{2,1,0:T(8,128)S(1)}, f32[4,16,1024]{2,1,0:T(8,128)S(1)}, u32[]{:S(2)}, u32[]{:S(2)}) collective-permute-start(f32[4,16,1024]{2,1,0:T(8,128)S(1)} %get-tuple-element.32), channel_id=1, source_target_pairs={{0,1},{1,0},{2,3},{3,2},{4,5},{5,4},{6,7},{7,6},{8,9},{9,8},{10,11... | collective-permute-start | bytes 786440 | tf_op jit(solution)/shard_map/ppermute | solution.py:208
  13.5 0.1 rev.20
  14.2 0.1 fusion.3
  14.3 0.8 %prep.2 = (bf16[4,192,256]{2,1,0:T(8,128)(2,1)S(1)}, bf16[4,64,256]{2,1,0:T(8,128)(2,1)S(1)}, bf16[4,1024,256]{2,1,0:T(8,128)(2,1)S(1)}) custom-call(f32[4,4,256]{2,1,0:T(4,128)S(1)} %get-tuple-element.36.taps_e, f32[4,4,256]{2,1,0:T(4,128)S(1)} %get-tuple-element.35.taps_l, f32[4,4,256]{2,1,0:T(4,128)S(1)} %pad_maximum_fusion.2.col_hi, ...), custom_call_target="tpu_custom_call" | custom-call | tf_op jit(solution)/shard_map/prep/pallas_call | solution.py:74
  15.1 0.1 fusion.5
  15.3 0.9 %multiply_reduce_fusion.5 = f32[]{:T(128)} fusion(f32[4,64,1024]{2,1,0:T(8,128)S(1)} %copy-done.3), kind=kLoop, calls=%fused_computation.14 | loop fusion | flops 524287 | bytes 1048580 | tf_op jit(solution)/shard_map/reduce_sum | solution.py:234
  16.2 1.3 %late.3 = f32[4,16,1024]{2,1,0:T(8,128)S(1)} custom-call(s32[1]{0:T(128)} %bitcast.1.odd_ref, f32[4,64,1024]{2,1,0:T(8,128)S(1)} %copy-done, f32[4,16,1024]{2,1,0:T(8,128)S(1)} %collective-permute-done.1.far_ref, bf16[4,64,256]{2,1,0:T(8,128)(2,1)S(1)} %get-tuple-element.12.r_ref, bf16[4,1024,256]{2,1,0:T(8,128)(2,1)S(1)} %get-tuple-element.11.c_ref), custom_call_target="tpu_custom_call" | custom-call | flops 536870912 | bytes 4194304 | tf_op jit(solution)/shard_map/late/pallas_call | solution.py:170
  17.5 2.7 %early.3 = f32[4,48,1024]{2,1,0:T(8,128)S(1)} custom-call(s32[1]{0:T(128)} %bitcast.1.odd_ref, f32[4,64,1024]{2,1,0:T(8,128)S(1)} %copy-done, f32[4,16,1024]{2,1,0:T(8,128)S(1)} %collective-permute-done.near_ref, bf16[4,192,256]{2,1,0:T(8,128)(2,1)S(1)} %get-tuple-element.10.r_ref, bf16[4,1024,256]{2,1,0:T(8,128)(2,1)S(1)} %get-tuple-element.11.c_ref), custom_call_target="tpu_custom_call" | custom-call | flops 1610612736 | bytes 8388608 | tf_op jit(solution)/shard_map/early/pallas_call | solution.py:135
  20.3 0.9 %multiply_reduce_fusion.4 = (f32[]{:T(128)}, f32[4,64,1024]{2,1,0:T(8,128)S(1)}) fusion(f32[4,48,1024]{2,1,0:T(8,128)S(1)} %early.3, f32[4,16,1024]{2,1,0:T(8,128)S(1)} %late.3, pred[]{:T(512)S(6)} %eq.4), kind=kLoop, calls=%fused_computation.13 | loop fusion | flops 1310719 | bytes 2097157 | tf_op jit(solution)/shard_map/reduce_sum | solution.py:235
  21.3 0.9 %collective-permute-start.5 = (f32[4,16,1024]{2,1,0:T(8,128)S(1)}, f32[4,16,1024]{2,1,0:T(8,128)S(1)}, u32[]{:S(2)}, u32[]{:S(2)}) collective-permute-start(f32[4,16,1024]{2,1,0:T(8,128)S(1)} %get-tuple-element.27), channel_id=1, source_target_pairs={{1,2},{2,1},{3,4},{4,3},{5,6},{6,5},{7,8},{8,7},{9,10},{10,9},{11,... | collective-permute-start | bytes 786440 | tf_op jit(solution)/shard_map/ppermute | solution.py:208
  22.1 7.3 %collective-permute-start.4 = (f32[4,16,1024]{2,1,0:T(8,128)S(1)}, f32[4,16,1024]{2,1,0:T(8,128)S(1)}, u32[]{:S(2)}, u32[]{:S(2)}) collective-permute-start(f32[4,16,1024]{2,1,0:T(8,128)S(1)} %get-tuple-element.28), channel_id=1, source_target_pairs={{0,1},{1,0},{2,3},{3,2},{4,5},{5,4},{6,7},{7,6},{8,9},{9,8},{10,11... | collective-permute-start | bytes 786440 | tf_op jit(solution)/shard_map/ppermute | solution.py:208
  30.1 0.8 %prep.3 = (bf16[4,192,256]{2,1,0:T(8,128)(2,1)S(1)}, bf16[4,64,256]{2,1,0:T(8,128)(2,1)S(1)}, bf16[4,1024,256]{2,1,0:T(8,128)(2,1)S(1)}) custom-call(f32[4,4,256]{2,1,0:T(4,128)S(1)} %get-tuple-element.34.taps_e, f32[4,4,256]{2,1,0:T(4,128)S(1)} %get-tuple-element.33.taps_l, f32[4,4,256]{2,1,0:T(4,128)S(1)} %pad_maximum_fusion.3.col_hi, ...), custom_call_target="tpu_custom_call" | custom-call | tf_op jit(solution)/shard_map/prep/pallas_call | solution.py:74
  30.9 1.3 %late.4 = f32[4,16,1024]{2,1,0:T(8,128)S(1)} custom-call(s32[1]{0:T(128)} %bitcast.1.odd_ref, f32[4,64,1024]{2,1,0:T(8,128)S(1)} %copy-done.1, f32[4,16,1024]{2,1,0:T(8,128)S(1)} %collective-permute-done.3.far_ref, bf16[4,64,256]{2,1,0:T(8,128)(2,1)S(1)} %get-tuple-element.15.r_ref, bf16[4,1024,256]{2,1,0:T(8,128)(2,1)S(1)} %get-tuple-element.14.c_ref), custom_call_target="tpu_custom_call" | custom-call | flops 536870912 | bytes 4194304 | tf_op jit(solution)/shard_map/late/pallas_call | solution.py:170
  32.2 3.7 %early.4 = f32[4,48,1024]{2,1,0:T(8,128)S(1)} custom-call(s32[1]{0:T(128)} %bitcast.1.odd_ref, f32[4,64,1024]{2,1,0:T(8,128)S(1)} %copy-done.1, f32[4,16,1024]{2,1,0:T(8,128)} %collective-permute-done.2.near_ref, bf16[4,192,256]{2,1,0:T(8,128)(2,1)S(1)} %get-tuple-element.13.r_ref, bf16[4,1024,256]{2,1,0:T(8,128)(2,1)S(1)} %get-tuple-element.14.c_ref), custom_call_target="tpu_custom_call" | custom-call | flops 1610612736 | bytes 8388608 | tf_op jit(solution)/shard_map/early/pallas_call | solution.py:135
  36.0 1.3 %late.5 = f32[4,16,1024]{2,1,0:T(8,128)S(1)} custom-call(s32[1]{0:T(128)} %bitcast.1.odd_ref, f32[4,64,1024]{2,1,0:T(8,128)S(1)} %get-tuple-element.24.v_ref, f32[4,16,1024]{2,1,0:T(8,128)S(1)} %collective-permute-done.5.far_ref, bf16[4,64,256]{2,1,0:T(8,128)(2,1)S(1)} %get-tuple-element.15.r_ref, bf16[4,1024,256]{2,1,0:T(8,128)(2,1)S(1)} %get-tuple-element.14.c_ref), custom_call_target="tpu_custom_call" | custom-call | flops 536870912 | bytes 4194304 | tf_op jit(solution)/shard_map/late/pallas_call | solution.py:170
  37.3 2.7 %early.5 = f32[4,48,1024]{2,1,0:T(8,128)S(1)} custom-call(s32[1]{0:T(128)} %bitcast.1.odd_ref, f32[4,64,1024]{2,1,0:T(8,128)S(1)} %get-tuple-element.24.v_ref, f32[4,16,1024]{2,1,0:T(8,128)S(1)} %collective-permute-done.4.near_ref, bf16[4,192,256]{2,1,0:T(8,128)(2,1)S(1)} %get-tuple-element.13.r_ref, bf16[4,1024,256]{2,1,0:T(8,128)(2,1)S(1)} %get-tuple-element.14.c_ref), custom_call_target="tpu_custom_call" | custom-call | flops 1610612736 | bytes 8388608 | tf_op jit(solution)/shard_map/early/pallas_call | solution.py:135
  40.1 2.6 %multiply_reduce_fusion = (f32[]{:T(128)}, f32[]{:T(128)}, f32[]{:T(128)}, f32[4,64,1024]{2,1,0:T(8,128)}, f32[4,64,1024]{2,1,0:T(8,128)}, /*index=5*/f32[]{:T(128)}) fusion(f32[4,64,1024]{2,1,0:T(8,128)S(1)} %copy-done.2, f32[]{:T(128)} %bitcast.32, f32[4,48,1024]{2,1,0:T(8,128)S(1)} %early.4, f32[4,16,1024]{2,1,0:T(8,128)S(1)} %late.4, pred[]{:T(512)S(6)} %eq.4, ...), kind=kLoop, calls=%fused_computation.9 | loop fusion | flops 4718588 | bytes 6291477 | tf_op jit(solution)/shard_map/reduce_sum | solution.py:239
  42.7 3.8 %stack.27 = f32[6]{0:T(128)S(1)} concatenate(f32[1]{0:T(128)} %bitcast, f32[1]{0:T(128)} %bitcast.2, f32[1]{0:T(128)} %bitcast.3, f32[1]{0:T(128)} %bitcast.7, f32[1]{0:T(128)} %bitcast.8, f32[1]{0:T(128)} %bitcast.9), dimensions={0} | concatenate | bytes 48 | tf_op jit(solution)/shard_map/stack | solution.py:233
  46.5 1.1 %collective-permute-done.6 = f32[6]{0:T(128)S(1)} collective-permute-done((f32[6]{0:T(128)S(1)}, f32[6]{0:T(128)S(1)}, u32[]{:S(2)}, u32[]{:S(2)}) %collective-permute-start.6) | collective-permute-done | bytes 56 | tf_op jit(solution)/shard_map/ppermute | solution.py:190
  47.8 3.4 %collective-permute-done.7 = f32[6]{0:T(128)S(1)} collective-permute-done((f32[6]{0:T(128)S(1)}, f32[6]{0:T(128)S(1)}, u32[]{:S(2)}, u32[]{:S(2)}) %collective-permute-start.7) | collective-permute-done | bytes 56 | tf_op jit(solution)/shard_map/ppermute | solution.py:190
  51.2 1.6 %collective-permute-start.8 = (f32[6]{0:T(128)S(1)}, f32[6]{0:T(128)S(1)}, u32[]{:S(2)}, u32[]{:S(2)}) collective-permute-start(f32[6]{0:T(128)S(1)} %add.103), channel_id=1, source_target_pairs={{0,4},{1,5},{2,6},{3,7},{4,0},{5,1},{6,2},{7,3},{8,12},{9,13},{10,... | collective-permute-start | bytes 80 | tf_op jit(solution)/shard_map/ppermute | solution.py:190
  52.8 2.0 %collective-permute-done.8 = f32[6]{0:T(128)S(1)} collective-permute-done((f32[6]{0:T(128)S(1)}, f32[6]{0:T(128)S(1)}, u32[]{:S(2)}, u32[]{:S(2)}) %collective-permute-start.8) | collective-permute-done | bytes 56 | tf_op jit(solution)/shard_map/ppermute | solution.py:190
  54.7 2.6 %collective-permute-start.9 = (f32[6]{0:T(128)S(1)}, f32[6]{0:T(128)S(1)}, u32[]{:S(2)}, u32[]{:S(2)}) collective-permute-start(f32[6]{0:T(128)S(1)} %add.104), channel_id=1, source_target_pairs={{0,8},{1,9},{2,10},{3,11},{4,12},{5,13},{6,14},{7,15},{8,0},{9,1},... | collective-permute-start | bytes 80 | tf_op jit(solution)/shard_map/ppermute | solution.py:190
  57.3 1.9 %collective-permute-done.9 = f32[6]{0:T(128)S(1)} collective-permute-done((f32[6]{0:T(128)S(1)}, f32[6]{0:T(128)S(1)}, u32[]{:S(2)}, u32[]{:S(2)}) %collective-permute-start.9) | collective-permute-done | bytes 56 | tf_op jit(solution)/shard_map/ppermute | solution.py:190
  59.2 0.7 fusion.10
  61.8 1.1 %multiply_subtract_fusion.1 = f32[4,64,1024]{2,1,0:T(8,128)} fusion(f32[4,64,1024]{2,1,0:T(8,128)S(1)} %copy-done.1, f32[4,64,1024]{2,1,0:T(8,128)S(1)} %get-tuple-element.24.v_ref, f32[]{:T(128)S(6)} %div.6), kind=kLoop, calls=%fused_computation.7 | loop fusion | flops 524288 | bytes 3145732 | tf_op jit(solution)/shard_map/sub | solution.py:247
  65.4 4.0 %multiply_add_fusion = (f32[4,64,1024]{2,1,0:T(8,128)}, f32[4,64,1024]{2,1,0:T(8,128)}, f32[4,64,1024]{2,1,0:T(8,128)}) fusion(f32[4,64,1024]{2,1,0:T(8,128)S(1)} %copy-done, f32[]{:T(128)S(6)} %div.7, f32[4,64,1024]{2,1,0:T(8,128)} %get-tuple-element.21, f32[4,64,1024]{2,1,0:T(8,128)} %get-tuple-element.22, f32[]{:T(128)S(6)} %div.6, f32[4,64,1024]{2,1,0:T(8,128)} %param.7), kind=kLoop, calls=%fused_computation.5 | loop fusion | flops 1572864 | bytes 7340040 | tf_op jit(solution)/shard_map/add | solution.py:249
  (52 shorter events, 2.0 us)
Async XLA Ops:
  0.6 15.5 %copy-start = (f32[4,64,1024]{2,1,0:T(8,128)S(1)}, f32[4,64,1024]{2,1,0:T(8,128)}, u32[]{:S(2)}) copy-start(f32[4,64,1024]{2,1,0:T(8,128)} %v_ref.5) | copy-start | bytes 3145732
  0.6 11.8 %copy-start.4 = (f32[4,4,31]{2,1,0:T(4,128)S(1)}, f32[4,4,31]{2,1,0:T(4,128)}, u32[]{:S(2)}) copy-start(f32[4,4,31]{2,1,0:T(4,128)} %param.12) | copy-start | bytes 5956
  0.7 12.9 %copy-start.5 = (f32[4,4,31]{2,1,0:T(4,128)S(1)}, f32[4,4,31]{2,1,0:T(4,128)}, u32[]{:S(2)}) copy-start(f32[4,4,31]{2,1,0:T(4,128)} %param.11) | copy-start | bytes 5956
  0.7 14.6 %copy-start.3 = (f32[4,64,1024]{2,1,0:T(8,128)S(1)}, f32[4,64,1024]{2,1,0:T(8,128)}, u32[]{:S(2)}) copy-start(f32[4,64,1024]{2,1,0:T(8,128)} %param.9) | copy-start | bytes 3145732
  2.7 28.2 %collective-permute-start.3 = (f32[4,16,1024]{2,1,0:T(8,128)}, f32[4,16,1024]{2,1,0:T(8,128)S(1)}, u32[]{:S(2)}, u32[]{:S(2)}) collective-permute-start(f32[4,16,1024]{2,1,0:T(8,128)} %get-tuple-element.29), channel_id=1, source_target_pairs={{1,2},{2,1},{3,4},{4,3},{5,6},{6,5},{7,8},{8,7},{9,10},{10,9},{11,... | collective-permute-start | bytes 786440 | tf_op jit(solution)/shard_map/ppermute | solution.py:208
  3.4 28.9 %collective-permute-start.2 = (f32[4,16,1024]{2,1,0:T(8,128)}, f32[4,16,1024]{2,1,0:T(8,128)}, u32[]{:S(2)}, u32[]{:S(2)}) collective-permute-start(f32[4,16,1024]{2,1,0:T(8,128)} %get-tuple-element.30), channel_id=1, source_target_pairs={{0,1},{1,0},{2,3},{3,2},{4,5},{5,4},{6,7},{7,6},{8,9},{9,8},{10,11... | collective-permute-start | bytes 786440 | tf_op jit(solution)/shard_map/ppermute | solution.py:208
  8.8 7.3 %collective-permute-start.1 = (f32[4,16,1024]{2,1,0:T(8,128)S(1)}, f32[4,16,1024]{2,1,0:T(8,128)S(1)}, u32[]{:S(2)}, u32[]{:S(2)}) collective-permute-start(f32[4,16,1024]{2,1,0:T(8,128)S(1)} %get-tuple-element.31), channel_id=1, source_target_pairs={{1,2},{2,1},{3,4},{4,3},{5,6},{6,5},{7,8},{8,7},{9,10},{10,9},{11,... | collective-permute-start | bytes 786440 | tf_op jit(solution)/shard_map/ppermute | solution.py:208
  9.5 8.0 %collective-permute-start = (f32[4,16,1024]{2,1,0:T(8,128)S(1)}, f32[4,16,1024]{2,1,0:T(8,128)S(1)}, u32[]{:S(2)}, u32[]{:S(2)}) collective-permute-start(f32[4,16,1024]{2,1,0:T(8,128)S(1)} %get-tuple-element.32), channel_id=1, source_target_pairs={{0,1},{1,0},{2,3},{3,2},{4,5},{5,4},{6,7},{7,6},{8,9},{9,8},{10,11... | collective-permute-start | bytes 786440 | tf_op jit(solution)/shard_map/ppermute | solution.py:208
  20.3 10.6 %copy-start.1 = (f32[4,64,1024]{2,1,0:T(8,128)S(1)}, f32[4,64,1024]{2,1,0:T(8,128)}, u32[]{:S(2)}) copy-start(f32[4,64,1024]{2,1,0:T(8,128)} %v_ref.7) | copy-start | bytes 3145732
  21.3 14.7 %collective-permute-start.5 = (f32[4,16,1024]{2,1,0:T(8,128)S(1)}, f32[4,16,1024]{2,1,0:T(8,128)S(1)}, u32[]{:S(2)}, u32[]{:S(2)}) collective-permute-start(f32[4,16,1024]{2,1,0:T(8,128)S(1)} %get-tuple-element.27), channel_id=1, source_target_pairs={{1,2},{2,1},{3,4},{4,3},{5,6},{6,5},{7,8},{8,7},{9,10},{10,9},{11,... | collective-permute-start | bytes 786440 | tf_op jit(solution)/shard_map/ppermute | solution.py:208
  22.1 15.2 %collective-permute-start.4 = (f32[4,16,1024]{2,1,0:T(8,128)S(1)}, f32[4,16,1024]{2,1,0:T(8,128)S(1)}, u32[]{:S(2)}, u32[]{:S(2)}) collective-permute-start(f32[4,16,1024]{2,1,0:T(8,128)S(1)} %get-tuple-element.28), channel_id=1, source_target_pairs={{0,1},{1,0},{2,3},{3,2},{4,5},{5,4},{6,7},{7,6},{8,9},{9,8},{10,11... | collective-permute-start | bytes 786440 | tf_op jit(solution)/shard_map/ppermute | solution.py:208
  37.3 2.8 %copy-start.2 = (f32[4,64,1024]{2,1,0:T(8,128)S(1)}, f32[4,64,1024]{2,1,0:T(8,128)}, u32[]{:S(2)}) copy-start(f32[4,64,1024]{2,1,0:T(8,128)} %param.7) | copy-start | bytes 3145732
  46.5 1.1 %collective-permute-start.6 = (f32[6]{0:T(128)S(1)}, f32[6]{0:T(128)S(1)}, u32[]{:S(2)}, u32[]{:S(2)}) collective-permute-start(f32[6]{0:T(128)S(1)} %stack.27), channel_id=1, source_target_pairs={{0,1},{1,0},{2,3},{3,2},{4,5},{5,4},{6,7},{7,6},{8,9},{9,8},{10,11... | collective-permute-start | bytes 80 | tf_op jit(solution)/shard_map/ppermute | solution.py:190
  47.7 3.5 %collective-permute-start.7 = (f32[6]{0:T(128)S(1)}, f32[6]{0:T(128)S(1)}, u32[]{:S(2)}, u32[]{:S(2)}) collective-permute-start(f32[6]{0:T(128)S(1)} %add.102), channel_id=1, source_target_pairs={{0,2},{1,3},{2,0},{3,1},{4,6},{5,7},{6,4},{7,5},{8,10},{9,11},{10,... | collective-permute-start | bytes 80 | tf_op jit(solution)/shard_map/ppermute | solution.py:190
  51.2 3.5 %collective-permute-start.8 = (f32[6]{0:T(128)S(1)}, f32[6]{0:T(128)S(1)}, u32[]{:S(2)}, u32[]{:S(2)}) collective-permute-start(f32[6]{0:T(128)S(1)} %add.103), channel_id=1, source_target_pairs={{0,4},{1,5},{2,6},{3,7},{4,0},{5,1},{6,2},{7,3},{8,12},{9,13},{10,... | collective-permute-start | bytes 80 | tf_op jit(solution)/shard_map/ppermute | solution.py:190
  54.7 4.4 %collective-permute-start.9 = (f32[6]{0:T(128)S(1)}, f32[6]{0:T(128)S(1)}, u32[]{:S(2)}, u32[]{:S(2)}) collective-permute-start(f32[6]{0:T(128)S(1)} %add.104), channel_id=1, source_target_pairs={{0,8},{1,9},{2,10},{3,11},{4,12},{5,13},{6,14},{7,15},{8,0},{9,1},... | collective-permute-start | bytes 80 | tf_op jit(solution)/shard_map/ppermute | solution.py:190

commit v2 on v1

v2 whole, which is shorter than its diff:
```python
import functools

import jax
import jax.numpy as jnp
from jax import lax
from jax.experimental import pallas as pl
from jax.experimental.pallas import tpu as pltpu
from jax.sharding import PartitionSpec as P

F32 = jnp.float32
BF16 = jnp.bfloat16
EDGE = 16
LANE = 128
WIDE = 256
VM = pl.BlockSpec(memory_space=pltpu.VMEM)
SM = pl.BlockSpec(memory_space=pltpu.SMEM)
ANY = pl.BlockSpec(memory_space=pl.ANY)
LIMIT = 40 * 2**20


def split(x):
    hi = x.astype(BF16)
    return hi, (x - hi.astype(F32)).astype(BF16)


def params():
    return pltpu.CompilerParams(vmem_limit_bytes=LIMIT)


def cost(us):
    return pl.CostEstimate(flops=int(us * 1.0e9), bytes_accessed=1 << 20, transcendentals=0)


def f32(*shape):
    return jax.ShapeDtypeStruct(shape, F32)


def edges_kernel(odd_ref, p_ref, r_ref, p_far, p_near, r_far, r_near, sems):
    inner = p_ref.shape[1] - EDGE
    odd = odd_ref[0]
    far = pl.multiple_of(odd * inner, EDGE)
    near = pl.multiple_of((1 - odd) * inner, EDGE)
    copies = []
    for k, (src, at, dst) in enumerate(((p_ref, far, p_far), (p_ref, near, p_near), (r_ref, far, r_far), (r_ref, near, r_near))):
        copies.append(pltpu.make_async_copy(src.at[:, pl.ds(at, EDGE), :], dst, sems.at[k]))
    for c in copies:
        c.start()
    for c in copies:
        c.wait()


def edges(odd, p, r):
    depth, rows, columns = p.shape
    return pl.pallas_call(
        edges_kernel,
        out_shape=(f32(depth, EDGE, columns),) * 4,
        in_specs=[SM, ANY, ANY],
        out_specs=[VM] * 4,
        scratch_shapes=[pltpu.SemaphoreType.DMA((4,))],
        compiler_params=params(),
        cost_estimate=cost(1.0),
        name="edges",
    )(odd, p, r)


def one_hot(count, at):
    tap = lax.broadcasted_iota(jnp.int32, (count, WIDE), 0)
    lane = lax.broadcasted_iota(jnp.int32, (count, WIDE), 1)
    return jnp.where(lane == (at(tap) + WIDE) % WIDE, 1.0, 0.0).astype(BF16)


def pick(parts_and_places):
    got = None
    for part, place in parts_and_places:
        term = jnp.dot(part, place, preferred_element_type=F32)
        got = term if got is None else got + term
    return got


def prep_kernel(depth, inner, row_ref, col_ref, *refs):
    outs, bases = refs[:6], refs[6:]
    count = row_ref.shape[1]
    last = count - 1
    row_hi, row_lo = split(row_ref[...])
    col_hi, col_lo = split(col_ref[...])
    window = LANE + 2 * EDGE
    lane = lax.broadcasted_iota(jnp.int32, (window, WIDE), 1)
    for adjoint in (False, True):
        r_early, r_late, c_out = outs[3:] if adjoint else outs[:3]
        turn = (lambda a: last - a) if adjoint else (lambda a: a)
        for base, gap in ((bases[0], inner + 2 * EDGE), (bases[1], 3 * EDGE)):
            base[...] = pick((
                (row_hi, one_hot(count, turn)),
                (row_hi, one_hot(count, lambda a: turn(a) + gap)),
                (row_lo, one_hot(count, lambda a: turn(a) + 2 * gap)),
            ))
        bases[2][...] = pick(((col_hi, one_hot(count, lambda a: -turn(a))),))
        bases[3][...] = pick(((col_lo, one_hot(count, lambda a: LANE - turn(a))),))

        def banded(base, pair, rows, shift):
            wide = jnp.broadcast_to(base[pl.ds(pair, 1), :], (rows, WIDE))
            return pltpu.roll(wide, shift, 1, stride=1, stride_axis=0)

        for o in range(depth):
            for s in range(depth):
                pair = s * depth + o if adjoint else o * depth + s
                r_early[s, o * inner:(o + 1) * inner, :] = banded(bases[0], pair, inner, 1).astype(BF16)
                r_late[s, o * EDGE:(o + 1) * EDGE, :] = banded(bases[1], pair, EDGE, 1).astype(BF16)
                band = jnp.where(lane < LANE, banded(bases[2], pair, window, 0), banded(bases[3], pair, window, 0))
                c_out[o, s * WIDE:s * WIDE + window, :] = band.astype(BF16)
                c_out[o, s * WIDE + window:(s + 1) * WIDE, :] = jnp.zeros((WIDE - window, WIDE), BF16)


def prep(row, col, inner):
    depth, _, count = row.shape
    pairs = depth * depth
    one = (
        jax.ShapeDtypeStruct((depth, depth * inner, WIDE), BF16),
        jax.ShapeDtypeStruct((depth, depth * EDGE, WIDE), BF16),
        jax.ShapeDtypeStruct((depth, depth * WIDE, WIDE), BF16),
    )
    return pl.pallas_call(
        functools.partial(prep_kernel, depth, inner),
        out_shape=one + one,
        in_specs=[VM] * 2,
        out_specs=[VM] * 6,
        scratch_shapes=[pltpu.VMEM((pairs, WIDE), F32)] * 4,
        compiler_params=params(),
        cost_estimate=cost(1.5),
        name="prep",
    )(row.reshape(pairs, count), col.reshape(pairs, count))


def shifted(x, border):
    wide = jnp.concatenate([x, jnp.zeros((x.shape[0], LANE), F32)], axis=1)
    return split(pltpu.roll(wide, border, 1))


def put(win, at, group, hi, lo):
    rows = hi.shape[0]
    for g, part in enumerate((hi, lo, hi)):
        win[pl.ds(pl.multiple_of(at + g * group, EDGE), rows), :] = part


def along_rows(r_ref, win, v_hi, v_lo, s, group):
    if 3 * group < WIDE:
        win[s, 3 * group:, :] = jnp.zeros((WIDE - 3 * group, win.shape[2]), BF16)
    got = jnp.dot(r_ref[s], win[s], preferred_element_type=F32)
    v_hi[s], v_lo[s] = split(got)


def along_columns(v_hi, v_lo, c_ref, o, rows, columns, depth):
    tall = []
    blocks = columns // LANE
    for part in (v_hi, v_lo):
        for n in range(blocks):
            tall.append(jnp.concatenate(
                [part[s, o * rows:(o + 1) * rows, n * LANE:n * LANE + WIDE] for s in range(depth)], axis=1))
    got = jnp.dot(jnp.concatenate(tall, axis=0), c_ref[o], preferred_element_type=F32)
    out = []
    for n in range(blocks):
        top = got[n * rows:(n + 1) * rows]
        low = got[(blocks + n) * rows:(blocks + n + 1) * rows]
        out.append(top[:, :LANE] + (top[:, LANE:] + low[:, :LANE]))
    return jnp.concatenate(out, axis=1)


def folded(x):
    part = jnp.sum(x.reshape(x.shape[0] // 8, 8, x.shape[1]), axis=0)
    part = sum(part[:, n:n + LANE] for n in range(0, x.shape[1], LANE))
    return jnp.sum(part, axis=0, keepdims=True)


def early_kernel(border, odd_ref, v_ref, near_ref, r_ref, c_ref, out_ref, win, v_hi, v_lo):
    depth, rows, columns = v_ref.shape
    inner = rows - EDGE
    group = rows + EDGE
    odd = odd_ref[0]
    for s in range(depth):
        put(win.at[s], odd * EDGE, group, *shifted(v_ref[s], border))
        put(win.at[s], (1 - odd) * rows, group, *shifted(near_ref[s], border))
        along_rows(r_ref, win, v_hi, v_lo, s, group)
    for o in range(depth):
        out_ref[o] = along_columns(v_hi, v_lo, c_ref, o, inner, columns, depth)


def early(odd, v, near, r, c, border):
    depth, rows, columns = v.shape
    inner = rows - EDGE
    wide = columns + LANE
    return pl.pallas_call(
        functools.partial(early_kernel, border),
        out_shape=f32(depth, inner, columns),
        in_specs=[SM, VM, VM, VM, VM],
        out_specs=VM,
        scratch_shapes=[
            pltpu.VMEM((depth, WIDE, wide), BF16),
            pltpu.VMEM((depth, depth * inner, wide), BF16),
            pltpu.VMEM((depth, depth * inner, wide), BF16),
        ],
        compiler_params=params(),
        cost_estimate=cost(2.8),
        name="early",
    )(odd, v, near, r, c)


def late_rows(border, odd, v_ref, far_ref, r_ref, win, v_hi, v_lo):
    depth, rows, _ = v_ref.shape
    group = 3 * EDGE
    start = pl.multiple_of(odd * (rows - 2 * EDGE), EDGE)
    for s in range(depth):
        put(win.at[s], (1 - odd) * EDGE, group, *shifted(v_ref[s, pl.ds(start, 2 * EDGE), :], border))
        put(win.at[s], odd * 2 * EDGE, group, *shifted(far_ref[s], border))
        along_rows(r_ref, win, v_hi, v_lo, s, group)


def late_scratch(depth, columns):
    wide = columns + LANE
    return [
        pltpu.VMEM((depth, WIDE, wide), BF16),
        pltpu.VMEM((depth, depth * EDGE, wide), BF16),
        pltpu.VMEM((depth, depth * EDGE, wide), BF16),
    ]


def image_kernel(border, odd_ref, v_ref, far_ref, r_ref, c_ref, in_ref, grad_ref, out_ref, edge_ref, sums_ref, win, v_hi, v_lo):
    depth, rows, columns = v_ref.shape
    inner = rows - EDGE
    odd = odd_ref[0]
    late_rows(border, odd, v_ref, far_ref, r_ref, win, v_hi, v_lo)
    sums_ref[...] = jnp.zeros_like(sums_ref)
    for o in range(depth):
        edge = along_columns(v_hi, v_lo, c_ref, o, EDGE, columns, depth)
        edge_ref[o] = edge
        out_ref[o, pl.ds(pl.multiple_of(odd * inner, EDGE), EDGE), :] = edge
        out_ref[o, pl.ds(pl.multiple_of((1 - odd) * EDGE, EDGE), inner), :] = in_ref[o]
        sums_ref[0:1, :] += folded(grad_ref[o] * grad_ref[o])
        sums_ref[1:2, :] += folded(in_ref[o] * in_ref[o]) + folded(edge * edge)
        sums_ref[2:3, :] += folded(v_ref[o] * v_ref[o])


def image_late(odd, v, far, r, c, inside, grad, border):
    depth, rows, columns = v.shape
    return pl.pallas_call(
        functools.partial(image_kernel, border),
        out_shape=(f32(depth, rows, columns), f32(depth, EDGE, columns), f32(8, LANE)),
        in_specs=[SM] + [VM] * 6,
        out_specs=[VM] * 3,
        scratch_shapes=late_scratch(depth, columns),
        compiler_params=params(),
        cost_estimate=cost(1.8),
        name="image_late",
    )(odd, v, far, r, c, inside, grad)


def back_kernel(border, odd_ref, damp_ref, v_ref, far_ref, r_ref, c_ref, in_ref, with_ref, out_ref, win, v_hi, v_lo):
    depth, rows, columns = v_ref.shape
    inner = rows - EDGE
    odd = odd_ref[0]
    damp = damp_ref[0]
    late_rows(border, odd, v_ref, far_ref, r_ref, win, v_hi, v_lo)
    for o in range(depth):
        edge = along_columns(v_hi, v_lo, c_ref, o, EDGE, columns, depth)
        at, rest = pl.multiple_of(odd * inner, EDGE), pl.multiple_of((1 - odd) * EDGE, EDGE)
        out_ref[o, pl.ds(at, EDGE), :] = edge - damp * with_ref[o, pl.ds(at, EDGE), :]
        out_ref[o, pl.ds(rest, inner), :] = in_ref[o] - damp * with_ref[o, pl.ds(rest, inner), :]


def back_late(odd, damp, v, far, r, c, inside, beside, border):
    depth, rows, columns = v.shape
    return pl.pallas_call(
        functools.partial(back_kernel, border),
        out_shape=f32(depth, rows, columns),
        in_specs=[SM, SM] + [VM] * 6,
        out_specs=VM,
        scratch_shapes=late_scratch(depth, columns),
        compiler_params=params(),
        cost_estimate=cost(1.6),
        name="back_late",
    )(odd, damp, v, far, r, c, inside, beside)


def last_kernel(border, odd_ref, damp_ref, v_ref, far_ref, r_ref, c_ref, in_ref, with_ref, g_ref, before_ref, out_ref, sums_ref, win, v_hi, v_lo):
    depth, rows, columns = v_ref.shape
    inner = rows - EDGE
    odd = odd_ref[0]
    damp = damp_ref[0]
    late_rows(border, odd, v_ref, far_ref, r_ref, win, v_hi, v_lo)
    sums_ref[...] = before_ref[...]
    for o in range(depth):
        edge = along_columns(v_hi, v_lo, c_ref, o, EDGE, columns, depth)
        for at, rows_now, value in (
            (pl.multiple_of(odd * inner, EDGE), EDGE, edge),
            (pl.multiple_of((1 - odd) * EDGE, EDGE), inner, in_ref[o]),
        ):
            here = pl.ds(at, rows_now)
            h = value + damp * with_ref[o, here, :]
            g = g_ref[o, here, :]
            out_ref[o, here, :] = h
            sums_ref[3:4, :] += folded(g * g)
            sums_ref[4:5, :] += folded(g * h)
            sums_ref[5:6, :] += folded(h * h)


def last_late(odd, damp, v, far, r, c, inside, beside, g, before, border):
    depth, rows, columns = v.shape
    return pl.pallas_call(
        functools.partial(last_kernel, border),
        out_shape=(f32(depth, rows, columns), f32(8, LANE)),
        in_specs=[SM, SM] + [VM] * 8,
        out_specs=[VM] * 2,
        scratch_shapes=late_scratch(depth, columns),
        compiler_params=params(),
        cost_estimate=cost(1.8),
        name="last_late",
    )(odd, damp, v, far, r, c, inside, beside, g, before)


def final_kernel(damp_ref, mine_ref, other_ref, x_ref, r_ref, p_ref, f_ref, g_ref, h_ref,
                 nx_out, nr_out, ng_out, np_out, nx, nr, ng, nd, sems):
    depth = x_ref.shape[0]
    damp = damp_ref[0]
    sums = jnp.sum(mine_ref[...] + other_ref[...], axis=1, keepdims=True)
    before, image, direction, gg, gh, hh = (sums[k:k + 1, :] for k in range(6))
    step = before / (image + damp * direction)
    after = gg - step * (2.0 * gh - step * hh)
    ratio = after / before
    copies = []
    for o in range(depth):
        p = p_ref[o]
        new = g_ref[o] - step * h_ref[o]
        for k, (buf, out, value) in enumerate((
            (nx, nx_out, x_ref[o] + step * p),
            (nr, nr_out, r_ref[o] - step * f_ref[o]),
            (ng, ng_out, new),
            (nd, np_out, new + ratio * p),
        )):
            buf[o] = value
            copies.append(pltpu.make_async_copy(buf.at[o], out.at[o], sems.at[o, k]))
            copies[-1].start()
    for c in copies:
        c.wait()


def final(damp, mine, other, x, r, p, f, g, h):
    shape = x.shape
    return pl.pallas_call(
        final_kernel,
        out_shape=(f32(*shape),) * 4,
        in_specs=[SM] + [VM] * 8,
        out_specs=[ANY] * 4,
        scratch_shapes=[pltpu.VMEM(shape, F32)] * 4 + [pltpu.SemaphoreType.DMA((shape[0], 4))],
        compiler_params=params(),
        cost_estimate=cost(2.0),
        name="final",
    )(damp, mine, other, x, r, p, f, g, h)


def swap(values, axis, step):
    return lax.ppermute(values, axis, [(i, i ^ step) for i in range(lax.axis_size(axis))])


def body(solution, residual, gradient, direction, row_taps, col_taps, damping):
    border = row_taps.shape[2] // 2
    depth, rows, columns = direction.shape
    inner = rows - EDGE
    peers = lax.axis_size("lat")
    odd = lax.axis_index("lat") % 2
    odd_arr = jnp.full((1,), odd, jnp.int32)
    far_pairs = [p for a in range(1, peers - 1, 2) for p in ((a, a + 1), (a + 1, a))]

    def near_swap(v):
        return swap(v, "lat", 1)

    def far_swap(v):
        return lax.ppermute(v, "lat", far_pairs)

    p_far_edge, p_near_edge, r_far_edge, r_near_edge = edges(odd_arr, direction, residual)
    p_far, p_near = far_swap(p_far_edge), near_swap(p_near_edge)
    r_far, r_near = far_swap(r_far_edge), near_swap(r_near_edge)
    re, rl, c, rae, ral, ca = prep(row_taps, col_taps, inner)

    image_in = early(odd_arr, direction, p_near, re, c, border)
    f_near = near_swap(lax.dynamic_slice_in_dim(image_in, (1 - odd) * (inner - EDGE), EDGE, axis=1))
    image, f_edge, sums = image_late(odd_arr, direction, p_far, rl, c, image_in, gradient, border)
    f_far = far_swap(f_edge)
    g_in = early(odd_arr, residual, r_near, rae, ca, border)
    g = back_late(odd_arr, damping, residual, r_far, ral, ca, g_in, solution, border)
    h_in = early(odd_arr, image, f_near, rae, ca, border)
    h, sums = last_late(odd_arr, damping, image, f_far, ral, ca, h_in, direction, g, sums, border)

    step = 1
    while 2 * step < peers:
        sums = sums + swap(sums, "lat", step)
        step *= 2
    other = swap(sums, "lat", step)
    return final(damping, sums, other, solution, residual, direction, image, g, h)


def solution(mesh):
    split_rows = P("stack", "lat", None)
    return jax.shard_map(
        body,
        mesh=mesh,
        in_specs=(split_rows,) * 4 + (P(),) * 3,
        out_specs=(split_rows,) * 4,
        check_vma=False,
    )
```

time: 69.8 us -> 47.8 us (0.68)
  other arithmetic: 10 us -> 0.01 us
  local copies, waits for them, and re-layouts: 9.31 us -> 2.5 us
  between operations: 5.99 us -> 1.68 us
  Pallas kernels: 14.7 us -> 17.1 us
  starting transfers between devices: 21 us -> 18.7 us
  waiting for transfers between devices: 8.38 us -> 7.61 us
    reduce_sum x3 -> x0, other arithmetic: 4.46 us -> none  [the longest x1 2.65 us: body(): jnp.sum(back_f * back_f)]
    add x7 -> x3, other arithmetic: 4.24 us -> 0.01 us  [body(): sums = sums + swap(sums, 'lat', step)]
    another operation x1 -> x0, local copies, waits for them, and re-layouts: 3.79 us -> none  [body(): jnp.stack([jnp.sum(gradient * gradient), jnp.sum(image * image), jnp.sum(...]
    dynamic_slice x3 -> x1, local copies, waits for them, and re-layouts: 3.12 us -> 0.03 us  [body(): lax.dynamic_slice_in_dim(image_in, (1 - odd) * (inner - EDGE), EDGE, axis=1)]
    unnamed x14 -> x16, local copies, waits for them, and re-layouts: 0.04 us -> 2.48 us
    pallas_call x8 -> x9, Pallas kernels: 14.7 us -> 17.1 us  [the longest x3 8.46 us: early(): pl.pallas_call(functools.partial(early_kernel, border), out_shape=f32(dep...]
    ppermute x10, starting transfers between devices: 21 us -> 18.7 us  [the longest x7 16.5 us: swap(): lax.ppermute(values, axis, [(i, i ^ step) for i in range(lax.axis_size(ax...]
    slice x15 -> x0, local copies, waits for them, and re-layouts: 1.78 us -> none  [the longest x12 0.97 us: place(): return jnp.roll(wide, 1 - count, axis=2)]
  transfers between devices with their start and end apart: 10 -> 10, of which waited for: 4 -> 4; matrix products, arithmetic and copies ran while one was open for 7% -> 0% of each run, Pallas kernels for 17% -> 27%
where the time goes in v2:
time: 47.8 us; the launch traced here: 47.6 us
  starting transfers between devices  18.7 us (39%)
  Pallas kernels  17.1 us (36%)
  waiting for transfers between devices  7.61 us (16%)
  local copies, waits for them, and re-layouts  2.5 us (5%)
  between operations  1.68 us (4%)
    ppermute x7, starting transfers between devices, swap(): lax.ppermute(values, axis, [(i, i ^ step) for i in range(lax.axis_size(ax...  16.5 us
    pallas_call x3, Pallas kernels, early(): pl.pallas_call(functools.partial(early_kernel, border), out_shape=f32(dep...  8.46 us
    ppermute x7, waiting for transfers between devices, swap(): lax.ppermute(values, axis, [(i, i ^ step) for i in range(lax.axis_size(ax...  7.6 us
    unnamed x16, local copies, waits for them, and re-layouts  2.48 us
    pallas_call x1, Pallas kernels, final(): pl.pallas_call(final_kernel, out_shape=(f32(*shape),) * 4, in_specs=[SM]...  2.29 us
    ppermute x3, starting transfers between devices, far_swap(): return lax.ppermute(v, 'lat', far_pairs)  2.2 us
    pallas_call x1, Pallas kernels, prep(): pl.pallas_call(functools.partial(prep_kernel, depth, inner), out_shape=on...  1.68 us
    pallas_call x1, Pallas kernels, last_late(): pl.pallas_call(functools.partial(last_kernel, border), out_shape=(f32(dep...  1.66 us
  transfers between devices with their start and end apart: 10, of which 4 were waited for; matrix products, arithmetic and copies ran while one was open for 0% of the time, Pallas kernels for 27%

profile of v2, /device:TPU:0, one launch (start us, length us, event | category | flops | bytes accessed | tf_op | source)
XLA Modules:
  0.0 47.6 jit_solution(15275653603869942742)
XLA Ops:
  0.7 0.0 copy-start
  0.7 1.2 %copy-done = f32[4,64,1024]{2,1,0:T(8,128)S(1)} copy-done((f32[4,64,1024]{2,1,0:T(8,128)S(1)}, f32[4,64,1024]{2,1,0:T(8,128)}, u32[]{:S(2)}) %copy-start) | copy-done | bytes 1048600
  1.9 1.2 %copy-done.4 = f32[4,64,1024]{2,1,0:T(8,128)S(1)} copy-done((f32[4,64,1024]{2,1,0:T(8,128)S(1)}, f32[4,64,1024]{2,1,0:T(8,128)}, u32[]{:S(2)}) %copy-start.4) | copy-done | bytes 1048600
  3.1 0.1 edges.1
  3.2 0.5 %collective-permute-start.1 = (f32[4,16,1024]{2,1,0:T(8,128)S(1)}, f32[4,16,1024]{2,1,0:T(8,128)S(1)}, u32[]{:S(2)}, u32[]{:S(2)}) collective-permute-start(f32[4,16,1024]{2,1,0:T(8,128)S(1)} %get-tuple-element.22), channel_id=1, source_target_pairs={{0,1},{1,0},{2,3},{3,2},{4,5},{5,4},{6,7},{7,6},{8,9},{9,8},{10,11... | collective-permute-start | bytes 786440 | tf_op jit(solution)/shard_map/ppermute | solution.py:360
  3.8 0.7 %collective-permute-start = (f32[4,16,1024]{2,1,0:T(8,128)S(1)}, f32[4,16,1024]{2,1,0:T(8,128)S(1)}, u32[]{:S(2)}, u32[]{:S(2)}) collective-permute-start(f32[4,16,1024]{2,1,0:T(8,128)S(1)} %get-tuple-element.19), channel_id=1, source_target_pairs={{1,2},{2,1},{3,4},{4,3},{5,6},{6,5},{7,8},{8,7},{9,10},{10,9},{11,... | collective-permute-start | bytes 786440 | tf_op jit(solution)/shard_map/ppermute | solution.py:376
  4.4 0.7 %collective-permute-start.4 = (f32[4,16,1024]{2,1,0:T(8,128)S(1)}, f32[4,16,1024]{2,1,0:T(8,128)S(1)}, u32[]{:S(2)}, u32[]{:S(2)}) collective-permute-start(f32[4,16,1024]{2,1,0:T(8,128)S(1)} %get-tuple-element.29), channel_id=1, source_target_pairs={{1,2},{2,1},{3,4},{4,3},{5,6},{6,5},{7,8},{8,7},{9,10},{10,9},{11,... | collective-permute-start | bytes 786440 | tf_op jit(solution)/shard_map/ppermute | solution.py:376
  5.1 5.2 %collective-permute-start.5 = (f32[4,16,1024]{2,1,0:T(8,128)S(1)}, f32[4,16,1024]{2,1,0:T(8,128)S(1)}, u32[]{:S(2)}, u32[]{:S(2)}) collective-permute-start(f32[4,16,1024]{2,1,0:T(8,128)S(1)} %get-tuple-element.30), channel_id=1, source_target_pairs={{0,1},{1,0},{2,3},{3,2},{4,5},{5,4},{6,7},{7,6},{8,9},{9,8},{10,11... | collective-permute-start | bytes 786440 | tf_op jit(solution)/shard_map/ppermute | solution.py:360
  11.0 0.0 copy-start.5
  11.0 1.7 %prep.1 = (bf16[4,192,256]{2,1,0:T(8,128)(2,1)S(1)}, bf16[4,64,256]{2,1,0:T(8,128)(2,1)S(1)}, bf16[4,1024,256]{2,1,0:T(8,128)(2,1)S(1)}, bf16[4,192,256]{2,1,0:T...) custom-call(f32[16,31]{1,0:T(8,128)S(1)} %bitcast.3, f32[16,31]{1,0:T(8,128)S(1)} %bitcast.4), custom_call_target="tpu_custom_call" | custom-call | flops 1500000000 | bytes 1048576 | tf_op jit(solution)/shard_map/prep/pallas_call | solution.py:122
  12.7 0.0 collective-permute-done.1.near_ref
  12.7 0.0 copy-start.3
  12.7 2.8 %early.3.in_ref = f32[4,48,1024]{2,1,0:T(8,128)S(1)} custom-call(s32[1]{0:T(128)} %bitcast.odd_ref, f32[4,64,1024]{2,1,0:T(8,128)S(1)} %copy-done.5, f32[4,16,1024]{2,1,0:T(8,128)S(1)} %collective-permute-done.1.near_ref, bf16[4,192,256]{2,1,0:T(8,128)(2,1)S(1)} %get-tuple-element.23.r_ref, bf16[4,1024,256]{2,1,0:T(8,128)(2,1)S(1)} %get-tuple-element.21.c_ref), custom_call_target="tpu_custom_call" | custom-call | flops 2800000000 | bytes 1048576 | tf_op jit(solution)/shard_map/early/pallas_call | solution.py:191
  15.5 0.0 collective-permute-done.far_ref
  15.6 0.0 copy-start.1
  15.6 1.5 %image_late.1 = (f32[4,64,1024]{2,1,0:T(8,128)S(1)}, f32[4,16,1024]{2,1,0:T(8,128)S(1)}, f32[8,128]{1,0:T(8,128)S(1)}) custom-call(s32[1]{0:T(128)} %bitcast.odd_ref, f32[4,64,1024]{2,1,0:T(8,128)S(1)} %copy-done.5, f32[4,16,1024]{2,1,0:T(8,128)S(1)} %collective-permute-done.far_ref, bf16[4,64,256]{2,1,0:T(8,128)(2,1)S(1)} %get-tuple-element.20.r_ref, ...), custom_call_target="tpu_custom_call" | custom-call | flops 1800000000 | bytes 1048576 | tf_op jit(solution)/shard_map/image_late/pallas_call | solution.py:244
  17.1 0.9 %collective-permute-start.2 = (f32[4,16,1024]{2,1,0:T(8,128)S(1)}, f32[4,16,1024]{2,1,0:T(8,128)S(1)}, u32[]{:S(2)}, u32[]{:S(2)}) collective-permute-start(f32[4,16,1024]{2,1,0:T(8,128)S(1)} %get-tuple-element.25), channel_id=1, source_target_pairs={{1,2},{2,1},{3,4},{4,3},{5,6},{6,5},{7,8},{8,7},{9,10},{10,9},{11,... | collective-permute-start | bytes 786440 | tf_op jit(solution)/shard_map/ppermute | solution.py:376
  18.0 5.4 %collective-permute-start.3 = (f32[4,16,1024]{2,1,0:T(8,128)S(1)}, f32[4,16,1024]{2,1,0:T(8,128)S(1)}, u32[]{:S(2)}, u32[]{:S(2)}) collective-permute-start(f32[4,16,1024]{2,1,0:T(8,128)S(1)} %constant_dynamic-slice_fusion), channel_id=1, source_target_pairs={{0,1},{1,0},{2,3},{3,2},{4,5},{5,4},{6,7},{7,6},{8,9},{9,8},{10,11... | collective-permute-start | bytes 786440 | tf_op jit(solution)/shard_map/ppermute | solution.py:360
  23.4 2.8 %early.5.in_ref = f32[4,48,1024]{2,1,0:T(8,128)S(1)} custom-call(s32[1]{0:T(128)} %bitcast.odd_ref, f32[4,64,1024]{2,1,0:T(8,128)S(1)} %copy-done.1, f32[4,16,1024]{2,1,0:T(8,128)S(1)} %collective-permute-done.5.near_ref, bf16[4,192,256]{2,1,0:T(8,128)(2,1)S(1)} %get-tuple-element.28.r_ref, bf16[4,1024,256]{2,1,0:T(8,128)(2,1)S(1)} %get-tuple-element.27.c_ref), custom_call_target="tpu_custom_call" | custom-call | flops 2800000000 | bytes 1048576 | tf_op jit(solution)/shard_map/early/pallas_call | solution.py:191
  26.3 1.4 %back_late.1.g_ref = f32[4,64,1024]{2,1,0:T(8,128)S(1)} custom-call(s32[1]{0:T(128)} %bitcast.odd_ref, f32[1]{0:T(128)S(6)} %copy.11.damp_ref, f32[4,64,1024]{2,1,0:T(8,128)S(1)} %copy-done.1, f32[4,16,1024]{2,1,0:T(8,128)S(1)} %collective-permute-done.4.far_ref, bf16[4,64,256]{2,1,0:T(8,128)(2,1)S(1)} %get-tuple-element.26.r_ref, ...), custom_call_target="tpu_custom_call" | custom-call | flops 1600000000 | bytes 1048576 | tf_op jit(solution)/shard_map/back_late/pallas_call | solution.py:271
  27.7 0.0 collective-permute-done.3.near_ref
  27.7 2.8 %early.4.in_ref = f32[4,48,1024]{2,1,0:T(8,128)S(1)} custom-call(s32[1]{0:T(128)} %bitcast.odd_ref, f32[4,64,1024]{2,1,0:T(8,128)S(1)} %get-tuple-element.24.v_ref.f_ref, f32[4,16,1024]{2,1,0:T(8,128)S(1)} %collective-permute-done.3.near_ref, bf16[4,192,256]{2,1,0:T(8,128)(2,1)S(1)} %get-tuple-element.28.r_ref, bf16[4,1024,256]{2,1,0:T(8,128)(2,1)S(1)} %get-tuple-element.27.c_ref), custom_call_target="tpu_custom_call" | custom-call | flops 2800000000 | bytes 1048576 | tf_op jit(solution)/shard_map/early/pallas_call | solution.py:191
  30.5 1.7 %last_late.1 = (f32[4,64,1024]{2,1,0:T(8,128)S(1)}, f32[8,128]{1,0:T(8,128)S(1)}) custom-call(s32[1]{0:T(128)} %bitcast.odd_ref, f32[1]{0:T(128)S(6)} %copy.11.damp_ref, f32[4,64,1024]{2,1,0:T(8,128)S(1)} %get-tuple-element.24.v_ref.f_ref, f32[4,16,1024]{2,1,0:T(8,128)S(1)} %collective-permute-done.2.far_ref, ...), custom_call_target="tpu_custom_call" | custom-call | flops 1800000000 | bytes 1048576 | tf_op jit(solution)/shard_map/last_late/pallas_call | solution.py:307
  32.2 0.1 collective-permute-start.6
  32.3 1.1 %collective-permute-done.6 = f32[8,128]{1,0:T(8,128)S(1)} collective-permute-done((f32[8,128]{1,0:T(8,128)S(1)}, f32[8,128]{1,0:T(8,128)S(1)}, u32[]{:S(2)}, u32[]{:S(2)}) %collective-permute-start.6) | collective-permute-done | bytes 4128 | tf_op jit(solution)/shard_map/ppermute | solution.py:360
  33.4 1.1 %collective-permute-start.7 = (f32[8,128]{1,0:T(8,128)S(1)}, f32[8,128]{1,0:T(8,128)S(1)}, u32[]{:S(2)}, u32[]{:S(2)}) collective-permute-start(f32[8,128]{1,0:T(8,128)S(1)} %add.18), channel_id=1, source_target_pairs={{0,2},{1,3},{2,0},{3,1},{4,6},{5,7},{6,4},{7,5},{8,10},{9,11},{10,... | collective-permute-start | bytes 12296 | tf_op jit(solution)/shard_map/ppermute | solution.py:360
  34.5 2.5 %collective-permute-done.7 = f32[8,128]{1,0:T(8,128)S(1)} collective-permute-done((f32[8,128]{1,0:T(8,128)S(1)}, f32[8,128]{1,0:T(8,128)S(1)}, u32[]{:S(2)}, u32[]{:S(2)}) %collective-permute-start.7) | collective-permute-done | bytes 4128 | tf_op jit(solution)/shard_map/ppermute | solution.py:360
  37.0 1.6 %collective-permute-start.8 = (f32[8,128]{1,0:T(8,128)S(1)}, f32[8,128]{1,0:T(8,128)S(1)}, u32[]{:S(2)}, u32[]{:S(2)}) collective-permute-start(f32[8,128]{1,0:T(8,128)S(1)} %add.19), channel_id=1, source_target_pairs={{0,4},{1,5},{2,6},{3,7},{4,0},{5,1},{6,2},{7,3},{8,12},{9,13},{10,... | collective-permute-start | bytes 12296 | tf_op jit(solution)/shard_map/ppermute | solution.py:360
  38.6 2.0 %collective-permute-done.8 = f32[8,128]{1,0:T(8,128)S(1)} collective-permute-done((f32[8,128]{1,0:T(8,128)S(1)}, f32[8,128]{1,0:T(8,128)S(1)}, u32[]{:S(2)}, u32[]{:S(2)}) %collective-permute-start.8) | collective-permute-done | bytes 4128 | tf_op jit(solution)/shard_map/ppermute | solution.py:360
  40.6 2.6 %collective-permute-start.9 = (f32[8,128]{1,0:T(8,128)S(1)}, f32[8,128]{1,0:T(8,128)S(1)}, u32[]{:S(2)}, u32[]{:S(2)}) collective-permute-start(f32[8,128]{1,0:T(8,128)S(1)} %add.20.mine_ref), channel_id=1, source_target_pairs={{0,8},{1,9},{2,10},{3,11},{4,12},{5,13},{6,14},{7,15},{8,0},{9,1},... | collective-permute-start | bytes 12296 | tf_op jit(solution)/shard_map/ppermute | solution.py:360
  43.2 1.9 %collective-permute-done.9.other_ref = f32[8,128]{1,0:T(8,128)S(1)} collective-permute-done((f32[8,128]{1,0:T(8,128)S(1)}, f32[8,128]{1,0:T(8,128)S(1)}, u32[]{:S(2)}, u32[]{:S(2)}) %collective-permute-start.9) | collective-permute-done | bytes 4128 | tf_op jit(solution)/shard_map/ppermute | solution.py:360
  45.2 2.3 %final.1 = (f32[4,64,1024]{2,1,0:T(8,128)}, f32[4,64,1024]{2,1,0:T(8,128)}, f32[4,64,1024]{2,1,0:T(8,128)}, f32[4,64,1024]{2,1,0:T(8,128)}) custom-call(f32[1]{0:T(128)S(6)} %copy.11.damp_ref, f32[8,128]{1,0:T(8,128)S(1)} %add.20.mine_ref, f32[8,128]{1,0:T(8,128)S(1)} %collective-permute-done.9.other_ref, f32[4,64,1024]{2,1,0:T(8,128)S(1)} %copy-done.2, ...), custom_call_target="tpu_custom_call" | custom-call | flops 2000000000 | bytes 1048576 | tf_op jit(solution)/shard_map/final/pallas_call | solution.py:347
  (17 shorter events, 0.1 us)
Async XLA Ops:
  0.6 10.3 %copy-start.6 = (f32[4,4,31]{2,1,0:T(4,128)S(1)}, f32[4,4,31]{2,1,0:T(4,128)}, u32[]{:S(2)}) copy-start(f32[4,4,31]{2,1,0:T(4,128)} %param.11) | copy-start | bytes 5956
  0.6 10.3 %copy-start.7 = (f32[4,4,31]{2,1,0:T(4,128)S(1)}, f32[4,4,31]{2,1,0:T(4,128)}, u32[]{:S(2)}) copy-start(f32[4,4,31]{2,1,0:T(4,128)} %param.12) | copy-start | bytes 5956
  0.7 1.2 %copy-start = (f32[4,64,1024]{2,1,0:T(8,128)S(1)}, f32[4,64,1024]{2,1,0:T(8,128)}, u32[]{:S(2)}) copy-start(f32[4,64,1024]{2,1,0:T(8,128)} %r_ref.3) | copy-start | bytes 3145732
  1.9 1.2 %copy-start.4 = (f32[4,64,1024]{2,1,0:T(8,128)S(1)}, f32[4,64,1024]{2,1,0:T(8,128)}, u32[]{:S(2)}) copy-start(f32[4,64,1024]{2,1,0:T(8,128)} %p_ref.3) | copy-start | bytes 3145732
  3.2 9.4 %collective-permute-start.1 = (f32[4,16,1024]{2,1,0:T(8,128)S(1)}, f32[4,16,1024]{2,1,0:T(8,128)S(1)}, u32[]{:S(2)}, u32[]{:S(2)}) collective-permute-start(f32[4,16,1024]{2,1,0:T(8,128)S(1)} %get-tuple-element.22), channel_id=1, source_target_pairs={{0,1},{1,0},{2,3},{3,2},{4,5},{5,4},{6,7},{7,6},{8,9},{9,8},{10,11... | collective-permute-start | bytes 786440 | tf_op jit(solution)/shard_map/ppermute | solution.py:360
  3.8 11.8 %collective-permute-start = (f32[4,16,1024]{2,1,0:T(8,128)S(1)}, f32[4,16,1024]{2,1,0:T(8,128)S(1)}, u32[]{:S(2)}, u32[]{:S(2)}) collective-permute-start(f32[4,16,1024]{2,1,0:T(8,128)S(1)} %get-tuple-element.19), channel_id=1, source_target_pairs={{1,2},{2,1},{3,4},{4,3},{5,6},{6,5},{7,8},{8,7},{9,10},{10,9},{11,... | collective-permute-start | bytes 786440 | tf_op jit(solution)/shard_map/ppermute | solution.py:376
  4.4 21.8 %collective-permute-start.4 = (f32[4,16,1024]{2,1,0:T(8,128)S(1)}, f32[4,16,1024]{2,1,0:T(8,128)S(1)}, u32[]{:S(2)}, u32[]{:S(2)}) collective-permute-start(f32[4,16,1024]{2,1,0:T(8,128)S(1)} %get-tuple-element.29), channel_id=1, source_target_pairs={{1,2},{2,1},{3,4},{4,3},{5,6},{6,5},{7,8},{8,7},{9,10},{10,9},{11,... | collective-permute-start | bytes 786440 | tf_op jit(solution)/shard_map/ppermute | solution.py:376
  5.1 18.3 %collective-permute-start.5 = (f32[4,16,1024]{2,1,0:T(8,128)S(1)}, f32[4,16,1024]{2,1,0:T(8,128)S(1)}, u32[]{:S(2)}, u32[]{:S(2)}) collective-permute-start(f32[4,16,1024]{2,1,0:T(8,128)S(1)} %get-tuple-element.30), channel_id=1, source_target_pairs={{0,1},{1,0},{2,3},{3,2},{4,5},{5,4},{6,7},{7,6},{8,9},{9,8},{10,11... | collective-permute-start | bytes 786440 | tf_op jit(solution)/shard_map/ppermute | solution.py:360
  11.0 1.7 %copy-start.5 = (f32[4,64,1024]{2,1,0:T(8,128)S(1)}, f32[4,64,1024]{2,1,0:T(8,128)}, u32[]{:S(2)}) copy-start(f32[4,64,1024]{2,1,0:T(8,128)} %p_ref.3) | copy-start | bytes 3145732
  12.7 2.9 %copy-start.3 = (f32[4,64,1024]{2,1,0:T(8,128)S(1)}, f32[4,64,1024]{2,1,0:T(8,128)}, u32[]{:S(2)}) copy-start(f32[4,64,1024]{2,1,0:T(8,128)} %grad_ref.1) | copy-start | bytes 3145732
  15.6 7.9 %copy-start.1 = (f32[4,64,1024]{2,1,0:T(8,128)S(1)}, f32[4,64,1024]{2,1,0:T(8,128)}, u32[]{:S(2)}) copy-start(f32[4,64,1024]{2,1,0:T(8,128)} %r_ref.3) | copy-start | bytes 3145732
  17.1 13.4 %collective-permute-start.2 = (f32[4,16,1024]{2,1,0:T(8,128)S(1)}, f32[4,16,1024]{2,1,0:T(8,128)S(1)}, u32[]{:S(2)}, u32[]{:S(2)}) collective-permute-start(f32[4,16,1024]{2,1,0:T(8,128)S(1)} %get-tuple-element.25), channel_id=1, source_target_pairs={{1,2},{2,1},{3,4},{4,3},{5,6},{6,5},{7,8},{8,7},{9,10},{10,9},{11,... | collective-permute-start | bytes 786440 | tf_op jit(solution)/shard_map/ppermute | solution.py:376
  18.0 9.7 %collective-permute-start.3 = (f32[4,16,1024]{2,1,0:T(8,128)S(1)}, f32[4,16,1024]{2,1,0:T(8,128)S(1)}, u32[]{:S(2)}, u32[]{:S(2)}) collective-permute-start(f32[4,16,1024]{2,1,0:T(8,128)S(1)} %constant_dynamic-slice_fusion), channel_id=1, source_target_pairs={{0,1},{1,0},{2,3},{3,2},{4,5},{5,4},{6,7},{7,6},{8,9},{9,8},{10,11... | collective-permute-start | bytes 786440 | tf_op jit(solution)/shard_map/ppermute | solution.py:360
  23.4 2.8 %copy-start.2 = (f32[4,64,1024]{2,1,0:T(8,128)S(1)}, f32[4,64,1024]{2,1,0:T(8,128)}, u32[]{:S(2)}) copy-start(f32[4,64,1024]{2,1,0:T(8,128)} %x_ref.1) | copy-start | bytes 3145732
  32.2 1.2 %collective-permute-start.6 = (f32[8,128]{1,0:T(8,128)S(1)}, f32[8,128]{1,0:T(8,128)S(1)}, u32[]{:S(2)}, u32[]{:S(2)}) collective-permute-start(f32[8,128]{1,0:T(8,128)S(1)} %get-tuple-element.32), channel_id=1, source_target_pairs={{0,1},{1,0},{2,3},{3,2},{4,5},{5,4},{6,7},{7,6},{8,9},{9,8},{10,11... | collective-permute-start | bytes 12296 | tf_op jit(solution)/shard_map/ppermute | solution.py:360
  33.4 3.6 %collective-permute-start.7 = (f32[8,128]{1,0:T(8,128)S(1)}, f32[8,128]{1,0:T(8,128)S(1)}, u32[]{:S(2)}, u32[]{:S(2)}) collective-permute-start(f32[8,128]{1,0:T(8,128)S(1)} %add.18), channel_id=1, source_target_pairs={{0,2},{1,3},{2,0},{3,1},{4,6},{5,7},{6,4},{7,5},{8,10},{9,11},{10,... | collective-permute-start | bytes 12296 | tf_op jit(solution)/shard_map/ppermute | solution.py:360
  37.0 3.6 %collective-permute-start.8 = (f32[8,128]{1,0:T(8,128)S(1)}, f32[8,128]{1,0:T(8,128)S(1)}, u32[]{:S(2)}, u32[]{:S(2)}) collective-permute-start(f32[8,128]{1,0:T(8,128)S(1)} %add.19), channel_id=1, source_target_pairs={{0,4},{1,5},{2,6},{3,7},{4,0},{5,1},{6,2},{7,3},{8,12},{9,13},{10,... | collective-permute-start | bytes 12296 | tf_op jit(solution)/shard_map/ppermute | solution.py:360
  40.6 4.5 %collective-permute-start.9 = (f32[8,128]{1,0:T(8,128)S(1)}, f32[8,128]{1,0:T(8,128)S(1)}, u32[]{:S(2)}, u32[]{:S(2)}) collective-permute-start(f32[8,128]{1,0:T(8,128)S(1)} %add.20.mine_ref), channel_id=1, source_target_pairs={{0,8},{1,9},{2,10},{3,11},{4,12},{5,13},{6,14},{7,15},{8,0},{9,1},... | collective-permute-start | bytes 12296 | tf_op jit(solution)/shard_map/ppermute | solution.py:360

commit v3 on v2

v3 whole, which is shorter than its diff:
```python
import functools

import jax
import jax.numpy as jnp
from jax import lax
from jax.experimental import pallas as pl
from jax.experimental.pallas import tpu as pltpu
from jax.sharding import PartitionSpec as P

F32 = jnp.float32
BF16 = jnp.bfloat16
EDGE = 16
LANE = 128
WIDE = 256
VM = pl.BlockSpec(memory_space=pltpu.VMEM)
SM = pl.BlockSpec(memory_space=pltpu.SMEM)
ANY = pl.BlockSpec(memory_space=pl.ANY)
LIMIT = 20 * 2**20


def split(x):
    hi = x.astype(BF16)
    return hi, (x - hi.astype(F32)).astype(BF16)


def params():
    return pltpu.CompilerParams(vmem_limit_bytes=LIMIT)


def cost(us):
    return pl.CostEstimate(flops=int(us * 1.0e9), bytes_accessed=1 << 20, transcendentals=0)


def f32(*shape):
    return jax.ShapeDtypeStruct(shape, F32)


def edges_kernel(odd_ref, v_ref, after_ref, far_out, near_out, sems):
    rows = v_ref.shape[1]
    odd = odd_ref[0]
    copies = []
    for k, (side, dst) in enumerate(((odd, far_out), (1 - odd, near_out))):
        count = dst.shape[1]
        here = pl.ds(pl.multiple_of(side * (rows - count), EDGE), count)
        copies.append(pltpu.make_async_copy(v_ref.at[:, here, :], dst, sems.at[k]))
    for c in copies:
        c.start()
    for c in copies:
        c.wait()


def edges(odd, v, after, far, near):
    depth, rows, columns = v.shape
    return pl.pallas_call(
        edges_kernel,
        out_shape=(f32(depth, far, columns), f32(depth, near, columns)),
        in_specs=[SM, VM, ANY],
        out_specs=[VM] * 2,
        scratch_shapes=[pltpu.SemaphoreType.DMA((2,))],
        compiler_params=params(),
        cost_estimate=cost(0.2),
        name="edges",
    )(odd, v, after)


def one_hot(count, at):
    tap = lax.broadcasted_iota(jnp.int32, (count, WIDE), 0)
    lane = lax.broadcasted_iota(jnp.int32, (count, WIDE), 1)
    return jnp.where(lane == (at(tap) + WIDE) % WIDE, 1.0, 0.0).astype(BF16)


def pick(parts_and_places):
    got = None
    for part, place in parts_and_places:
        term = jnp.dot(part, place, preferred_element_type=F32)
        got = term if got is None else got + term
    return got


def prep_kernel(depth, inner, row_ref, col_ref, p_ref, *refs):
    outs, sums_ref, bases = refs[:6], refs[6], refs[7:]
    sums_ref[...] = jnp.zeros_like(sums_ref)
    for o in range(depth):
        sums_ref[2:3, :] += folded(p_ref[o] * p_ref[o])
    count = row_ref.shape[1]
    last = count - 1
    row_hi, row_lo = split(row_ref[...])
    col_hi, col_lo = split(col_ref[...])
    window = LANE + 2 * EDGE
    lane = lax.broadcasted_iota(jnp.int32, (window, WIDE), 1)
    for adjoint in (False, True):
        r_early, r_late, c_out = outs[3:] if adjoint else outs[:3]
        tall = EDGE if adjoint else 2 * EDGE
        turn = (lambda a: last - a) if adjoint else (lambda a: a)
        for base, gap in ((bases[0], inner + 2 * EDGE), (bases[1], tall + 2 * EDGE)):
            base[...] = pick((
                (row_hi, one_hot(count, turn)),
                (row_hi, one_hot(count, lambda a: turn(a) + gap)),
                (row_lo, one_hot(count, lambda a: turn(a) + 2 * gap)),
            ))
        bases[2][...] = pick(((col_hi, one_hot(count, lambda a: -turn(a))),))
        bases[3][...] = pick(((col_lo, one_hot(count, lambda a: LANE - turn(a))),))

        def banded(base, pair, rows, shift):
            wide = jnp.broadcast_to(base[pl.ds(pair, 1), :], (rows, WIDE))
            return pltpu.roll(wide, shift, 1, stride=1, stride_axis=0)

        for o in range(depth):
            for s in range(depth):
                pair = s * depth + o if adjoint else o * depth + s
                r_early[s, o * inner:(o + 1) * inner, :] = banded(bases[0], pair, inner, 1).astype(BF16)
                r_late[s, o * tall:(o + 1) * tall, :] = banded(bases[1], pair, tall, 1).astype(BF16)
                band = jnp.where(lane < LANE, banded(bases[2], pair, window, 0), banded(bases[3], pair, window, 0))
                c_out[o, s * WIDE:s * WIDE + window, :] = band.astype(BF16)
                c_out[o, s * WIDE + window:(s + 1) * WIDE, :] = jnp.zeros((WIDE - window, WIDE), BF16)


def prep(row, col, inner, direction):
    depth, _, count = row.shape
    pairs = depth * depth

    def bands(tall):
        return (
            jax.ShapeDtypeStruct((depth, depth * inner, WIDE), BF16),
            jax.ShapeDtypeStruct((depth, depth * tall, WIDE), BF16),
            jax.ShapeDtypeStruct((depth, depth * WIDE, WIDE), BF16),
        )

    return pl.pallas_call(
        functools.partial(prep_kernel, depth, inner),
        out_shape=bands(2 * EDGE) + bands(EDGE) + (f32(8, LANE),),
        in_specs=[VM] * 3,
        out_specs=[VM] * 7,
        scratch_shapes=[pltpu.VMEM((pairs, WIDE), F32)] * 4,
        compiler_params=params(),
        cost_estimate=cost(1.5),
        name="prep",
    )(row.reshape(pairs, count), col.reshape(pairs, count), direction)


def shifted(x, border):
    wide = jnp.concatenate([x, jnp.zeros((x.shape[0], LANE), F32)], axis=1)
    return split(pltpu.roll(wide, border, 1))


def put(win, at, group, hi, lo):
    rows = hi.shape[0]
    for g, part in enumerate((hi, lo, hi)):
        win[pl.ds(pl.multiple_of(at + g * group, EDGE), rows), :] = part


def along_rows(r_ref, win, v_hi, v_lo, s, group):
    if 3 * group < WIDE:
        win[s, 3 * group:, :] = jnp.zeros((WIDE - 3 * group, win.shape[2]), BF16)
    got = jnp.dot(r_ref[s], win[s], preferred_element_type=F32)
    v_hi[s], v_lo[s] = split(got)


def along_columns(sources, c_ref, o, rows, columns, depth):
    tall = []
    blocks = columns // LANE
    for pair in sources:
        for part in pair:
            for n in range(blocks):
                tall.append(jnp.concatenate(
                    [part[s, o * rows:(o + 1) * rows, n * LANE:n * LANE + WIDE] for s in range(depth)], axis=1))
    got = jnp.dot(jnp.concatenate(tall, axis=0), c_ref[o], preferred_element_type=F32)
    planes = []
    for k in range(len(sources)):
        out = []
        for n in range(blocks):
            at = (2 * k * blocks + n) * rows
            top, low = got[at:at + rows], got[at + blocks * rows:at + (blocks + 1) * rows]
            out.append(top[:, :LANE] + (top[:, LANE:] + low[:, :LANE]))
        planes.append(jnp.concatenate(out, axis=1))
    return planes


def folded(x):
    part = jnp.sum(x.reshape(x.shape[0] // 8, 8, x.shape[1]), axis=0)
    part = sum(part[:, n:n + LANE] for n in range(0, x.shape[1], LANE))
    return jnp.sum(part, axis=0, keepdims=True)


def early_kernel(border, odd_ref, v_ref, near_ref, r_ref, c_ref, out_ref, win, v_hi, v_lo):
    depth, rows, columns = v_ref.shape
    inner = rows - EDGE
    group = rows + EDGE
    odd = odd_ref[0]
    for s in range(depth):
        put(win.at[s], odd * EDGE, group, *shifted(v_ref[s], border))
        put(win.at[s], (1 - odd) * rows, group, *shifted(near_ref[s], border))
        along_rows(r_ref, win, v_hi, v_lo, s, group)
    for o in range(depth):
        out_ref[o], = along_columns(((v_hi, v_lo),), c_ref, o, inner, columns, depth)


def early(odd, v, near, r, c, border):
    depth, rows, columns = v.shape
    inner = rows - EDGE
    wide = columns + LANE
    return pl.pallas_call(
        functools.partial(early_kernel, border),
        out_shape=f32(depth, inner, columns),
        in_specs=[SM, VM, VM, VM, VM],
        out_specs=VM,
        scratch_shapes=[
            pltpu.VMEM((depth, WIDE, wide), BF16),
            pltpu.VMEM((depth, depth * inner, wide), BF16),
            pltpu.VMEM((depth, depth * inner, wide), BF16),
        ],
        compiler_params=params(),
        cost_estimate=cost(2.8),
        name="early",
    )(odd, v, near, r, c)


def late_rows(border, odd, v_ref, far_ref, r_ref, win, v_hi, v_lo):
    depth, rows, _ = v_ref.shape
    beyond = far_ref.shape[1]
    group = beyond + 2 * EDGE
    start = pl.multiple_of(odd * (rows - 2 * EDGE), EDGE)
    for s in range(depth):
        put(win.at[s], (1 - odd) * beyond, group, *shifted(v_ref[s, pl.ds(start, 2 * EDGE), :], border))
        put(win.at[s], odd * 2 * EDGE, group, *shifted(far_ref[s], border))
        along_rows(r_ref, win, v_hi, v_lo, s, group)


def late_scratch(depth, columns, tall):
    wide = columns + LANE
    return [
        pltpu.VMEM((depth, WIDE, wide), BF16),
        pltpu.VMEM((depth, depth * tall, wide), BF16),
        pltpu.VMEM((depth, depth * tall, wide), BF16),
    ]


def image_kernel(border, odd_ref, more_ref, v_ref, far_ref, r_ref, c_ref, in_ref, grad_ref, before_ref, after_ref, out_ref, beyond_ref, sums_ref, win, v_hi, v_lo):
    depth, rows, columns = v_ref.shape
    inner = rows - EDGE
    odd = odd_ref[0]
    more = more_ref[0]
    late_rows(border, odd, v_ref, far_ref, r_ref, win, v_hi, v_lo)
    sums_ref[...] = before_ref[...]
    for o in range(depth):
        both, = along_columns(((v_hi, v_lo),), c_ref, o, 2 * EDGE, columns, depth)
        first, second = both[:EDGE], both[EDGE:]
        edge = jnp.where(odd == 1, first, second)
        beyond_ref[o] = jnp.where(more == 1, jnp.where(odd == 1, second, first), 0.0)
        out_ref[o, pl.ds(pl.multiple_of(odd * inner, EDGE), EDGE), :] = edge
        out_ref[o, pl.ds(pl.multiple_of((1 - odd) * EDGE, EDGE), inner), :] = in_ref[o]
        sums_ref[0:1, :] += folded(grad_ref[o] * grad_ref[o])
        sums_ref[1:2, :] += folded(in_ref[o] * in_ref[o]) + folded(edge * edge)


def image_late(odd, more, v, far, r, c, inside, grad, before, after, border):
    depth, rows, columns = v.shape
    return pl.pallas_call(
        functools.partial(image_kernel, border),
        out_shape=(f32(depth, rows, columns), f32(depth, EDGE, columns), f32(8, LANE)),
        in_specs=[SM, SM] + [VM] * 7 + [ANY],
        out_specs=[VM] * 3,
        scratch_shapes=late_scratch(depth, columns, 2 * EDGE),
        compiler_params=params(),
        cost_estimate=cost(2.0),
        name="image_late",
    )(odd, more, v, far, r, c, inside, grad, before, after)


def last_kernel(border, odd_ref, damp_ref, res_ref, res_far_ref, g_in_ref, x_ref, f_ref, f_far_ref, h_in_ref, p_ref, r_ref, c_ref, before_ref,
                g_ref, h_ref, sums_ref, win, v_hi, v_lo, win2, v_hi2, v_lo2):
    depth, rows, columns = res_ref.shape
    inner = rows - EDGE
    odd = odd_ref[0]
    damp = damp_ref[0]
    late_rows(border, odd, res_ref, res_far_ref, r_ref, win, v_hi, v_lo)
    late_rows(border, odd, f_ref, f_far_ref, r_ref, win2, v_hi2, v_lo2)
    sums_ref[...] = before_ref[...]
    for o in range(depth):
        g_edge, h_edge = along_columns(((v_hi, v_lo), (v_hi2, v_lo2)), c_ref, o, EDGE, columns, depth)
        for at, count, g, h in (
            (pl.multiple_of(odd * inner, EDGE), EDGE, g_edge, h_edge),
            (pl.multiple_of((1 - odd) * EDGE, EDGE), inner, g_in_ref[o], h_in_ref[o]),
        ):
            here = pl.ds(at, count)
            g = g - damp * x_ref[o, here, :]
            h = h + damp * p_ref[o, here, :]
            g_ref[o, here, :] = g
            h_ref[o, here, :] = h
            sums_ref[3:4, :] += folded(g * g)
            sums_ref[4:5, :] += folded(g * h)
            sums_ref[5:6, :] += folded(h * h)


def last_late(odd, damp, res, res_far, g_in, x, image, image_far, h_in, p, r, c, before, border):
    depth, rows, columns = res.shape
    return pl.pallas_call(
        functools.partial(last_kernel, border),
        out_shape=(f32(depth, rows, columns), f32(depth, rows, columns), f32(8, LANE)),
        in_specs=[SM, SM] + [VM] * 11,
        out_specs=[VM] * 3,
        scratch_shapes=late_scratch(depth, columns, EDGE) * 2,
        compiler_params=params(),
        cost_estimate=cost(2.6),
        name="last_late",
    )(odd, damp, res, res_far, g_in, x, image, image_far, h_in, p, r, c, before)


def final_kernel(damp_ref, mine_ref, other_ref, x_ref, r_ref, p_ref, f_ref, g_ref, h_ref,
                 nx_out, nr_out, ng_out, np_out, nx, nr, ng, nd, sems):
    depth = x_ref.shape[0]
    damp = damp_ref[0]
    sums = jnp.sum(mine_ref[...] + other_ref[...], axis=1, keepdims=True)
    before, image, direction, gg, gh, hh = (sums[k:k + 1, :] for k in range(6))
    step = before / (image + damp * direction)
    after = gg - step * (2.0 * gh - step * hh)
    ratio = after / before
    copies = []
    for o in range(depth):
        p = p_ref[o]
        new = g_ref[o] - step * h_ref[o]
        for k, (buf, out, value) in enumerate((
            (nx, nx_out, x_ref[o] + step * p),
            (nr, nr_out, r_ref[o] - step * f_ref[o]),
            (ng, ng_out, new),
            (nd, np_out, new + ratio * p),
        )):
            buf[o] = value
            copies.append(pltpu.make_async_copy(buf.at[o], out.at[o], sems.at[o, k]))
            copies[-1].start()
    for c in copies:
        c.wait()


def final(damp, mine, other, x, r, p, f, g, h):
    shape = x.shape
    return pl.pallas_call(
        final_kernel,
        out_shape=(f32(*shape),) * 4,
        in_specs=[SM] + [VM] * 8,
        out_specs=[ANY] * 4,
        scratch_shapes=[pltpu.VMEM(shape, F32)] * 4 + [pltpu.SemaphoreType.DMA((shape[0], 4))],
        compiler_params=params(),
        cost_estimate=cost(2.0),
        name="final",
    )(damp, mine, other, x, r, p, f, g, h)


def swap(values, axis, step):
    return lax.ppermute(values, axis, [(i, i ^ step) for i in range(lax.axis_size(axis))])


def body(solution, residual, gradient, direction, row_taps, col_taps, damping):
    border = row_taps.shape[2] // 2
    depth, rows, columns = direction.shape
    inner = rows - EDGE
    peers = lax.axis_size("lat")
    odd = lax.axis_index("lat") % 2
    odd_arr = jnp.full((1,), odd, jnp.int32)
    far_pairs = [p for a in range(1, peers - 1, 2) for p in ((a, a + 1), (a + 1, a))]

    def near_swap(v):
        return swap(v, "lat", 1)

    def far_swap(v):
        return lax.ppermute(v, "lat", far_pairs)

    place = lax.axis_index("lat")
    more = jnp.full((1,), jnp.where(odd == 1, place < peers - 1, place > 0), jnp.int32)

    p_far_edge, p_near_edge = edges(odd_arr, direction, odd_arr, 2 * EDGE, EDGE)
    p_far, p_near = far_swap(p_far_edge), near_swap(p_near_edge)
    re, rl, c, rae, ral, ca, sums = prep(row_taps, col_taps, inner, direction)

    r_far_edge = lax.dynamic_slice_in_dim(residual, odd * inner, EDGE, axis=1)
    r_near_edge = lax.dynamic_slice_in_dim(residual, (1 - odd) * inner, EDGE, axis=1)
    p_near, r_near_edge = lax.optimization_barrier((p_near, r_near_edge))
    r_near = near_swap(r_near_edge)
    image_in = early(odd_arr, direction, p_near, re, c, border)
    f_near = near_swap(lax.dynamic_slice_in_dim(image_in, (1 - odd) * (inner - EDGE), EDGE, axis=1))
    g_in = early(odd_arr, residual, r_near, rae, ca, border)
    g_in, r_far_edge = lax.optimization_barrier((g_in, r_far_edge))
    r_far = far_swap(r_far_edge)
    image, f_far, sums = image_late(odd_arr, more, direction, p_far, rl, c, image_in, gradient, sums, g_in, border)
    h_in = early(odd_arr, image, f_near, rae, ca, border)
    g, h, sums = last_late(odd_arr, damping, residual, r_far, g_in, solution, image, f_far, h_in, direction, ral, ca, sums, border)

    step = 1
    while 2 * step < peers:
        sums = sums + swap(sums, "lat", step)
        step *= 2
    other = swap(sums, "lat", step)
    return final(damping, sums, other, solution, residual, direction, image, g, h)


def solution(mesh):
    split_rows = P("stack", "lat", None)
    return jax.shard_map(
        body,
        mesh=mesh,
        in_specs=(split_rows,) * 4 + (P(),) * 3,
        out_specs=(split_rows,) * 4,
        check_vma=False,
    )
```

time: 47.8 us -> 45.3 us (0.948)
  waiting for transfers between devices: 7.61 us -> 5.59 us
  starting transfers between devices: 18.7 us -> 18 us
    ppermute x7, waiting for transfers between devices: 7.6 us -> 5.58 us  [swap(): lax.ppermute(values, axis, [(i, i ^ step) for i in range(lax.axis_size(ax...]
    pallas_call x3 -> x2, Pallas kernels: 3.18 us -> 1.86 us  [the longest x1 1.79 us: prep(): pl.pallas_call(functools.partial(prep_kernel, depth, inner), out_shape=ba...]
    unnamed x16 -> x14, local copies, waits for them, and re-layouts: 2.48 us -> 1.24 us
    pallas_call x1, Pallas kernels: 1.66 us -> 2.75 us  [last_late(): pl.pallas_call(functools.partial(last_kernel, border), out_shape=(f32(dep...]
    dynamic_slice x0 -> x1, local copies, waits for them, and re-layouts: none -> 1.08 us  [body(): r_far_edge = lax.dynamic_slice_in_dim(residual, odd * inner, EDGE, axis=1)]
    ppermute x3 -> x2, starting transfers between devices: 2.2 us -> 1.54 us  [far_swap(): return lax.ppermute(v, 'lat', far_pairs)]
    pallas_call x1, Pallas kernels: 1.51 us -> 2.1 us  [image_late(): pl.pallas_call(functools.partial(image_kernel, border), out_shape=(f32(de...]
  transfers between devices with their start and end apart: 10 -> 9, of which waited for: 4 -> 4; matrix products, arithmetic and copies ran while one was open for 0% -> 2% of each run, Pallas kernels for 27% -> 27%
where the time goes in v3:
time: 45.3 us; the launch traced here: 45.1 us
  starting transfers between devices  18 us (40%)
  Pallas kernels  17.4 us (38%)
  waiting for transfers between devices  5.59 us (12%)
  local copies, waits for them, and re-layouts  2.35 us (5%)
  between operations  1.68 us (4%)
    ppermute x7, starting transfers between devices, swap(): lax.ppermute(values, axis, [(i, i ^ step) for i in range(lax.axis_size(ax...  16.5 us
    pallas_call x3, Pallas kernels, early(): pl.pallas_call(functools.partial(early_kernel, border), out_shape=f32(dep...  8.41 us
    ppermute x7, waiting for transfers between devices, swap(): lax.ppermute(values, axis, [(i, i ^ step) for i in range(lax.axis_size(ax...  5.58 us
    pallas_call x1, Pallas kernels, last_late(): pl.pallas_call(functools.partial(last_kernel, border), out_shape=(f32(dep...  2.75 us
    pallas_call x1, Pallas kernels, final(): pl.pallas_call(final_kernel, out_shape=(f32(*shape),) * 4, in_specs=[SM]...  2.29 us
    pallas_call x1, Pallas kernels, image_late(): pl.pallas_call(functools.partial(image_kernel, border), out_shape=(f32(de...  2.1 us
    pallas_call x1, Pallas kernels, prep(): pl.pallas_call(functools.partial(prep_kernel, depth, inner), out_shape=ba...  1.79 us
    ppermute x2, starting transfers between devices, far_swap(): return lax.ppermute(v, 'lat', far_pairs)  1.54 us
  transfers between devices with their start and end apart: 9, of which 4 were waited for; matrix products, arithmetic and copies ran while one was open for 2% of the time, Pallas kernels for 27%

profile of v3, /device:TPU:0, one launch (start us, length us, event | category | flops | bytes accessed | tf_op | source)
XLA Modules:
  0.0 45.1 jit_solution(11449930016190866106)
XLA Ops:
  0.7 1.2 %copy-done = f32[4,64,1024]{2,1,0:T(8,128)S(1)} copy-done((f32[4,64,1024]{2,1,0:T(8,128)S(1)}, f32[4,64,1024]{2,1,0:T(8,128)}, u32[]{:S(2)}) %copy-start) | copy-done | bytes 1048600
  1.9 0.1 edges.1
  2.0 0.5 %collective-permute-start = (f32[4,16,1024]{2,1,0:T(8,128)S(1)}, f32[4,16,1024]{2,1,0:T(8,128)S(1)}, u32[]{:S(2)}, u32[]{:S(2)}) collective-permute-start(f32[4,16,1024]{2,1,0:T(8,128)S(1)} %get-tuple-element.23), channel_id=1, source_target_pairs={{0,1},{1,0},{2,3},{3,2},{4,5},{5,4},{6,7},{7,6},{8,9},{9,8},{10,11... | collective-permute-start | bytes 786440 | tf_op jit(solution)/shard_map/ppermute | solution.py:350
  2.5 0.7 %collective-permute-start.3 = (f32[4,32,1024]{2,1,0:T(8,128)S(1)}, f32[4,32,1024]{2,1,0:T(8,128)S(1)}, u32[]{:S(2)}, u32[]{:S(2)}) collective-permute-start(f32[4,32,1024]{2,1,0:T(8,128)S(1)} %get-tuple-element.29), channel_id=1, source_target_pairs={{1,2},{2,1},{3,4},{4,3},{5,6},{6,5},{7,8},{8,7},{9,10},{10,9},{11,... | collective-permute-start | bytes 1572872 | tf_op jit(solution)/shard_map/ppermute | solution.py:366
  3.9 1.1 %constant_dynamic-slice_fusion.1 = (f32[4,16,1024]{2,1,0:T(8,128)S(1)}, f32[4,16,1024]{2,1,0:T(8,128)S(1)}) fusion(f32[4,64,1024]{2,1,0:T(8,128)} %r_ref.1, s32[]{:T(128)S(6)} %select_n.22, s32[]{:T(128)S(6)} %select_n.21), kind=kLoop, calls=%fused_computation.1 | loop fusion | bytes 1048584 | tf_op jit(solution)/shard_map/dynamic_slice | solution.py:375
  5.0 1.8 %prep.1 = (bf16[4,192,256]{2,1,0:T(8,128)(2,1)S(1)}, bf16[4,128,256]{2,1,0:T(8,128)(2,1)S(1)}, bf16[4,1024,256]{2,1,0:T(8,128)(2,1)S(1)}, bf16[4,192,256]{2,1,0:...) custom-call(f32[16,31]{1,0:T(8,128)S(1)} %bitcast.4, ...), custom_call_target="tpu_custom_call" | custom-call | flops 1500000000 | bytes 1048576 | tf_op jit(solution)/shard_map/prep/pallas_call | solution.py:129
  6.8 0.0 collective-permute-done.near_ref
  6.8 4.1 %collective-permute-start.1 = (f32[4,16,1024]{2,1,0:T(8,128)S(1)}, f32[4,16,1024]{2,1,0:T(8,128)S(1)}, u32[]{:S(2)}, u32[]{:S(2)}) collective-permute-start(f32[4,16,1024]{2,1,0:T(8,128)S(1)} %get-tuple-element.24), channel_id=1, source_target_pairs={{0,1},{1,0},{2,3},{3,2},{4,5},{5,4},{6,7},{7,6},{8,9},{9,8},{10,11... | collective-permute-start | bytes 786440 | tf_op jit(solution)/shard_map/ppermute | solution.py:350
  10.9 2.8 %early.4.in_ref = f32[4,48,1024]{2,1,0:T(8,128)S(1)} custom-call(s32[1]{0:T(128)} %bitcast.odd_ref.after_ref, f32[4,64,1024]{2,1,0:T(8,128)S(1)} %copy-done.1, f32[4,16,1024]{2,1,0:T(8,128)S(1)} %collective-permute-done.near_ref, bf16[4,192,256]{2,1,0:T(8,128)(2,1)S(1)} %get-tuple-element.33.r_ref, bf16[4,1024,256]{2,1,0:T(8,128)(2,1)S(1)} %get-tuple-element.31.c_ref), custom_call_target="tpu_custom_call" | custom-call | flops 2800000000 | bytes 1048576 | tf_op jit(solution)/shard_map/early/pallas_call | solution.py:202
  13.7 0.1 collective-permute-start.4
  13.8 0.0 collective-permute-done.1.near_ref
  13.8 0.0 copy-done.2
  13.8 2.8 %early.3.after_ref.g_in_ref = f32[4,48,1024]{2,1,0:T(8,128)S(1)} custom-call(s32[1]{0:T(128)} %bitcast.odd_ref.after_ref, f32[4,64,1024]{2,1,0:T(8,128)S(1)} %copy-done.2, f32[4,16,1024]{2,1,0:T(8,128)S(1)} %collective-permute-done.1.near_ref, bf16[4,192,256]{2,1,0:T(8,128)(2,1)S(1)} %get-tuple-element.25.r_ref, ...), custom_call_target="tpu_custom_call" | custom-call | flops 2800000000 | bytes 1048576 | tf_op jit(solution)/shard_map/early/pallas_call | solution.py:202
  16.6 0.9 %collective-permute-start.2 = (f32[4,16,1024]{2,1,0:T(8,128)S(1)}, f32[4,16,1024]{2,1,0:T(8,128)S(1)}, u32[]{:S(2)}, u32[]{:S(2)}) collective-permute-start(f32[4,16,1024]{2,1,0:T(8,128)S(1)} %get-tuple-element.27), channel_id=1, source_target_pairs={{1,2},{2,1},{3,4},{4,3},{5,6},{6,5},{7,8},{8,7},{9,10},{10,9},{11,... | collective-permute-start | bytes 786440 | tf_op jit(solution)/shard_map/ppermute | solution.py:366
  17.5 0.0 collective-permute-done.3.far_ref
  17.5 0.0 copy-done.3
  17.5 2.1 %image_late.1 = (f32[4,64,1024]{2,1,0:T(8,128)S(1)}, f32[4,16,1024]{2,1,0:T(8,128)S(1)}, f32[8,128]{1,0:T(8,128)S(1)}) custom-call(s32[1]{0:T(128)} %bitcast.odd_ref.after_ref, s32[1]{0:T(128)} %bitcast.3.more_ref, f32[4,64,1024]{2,1,0:T(8,128)S(1)} %copy-done.1, f32[4,32,1024]{2,1,0:T(8,128)S(1)} %collective-permute-done.3.far_ref, ...), custom_call_target="tpu_custom_call" | custom-call | flops 2000000000 | bytes 1048576 | tf_op jit(solution)/shard_map/image_late/pallas_call | solution.py:258
  19.6 0.0 collective-permute-done.4.near_ref
  19.6 0.0 copy-start.4
  19.6 2.8 %early.5.h_in_ref = f32[4,48,1024]{2,1,0:T(8,128)S(1)} custom-call(s32[1]{0:T(128)} %bitcast.odd_ref.after_ref, f32[4,64,1024]{2,1,0:T(8,128)S(1)} %get-tuple-element.35.v_ref.f_ref, f32[4,16,1024]{2,1,0:T(8,128)S(1)} %collective-permute-done.4.near_ref, bf16[4,192,256]{2,1,0:T(8,128)(2,1)S(1)} %get-tuple-element.25.r_ref, ...), custom_call_target="tpu_custom_call" | custom-call | flops 2800000000 | bytes 1048576 | tf_op jit(solution)/shard_map/early/pallas_call | solution.py:202
  22.4 0.0 collective-permute-done.2.res_far_ref
  22.5 0.0 copy-done.4
  22.5 2.7 %last_late.1 = (f32[4,64,1024]{2,1,0:T(8,128)S(1)}, f32[4,64,1024]{2,1,0:T(8,128)S(1)}, f32[8,128]{1,0:T(8,128)S(1)}) custom-call(s32[1]{0:T(128)} %bitcast.odd_ref.after_ref, f32[1]{0:T(128)S(6)} %copy.11.damp_ref, f32[4,64,1024]{2,1,0:T(8,128)S(1)} %copy-done.2, f32[4,16,1024]{2,1,0:T(8,128)S(1)} %collective-permute-done.2.res_far_ref, ...), custom_call_target="tpu_custom_call" | custom-call | flops 2600000000 | bytes 1048576 | tf_op jit(solution)/shard_map/last_late/pallas_call | solution.py:297
  25.2 3.9 %collective-permute-start.5 = (f32[8,128]{1,0:T(8,128)S(1)}, f32[8,128]{1,0:T(8,128)S(1)}, u32[]{:S(2)}, u32[]{:S(2)}) collective-permute-start(f32[8,128]{1,0:T(8,128)S(1)} %get-tuple-element.39), channel_id=1, source_target_pairs={{0,1},{1,0},{2,3},{3,2},{4,5},{5,4},{6,7},{7,6},{8,9},{9,8},{10,11... | collective-permute-start | bytes 12296 | tf_op jit(solution)/shard_map/ppermute | solution.py:350
  29.1 0.8 %collective-permute-done.5 = f32[8,128]{1,0:T(8,128)S(1)} collective-permute-done((f32[8,128]{1,0:T(8,128)S(1)}, f32[8,128]{1,0:T(8,128)S(1)}, u32[]{:S(2)}, u32[]{:S(2)}) %collective-permute-start.5) | collective-permute-done | bytes 4128 | tf_op jit(solution)/shard_map/ppermute | solution.py:350
  29.9 2.7 %collective-permute-start.6 = (f32[8,128]{1,0:T(8,128)S(1)}, f32[8,128]{1,0:T(8,128)S(1)}, u32[]{:S(2)}, u32[]{:S(2)}) collective-permute-start(f32[8,128]{1,0:T(8,128)S(1)} %add.26), channel_id=1, source_target_pairs={{0,2},{1,3},{2,0},{3,1},{4,6},{5,7},{6,4},{7,5},{8,10},{9,11},{10,... | collective-permute-start | bytes 12296 | tf_op jit(solution)/shard_map/ppermute | solution.py:350
  32.6 1.6 %collective-permute-done.6 = f32[8,128]{1,0:T(8,128)S(1)} collective-permute-done((f32[8,128]{1,0:T(8,128)S(1)}, f32[8,128]{1,0:T(8,128)S(1)}, u32[]{:S(2)}, u32[]{:S(2)}) %collective-permute-start.6) | collective-permute-done | bytes 4128 | tf_op jit(solution)/shard_map/ppermute | solution.py:350
  34.2 2.2 %collective-permute-start.7 = (f32[8,128]{1,0:T(8,128)S(1)}, f32[8,128]{1,0:T(8,128)S(1)}, u32[]{:S(2)}, u32[]{:S(2)}) collective-permute-start(f32[8,128]{1,0:T(8,128)S(1)} %add.27), channel_id=1, source_target_pairs={{0,4},{1,5},{2,6},{3,7},{4,0},{5,1},{6,2},{7,3},{8,12},{9,13},{10,... | collective-permute-start | bytes 12296 | tf_op jit(solution)/shard_map/ppermute | solution.py:350
  36.4 1.6 %collective-permute-done.7 = f32[8,128]{1,0:T(8,128)S(1)} collective-permute-done((f32[8,128]{1,0:T(8,128)S(1)}, f32[8,128]{1,0:T(8,128)S(1)}, u32[]{:S(2)}, u32[]{:S(2)}) %collective-permute-start.7) | collective-permute-done | bytes 4128 | tf_op jit(solution)/shard_map/ppermute | solution.py:350
  38.0 3.0 %collective-permute-start.8 = (f32[8,128]{1,0:T(8,128)S(1)}, f32[8,128]{1,0:T(8,128)S(1)}, u32[]{:S(2)}, u32[]{:S(2)}) collective-permute-start(f32[8,128]{1,0:T(8,128)S(1)} %add.28.mine_ref), channel_id=1, source_target_pairs={{0,8},{1,9},{2,10},{3,11},{4,12},{5,13},{6,14},{7,15},{8,0},{9,1},... | collective-permute-start | bytes 12296 | tf_op jit(solution)/shard_map/ppermute | solution.py:350
  41.0 1.6 %collective-permute-done.8.other_ref = f32[8,128]{1,0:T(8,128)S(1)} collective-permute-done((f32[8,128]{1,0:T(8,128)S(1)}, f32[8,128]{1,0:T(8,128)S(1)}, u32[]{:S(2)}, u32[]{:S(2)}) %collective-permute-start.8) | collective-permute-done | bytes 4128 | tf_op jit(solution)/shard_map/ppermute | solution.py:350
  42.6 2.3 %final.1 = (f32[4,64,1024]{2,1,0:T(8,128)}, f32[4,64,1024]{2,1,0:T(8,128)}, f32[4,64,1024]{2,1,0:T(8,128)}, f32[4,64,1024]{2,1,0:T(8,128)}) custom-call(f32[1]{0:T(128)S(6)} %copy.11.damp_ref, f32[8,128]{1,0:T(8,128)S(1)} %add.28.mine_ref, f32[8,128]{1,0:T(8,128)S(1)} %collective-permute-done.8.other_ref, f32[4,64,1024]{2,1,0:T(8,128)S(1)} %copy-done.4, ...), custom_call_target="tpu_custom_call" | custom-call | flops 2000000000 | bytes 1048576 | tf_op jit(solution)/shard_map/final/pallas_call | solution.py:337
  (13 shorter events, 0.1 us)
Async XLA Ops:
  0.6 4.3 %copy-start.5 = (f32[4,4,31]{2,1,0:T(4,128)S(1)}, f32[4,4,31]{2,1,0:T(4,128)}, u32[]{:S(2)}) copy-start(f32[4,4,31]{2,1,0:T(4,128)} %param.11) | copy-start | bytes 5956
  0.6 4.3 %copy-start.6 = (f32[4,4,31]{2,1,0:T(4,128)S(1)}, f32[4,4,31]{2,1,0:T(4,128)}, u32[]{:S(2)}) copy-start(f32[4,4,31]{2,1,0:T(4,128)} %param.12) | copy-start | bytes 5956
  0.7 1.2 %copy-start = (f32[4,64,1024]{2,1,0:T(8,128)S(1)}, f32[4,64,1024]{2,1,0:T(8,128)}, u32[]{:S(2)}) copy-start(f32[4,64,1024]{2,1,0:T(8,128)} %p_ref.5) | copy-start | bytes 3145732
  1.9 3.1 %copy-start.1 = (f32[4,64,1024]{2,1,0:T(8,128)S(1)}, f32[4,64,1024]{2,1,0:T(8,128)}, u32[]{:S(2)}) copy-start(f32[4,64,1024]{2,1,0:T(8,128)} %p_ref.5) | copy-start | bytes 3145732
  2.0 4.8 %collective-permute-start = (f32[4,16,1024]{2,1,0:T(8,128)S(1)}, f32[4,16,1024]{2,1,0:T(8,128)S(1)}, u32[]{:S(2)}, u32[]{:S(2)}) collective-permute-start(f32[4,16,1024]{2,1,0:T(8,128)S(1)} %get-tuple-element.23), channel_id=1, source_target_pairs={{0,1},{1,0},{2,3},{3,2},{4,5},{5,4},{6,7},{7,6},{8,9},{9,8},{10,11... | collective-permute-start | bytes 786440 | tf_op jit(solution)/shard_map/ppermute | solution.py:350
  2.5 15.0 %collective-permute-start.3 = (f32[4,32,1024]{2,1,0:T(8,128)S(1)}, f32[4,32,1024]{2,1,0:T(8,128)S(1)}, u32[]{:S(2)}, u32[]{:S(2)}) collective-permute-start(f32[4,32,1024]{2,1,0:T(8,128)S(1)} %get-tuple-element.29), channel_id=1, source_target_pairs={{1,2},{2,1},{3,4},{4,3},{5,6},{6,5},{7,8},{8,7},{9,10},{10,9},{11,... | collective-permute-start | bytes 1572872 | tf_op jit(solution)/shard_map/ppermute | solution.py:366
  6.8 7.0 %collective-permute-start.1 = (f32[4,16,1024]{2,1,0:T(8,128)S(1)}, f32[4,16,1024]{2,1,0:T(8,128)S(1)}, u32[]{:S(2)}, u32[]{:S(2)}) collective-permute-start(f32[4,16,1024]{2,1,0:T(8,128)S(1)} %get-tuple-element.24), channel_id=1, source_target_pairs={{0,1},{1,0},{2,3},{3,2},{4,5},{5,4},{6,7},{7,6},{8,9},{9,8},{10,11... | collective-permute-start | bytes 786440 | tf_op jit(solution)/shard_map/ppermute | solution.py:350
  10.8 3.0 %copy-start.2 = (f32[4,64,1024]{2,1,0:T(8,128)S(1)}, f32[4,64,1024]{2,1,0:T(8,128)}, u32[]{:S(2)}) copy-start(f32[4,64,1024]{2,1,0:T(8,128)} %r_ref.1) | copy-start | bytes 3145732
  13.7 5.9 %collective-permute-start.4 = (f32[4,16,1024]{2,1,0:T(8,128)S(1)}, f32[4,16,1024]{2,1,0:T(8,128)S(1)}, u32[]{:S(2)}, u32[]{:S(2)}) collective-permute-start(f32[4,16,1024]{2,1,0:T(8,128)S(1)} %constant_dynamic-slice_fusion), channel_id=1, source_target_pairs={{0,1},{1,0},{2,3},{3,2},{4,5},{5,4},{6,7},{7,6},{8,9},{9,8},{10,11... | collective-permute-start | bytes 786440 | tf_op jit(solution)/shard_map/ppermute | solution.py:350
  13.8 3.7 %copy-start.3 = (f32[4,64,1024]{2,1,0:T(8,128)S(1)}, f32[4,64,1024]{2,1,0:T(8,128)}, u32[]{:S(2)}) copy-start(f32[4,64,1024]{2,1,0:T(8,128)} %grad_ref.1) | copy-start | bytes 3145732
  16.6 5.8 %collective-permute-start.2 = (f32[4,16,1024]{2,1,0:T(8,128)S(1)}, f32[4,16,1024]{2,1,0:T(8,128)S(1)}, u32[]{:S(2)}, u32[]{:S(2)}) collective-permute-start(f32[4,16,1024]{2,1,0:T(8,128)S(1)} %get-tuple-element.27), channel_id=1, source_target_pairs={{1,2},{2,1},{3,4},{4,3},{5,6},{6,5},{7,8},{8,7},{9,10},{10,9},{11,... | collective-permute-start | bytes 786440 | tf_op jit(solution)/shard_map/ppermute | solution.py:366
  19.6 2.8 %copy-start.4 = (f32[4,64,1024]{2,1,0:T(8,128)S(1)}, f32[4,64,1024]{2,1,0:T(8,128)}, u32[]{:S(2)}) copy-start(f32[4,64,1024]{2,1,0:T(8,128)} %x_ref.3) | copy-start | bytes 3145732
  25.2 4.7 %collective-permute-start.5 = (f32[8,128]{1,0:T(8,128)S(1)}, f32[8,128]{1,0:T(8,128)S(1)}, u32[]{:S(2)}, u32[]{:S(2)}) collective-permute-start(f32[8,128]{1,0:T(8,128)S(1)} %get-tuple-element.39), channel_id=1, source_target_pairs={{0,1},{1,0},{2,3},{3,2},{4,5},{5,4},{6,7},{7,6},{8,9},{9,8},{10,11... | collective-permute-start | bytes 12296 | tf_op jit(solution)/shard_map/ppermute | solution.py:350
  29.9 4.3 %collective-permute-start.6 = (f32[8,128]{1,0:T(8,128)S(1)}, f32[8,128]{1,0:T(8,128)S(1)}, u32[]{:S(2)}, u32[]{:S(2)}) collective-permute-start(f32[8,128]{1,0:T(8,128)S(1)} %add.26), channel_id=1, source_target_pairs={{0,2},{1,3},{2,0},{3,1},{4,6},{5,7},{6,4},{7,5},{8,10},{9,11},{10,... | collective-permute-start | bytes 12296 | tf_op jit(solution)/shard_map/ppermute | solution.py:350
  34.2 3.8 %collective-permute-start.7 = (f32[8,128]{1,0:T(8,128)S(1)}, f32[8,128]{1,0:T(8,128)S(1)}, u32[]{:S(2)}, u32[]{:S(2)}) collective-permute-start(f32[8,128]{1,0:T(8,128)S(1)} %add.27), channel_id=1, source_target_pairs={{0,4},{1,5},{2,6},{3,7},{4,0},{5,1},{6,2},{7,3},{8,12},{9,13},{10,... | collective-permute-start | bytes 12296 | tf_op jit(solution)/shard_map/ppermute | solution.py:350
  38.0 4.6 %collective-permute-start.8 = (f32[8,128]{1,0:T(8,128)S(1)}, f32[8,128]{1,0:T(8,128)S(1)}, u32[]{:S(2)}, u32[]{:S(2)}) collective-permute-start(f32[8,128]{1,0:T(8,128)S(1)} %add.28.mine_ref), channel_id=1, source_target_pairs={{0,8},{1,9},{2,10},{3,11},{4,12},{5,13},{6,14},{7,15},{8,0},{9,1},... | collective-permute-start | bytes 12296 | tf_op jit(solution)/shard_map/ppermute | solution.py:350

commit v4 on v3

--- a/solution.py
+++ b/solution.py
@@ -88,6 +88,8 @@
     col_hi, col_lo = split(col_ref[...])
     window = LANE + 2 * EDGE
     lane = lax.broadcasted_iota(jnp.int32, (window, WIDE), 1)
+    back = lax.broadcasted_iota(jnp.int32, (window, WIDE), 0) - jnp.where(lane < LANE, lane, lane - LANE)
+    inside = (back >= 0) & (back <= last)
     for adjoint in (False, True):
         r_early, r_late, c_out = outs[3:] if adjoint else outs[:3]
         tall = EDGE if adjoint else 2 * EDGE
@@ -98,8 +100,7 @@
                 (row_hi, one_hot(count, lambda a: turn(a) + gap)),
                 (row_lo, one_hot(count, lambda a: turn(a) + 2 * gap)),
             ))
-        bases[2][...] = pick(((col_hi, one_hot(count, lambda a: -turn(a))),))
-        bases[3][...] = pick(((col_lo, one_hot(count, lambda a: LANE - turn(a))),))
+        bases[2][...] = pick(((col_hi, one_hot(count, lambda a: -turn(a))), (col_lo, one_hot(count, lambda a: LANE - turn(a)))))
 
         def banded(base, pair, rows, shift):
             wide = jnp.broadcast_to(base[pl.ds(pair, 1), :], (rows, WIDE))
@@ -110,7 +111,7 @@
                 pair = s * depth + o if adjoint else o * depth + s
                 r_early[s, o * inner:(o + 1) * inner, :] = banded(bases[0], pair, inner, 1).astype(BF16)
                 r_late[s, o * tall:(o + 1) * tall, :] = banded(bases[1], pair, tall, 1).astype(BF16)
-                band = jnp.where(lane < LANE, banded(bases[2], pair, window, 0), banded(bases[3], pair, window, 0))
+                band = jnp.where(inside, banded(bases[2], pair, window, 0), 0.0)
                 c_out[o, s * WIDE:s * WIDE + window, :] = band.astype(BF16)
                 c_out[o, s * WIDE + window:(s + 1) * WIDE, :] = jnp.zeros((WIDE - window, WIDE), BF16)
 
@@ -131,7 +132,7 @@
         out_shape=bands(2 * EDGE) + bands(EDGE) + (f32(8, LANE),),
         in_specs=[VM] * 3,
         out_specs=[VM] * 7,
-        scratch_shapes=[pltpu.VMEM((pairs, WIDE), F32)] * 4,
+        scratch_shapes=[pltpu.VMEM((pairs, WIDE), F32)] * 3,
         compiler_params=params(),
         cost_estimate=cost(1.5),
         name="prep",

time: 45.3 us -> 44.8 us (0.989)
  no operation moved by 1% of the time
where the time goes in v4:
time: 44.8 us; the launch traced here: 44.6 us
  starting transfers between devices  18 us (40%)
  Pallas kernels  17 us (38%)
  waiting for transfers between devices  5.59 us (12%)
  local copies, waits for them, and re-layouts  2.35 us (5%)
  between operations  1.68 us (4%)
    ppermute x7, starting transfers between devices, swap(): lax.ppermute(values, axis, [(i, i ^ step) for i in range(lax.axis_size(ax...  16.5 us
    pallas_call x3, Pallas kernels, early(): pl.pallas_call(functools.partial(early_kernel, border), out_shape=f32(dep...  8.41 us
    ppermute x7, waiting for transfers between devices, swap(): lax.ppermute(values, axis, [(i, i ^ step) for i in range(lax.axis_size(ax...  5.58 us
    pallas_call x1, Pallas kernels, last_late(): pl.pallas_call(functools.partial(last_kernel, border), out_shape=(f32(dep...  2.75 us
    pallas_call x1, Pallas kernels, final(): pl.pallas_call(final_kernel, out_shape=(f32(*shape),) * 4, in_specs=[SM]...  2.29 us
    pallas_call x1, Pallas kernels, image_late(): pl.pallas_call(functools.partial(image_kernel, border), out_shape=(f32(de...  2.1 us
    ppermute x2, starting transfers between devices, far_swap(): return lax.ppermute(v, 'lat', far_pairs)  1.54 us
    pallas_call x1, Pallas kernels, prep(): pl.pallas_call(functools.partial(prep_kernel, depth, inner), out_shape=ba...  1.36 us
  transfers between devices with their start and end apart: 9, of which 4 were waited for; matrix products, arithmetic and copies ran while one was open for 2% of the time, Pallas kernels for 27%

profile of v4, /device:TPU:0, one launch (start us, length us, event | category | flops | bytes accessed | tf_op | source)
XLA Modules:
  0.0 44.6 jit_solution(8669589874049835261)
XLA Ops:
  0.6 0.0 copy-start.5
  0.6 0.0 copy-start.6
  0.7 0.0 copy-start
  0.7 1.2 %copy-done = f32[4,64,1024]{2,1,0:T(8,128)S(1)} copy-done((f32[4,64,1024]{2,1,0:T(8,128)S(1)}, f32[4,64,1024]{2,1,0:T(8,128)}, u32[]{:S(2)}) %copy-start) | copy-done | bytes 1048600
  1.9 0.1 edges.1
  2.0 0.5 %collective-permute-start = (f32[4,16,1024]{2,1,0:T(8,128)S(1)}, f32[4,16,1024]{2,1,0:T(8,128)S(1)}, u32[]{:S(2)}, u32[]{:S(2)}) collective-permute-start(f32[4,16,1024]{2,1,0:T(8,128)S(1)} %get-tuple-element.23), channel_id=1, source_target_pairs={{0,1},{1,0},{2,3},{3,2},{4,5},{5,4},{6,7},{7,6},{8,9},{9,8},{10,11... | collective-permute-start | bytes 786440 | tf_op jit(solution)/shard_map/ppermute | solution.py:351
  2.5 0.7 %collective-permute-start.3 = (f32[4,32,1024]{2,1,0:T(8,128)S(1)}, f32[4,32,1024]{2,1,0:T(8,128)S(1)}, u32[]{:S(2)}, u32[]{:S(2)}) collective-permute-start(f32[4,32,1024]{2,1,0:T(8,128)S(1)} %get-tuple-element.29), channel_id=1, source_target_pairs={{1,2},{2,1},{3,4},{4,3},{5,6},{6,5},{7,8},{8,7},{9,10},{10,9},{11,... | collective-permute-start | bytes 1572872 | tf_op jit(solution)/shard_map/ppermute | solution.py:367
  3.9 1.1 %constant_dynamic-slice_fusion.1 = (f32[4,16,1024]{2,1,0:T(8,128)S(1)}, f32[4,16,1024]{2,1,0:T(8,128)S(1)}) fusion(f32[4,64,1024]{2,1,0:T(8,128)} %r_ref.1, s32[]{:T(128)S(6)} %select_n.22, s32[]{:T(128)S(6)} %select_n.21), kind=kLoop, calls=%fused_computation.1 | loop fusion | bytes 1048584 | tf_op jit(solution)/shard_map/dynamic_slice | solution.py:376
  5.0 1.4 %prep.1 = (bf16[4,192,256]{2,1,0:T(8,128)(2,1)S(1)}, bf16[4,128,256]{2,1,0:T(8,128)(2,1)S(1)}, bf16[4,1024,256]{2,1,0:T(8,128)(2,1)S(1)}, bf16[4,192,256]{2,1,0:...) custom-call(f32[16,31]{1,0:T(8,128)S(1)} %bitcast.4, ...), custom_call_target="tpu_custom_call" | custom-call | flops 1500000000 | bytes 1048576 | tf_op jit(solution)/shard_map/prep/pallas_call | solution.py:130
  6.3 0.0 collective-permute-done.near_ref
  6.3 4.1 %collective-permute-start.1 = (f32[4,16,1024]{2,1,0:T(8,128)S(1)}, f32[4,16,1024]{2,1,0:T(8,128)S(1)}, u32[]{:S(2)}, u32[]{:S(2)}) collective-permute-start(f32[4,16,1024]{2,1,0:T(8,128)S(1)} %get-tuple-element.24), channel_id=1, source_target_pairs={{0,1},{1,0},{2,3},{3,2},{4,5},{5,4},{6,7},{7,6},{8,9},{9,8},{10,11... | collective-permute-start | bytes 786440 | tf_op jit(solution)/shard_map/ppermute | solution.py:351
  10.4 2.8 %early.4.in_ref = f32[4,48,1024]{2,1,0:T(8,128)S(1)} custom-call(s32[1]{0:T(128)} %bitcast.odd_ref.after_ref, f32[4,64,1024]{2,1,0:T(8,128)S(1)} %copy-done.1, f32[4,16,1024]{2,1,0:T(8,128)S(1)} %collective-permute-done.near_ref, bf16[4,192,256]{2,1,0:T(8,128)(2,1)S(1)} %get-tuple-element.33.r_ref, bf16[4,1024,256]{2,1,0:T(8,128)(2,1)S(1)} %get-tuple-element.31.c_ref), custom_call_target="tpu_custom_call" | custom-call | flops 2800000000 | bytes 1048576 | tf_op jit(solution)/shard_map/early/pallas_call | solution.py:203
  13.3 0.1 collective-permute-start.4
  13.4 0.0 collective-permute-done.1.near_ref
  13.4 2.8 %early.3.after_ref.g_in_ref = f32[4,48,1024]{2,1,0:T(8,128)S(1)} custom-call(s32[1]{0:T(128)} %bitcast.odd_ref.after_ref, f32[4,64,1024]{2,1,0:T(8,128)S(1)} %copy-done.2, f32[4,16,1024]{2,1,0:T(8,128)S(1)} %collective-permute-done.1.near_ref, bf16[4,192,256]{2,1,0:T(8,128)(2,1)S(1)} %get-tuple-element.25.r_ref, ...), custom_call_target="tpu_custom_call" | custom-call | flops 2800000000 | bytes 1048576 | tf_op jit(solution)/shard_map/early/pallas_call | solution.py:203
  16.2 0.9 %collective-permute-start.2 = (f32[4,16,1024]{2,1,0:T(8,128)S(1)}, f32[4,16,1024]{2,1,0:T(8,128)S(1)}, u32[]{:S(2)}, u32[]{:S(2)}) collective-permute-start(f32[4,16,1024]{2,1,0:T(8,128)S(1)} %get-tuple-element.27), channel_id=1, source_target_pairs={{1,2},{2,1},{3,4},{4,3},{5,6},{6,5},{7,8},{8,7},{9,10},{10,9},{11,... | collective-permute-start | bytes 786440 | tf_op jit(solution)/shard_map/ppermute | solution.py:367
  17.1 0.0 collective-permute-done.3.far_ref
  17.1 2.1 %image_late.1 = (f32[4,64,1024]{2,1,0:T(8,128)S(1)}, f32[4,16,1024]{2,1,0:T(8,128)S(1)}, f32[8,128]{1,0:T(8,128)S(1)}) custom-call(s32[1]{0:T(128)} %bitcast.odd_ref.after_ref, s32[1]{0:T(128)} %bitcast.3.more_ref, f32[4,64,1024]{2,1,0:T(8,128)S(1)} %copy-done.1, f32[4,32,1024]{2,1,0:T(8,128)S(1)} %collective-permute-done.3.far_ref, ...), custom_call_target="tpu_custom_call" | custom-call | flops 2000000000 | bytes 1048576 | tf_op jit(solution)/shard_map/image_late/pallas_call | solution.py:259
  19.2 0.0 collective-permute-done.4.near_ref
  19.2 0.0 copy-start.4
  19.2 2.8 %early.5.h_in_ref = f32[4,48,1024]{2,1,0:T(8,128)S(1)} custom-call(s32[1]{0:T(128)} %bitcast.odd_ref.after_ref, f32[4,64,1024]{2,1,0:T(8,128)S(1)} %get-tuple-element.35.v_ref.f_ref, f32[4,16,1024]{2,1,0:T(8,128)S(1)} %collective-permute-done.4.near_ref, bf16[4,192,256]{2,1,0:T(8,128)(2,1)S(1)} %get-tuple-element.25.r_ref, ...), custom_call_target="tpu_custom_call" | custom-call | flops 2800000000 | bytes 1048576 | tf_op jit(solution)/shard_map/early/pallas_call | solution.py:203
  22.0 0.0 collective-permute-done.2.res_far_ref
  22.0 2.7 %last_late.1 = (f32[4,64,1024]{2,1,0:T(8,128)S(1)}, f32[4,64,1024]{2,1,0:T(8,128)S(1)}, f32[8,128]{1,0:T(8,128)S(1)}) custom-call(s32[1]{0:T(128)} %bitcast.odd_ref.after_ref, f32[1]{0:T(128)S(6)} %copy.11.damp_ref, f32[4,64,1024]{2,1,0:T(8,128)S(1)} %copy-done.2, f32[4,16,1024]{2,1,0:T(8,128)S(1)} %collective-permute-done.2.res_far_ref, ...), custom_call_target="tpu_custom_call" | custom-call | flops 2600000000 | bytes 1048576 | tf_op jit(solution)/shard_map/last_late/pallas_call | solution.py:298
  24.8 3.9 %collective-permute-start.5 = (f32[8,128]{1,0:T(8,128)S(1)}, f32[8,128]{1,0:T(8,128)S(1)}, u32[]{:S(2)}, u32[]{:S(2)}) collective-permute-start(f32[8,128]{1,0:T(8,128)S(1)} %get-tuple-element.39), channel_id=1, source_target_pairs={{0,1},{1,0},{2,3},{3,2},{4,5},{5,4},{6,7},{7,6},{8,9},{9,8},{10,11... | collective-permute-start | bytes 12296 | tf_op jit(solution)/shard_map/ppermute | solution.py:351
  28.7 0.8 %collective-permute-done.5 = f32[8,128]{1,0:T(8,128)S(1)} collective-permute-done((f32[8,128]{1,0:T(8,128)S(1)}, f32[8,128]{1,0:T(8,128)S(1)}, u32[]{:S(2)}, u32[]{:S(2)}) %collective-permute-start.5) | collective-permute-done | bytes 4128 | tf_op jit(solution)/shard_map/ppermute | solution.py:351
  29.5 2.7 %collective-permute-start.6 = (f32[8,128]{1,0:T(8,128)S(1)}, f32[8,128]{1,0:T(8,128)S(1)}, u32[]{:S(2)}, u32[]{:S(2)}) collective-permute-start(f32[8,128]{1,0:T(8,128)S(1)} %add.26), channel_id=1, source_target_pairs={{0,2},{1,3},{2,0},{3,1},{4,6},{5,7},{6,4},{7,5},{8,10},{9,11},{10,... | collective-permute-start | bytes 12296 | tf_op jit(solution)/shard_map/ppermute | solution.py:351
  32.2 1.6 %collective-permute-done.6 = f32[8,128]{1,0:T(8,128)S(1)} collective-permute-done((f32[8,128]{1,0:T(8,128)S(1)}, f32[8,128]{1,0:T(8,128)S(1)}, u32[]{:S(2)}, u32[]{:S(2)}) %collective-permute-start.6) | collective-permute-done | bytes 4128 | tf_op jit(solution)/shard_map/ppermute | solution.py:351
  33.8 2.2 %collective-permute-start.7 = (f32[8,128]{1,0:T(8,128)S(1)}, f32[8,128]{1,0:T(8,128)S(1)}, u32[]{:S(2)}, u32[]{:S(2)}) collective-permute-start(f32[8,128]{1,0:T(8,128)S(1)} %add.27), channel_id=1, source_target_pairs={{0,4},{1,5},{2,6},{3,7},{4,0},{5,1},{6,2},{7,3},{8,12},{9,13},{10,... | collective-permute-start | bytes 12296 | tf_op jit(solution)/shard_map/ppermute | solution.py:351
  36.0 1.6 %collective-permute-done.7 = f32[8,128]{1,0:T(8,128)S(1)} collective-permute-done((f32[8,128]{1,0:T(8,128)S(1)}, f32[8,128]{1,0:T(8,128)S(1)}, u32[]{:S(2)}, u32[]{:S(2)}) %collective-permute-start.7) | collective-permute-done | bytes 4128 | tf_op jit(solution)/shard_map/ppermute | solution.py:351
  37.6 3.0 %collective-permute-start.8 = (f32[8,128]{1,0:T(8,128)S(1)}, f32[8,128]{1,0:T(8,128)S(1)}, u32[]{:S(2)}, u32[]{:S(2)}) collective-permute-start(f32[8,128]{1,0:T(8,128)S(1)} %add.28.mine_ref), channel_id=1, source_target_pairs={{0,8},{1,9},{2,10},{3,11},{4,12},{5,13},{6,14},{7,15},{8,0},{9,1},... | collective-permute-start | bytes 12296 | tf_op jit(solution)/shard_map/ppermute | solution.py:351
  40.6 1.6 %collective-permute-done.8.other_ref = f32[8,128]{1,0:T(8,128)S(1)} collective-permute-done((f32[8,128]{1,0:T(8,128)S(1)}, f32[8,128]{1,0:T(8,128)S(1)}, u32[]{:S(2)}, u32[]{:S(2)}) %collective-permute-start.8) | collective-permute-done | bytes 4128 | tf_op jit(solution)/shard_map/ppermute | solution.py:351
  42.2 2.3 %final.1 = (f32[4,64,1024]{2,1,0:T(8,128)}, f32[4,64,1024]{2,1,0:T(8,128)}, f32[4,64,1024]{2,1,0:T(8,128)}, f32[4,64,1024]{2,1,0:T(8,128)}) custom-call(f32[1]{0:T(128)S(6)} %copy.11.damp_ref, f32[8,128]{1,0:T(8,128)S(1)} %add.28.mine_ref, f32[8,128]{1,0:T(8,128)S(1)} %collective-permute-done.8.other_ref, f32[4,64,1024]{2,1,0:T(8,128)S(1)} %copy-done.4, ...), custom_call_target="tpu_custom_call" | custom-call | flops 2000000000 | bytes 1048576 | tf_op jit(solution)/shard_map/final/pallas_call | solution.py:338
  (13 shorter events, 0.1 us)
Async XLA Ops:
  0.6 4.3 %copy-start.5 = (f32[4,4,31]{2,1,0:T(4,128)S(1)}, f32[4,4,31]{2,1,0:T(4,128)}, u32[]{:S(2)}) copy-start(f32[4,4,31]{2,1,0:T(4,128)} %param.11) | copy-start | bytes 5956
  0.6 4.3 %copy-start.6 = (f32[4,4,31]{2,1,0:T(4,128)S(1)}, f32[4,4,31]{2,1,0:T(4,128)}, u32[]{:S(2)}) copy-start(f32[4,4,31]{2,1,0:T(4,128)} %param.12) | copy-start | bytes 5956
  0.7 1.2 %copy-start = (f32[4,64,1024]{2,1,0:T(8,128)S(1)}, f32[4,64,1024]{2,1,0:T(8,128)}, u32[]{:S(2)}) copy-start(f32[4,64,1024]{2,1,0:T(8,128)} %p_ref.5) | copy-start | bytes 3145732
  1.9 3.1 %copy-start.1 = (f32[4,64,1024]{2,1,0:T(8,128)S(1)}, f32[4,64,1024]{2,1,0:T(8,128)}, u32[]{:S(2)}) copy-start(f32[4,64,1024]{2,1,0:T(8,128)} %p_ref.5) | copy-start | bytes 3145732
  2.0 4.4 %collective-permute-start = (f32[4,16,1024]{2,1,0:T(8,128)S(1)}, f32[4,16,1024]{2,1,0:T(8,128)S(1)}, u32[]{:S(2)}, u32[]{:S(2)}) collective-permute-start(f32[4,16,1024]{2,1,0:T(8,128)S(1)} %get-tuple-element.23), channel_id=1, source_target_pairs={{0,1},{1,0},{2,3},{3,2},{4,5},{5,4},{6,7},{7,6},{8,9},{9,8},{10,11... | collective-permute-start | bytes 786440 | tf_op jit(solution)/shard_map/ppermute | solution.py:351
  2.5 14.6 %collective-permute-start.3 = (f32[4,32,1024]{2,1,0:T(8,128)S(1)}, f32[4,32,1024]{2,1,0:T(8,128)S(1)}, u32[]{:S(2)}, u32[]{:S(2)}) collective-permute-start(f32[4,32,1024]{2,1,0:T(8,128)S(1)} %get-tuple-element.29), channel_id=1, source_target_pairs={{1,2},{2,1},{3,4},{4,3},{5,6},{6,5},{7,8},{8,7},{9,10},{10,9},{11,... | collective-permute-start | bytes 1572872 | tf_op jit(solution)/shard_map/ppermute | solution.py:367
  6.3 7.0 %collective-permute-start.1 = (f32[4,16,1024]{2,1,0:T(8,128)S(1)}, f32[4,16,1024]{2,1,0:T(8,128)S(1)}, u32[]{:S(2)}, u32[]{:S(2)}) collective-permute-start(f32[4,16,1024]{2,1,0:T(8,128)S(1)} %get-tuple-element.24), channel_id=1, source_target_pairs={{0,1},{1,0},{2,3},{3,2},{4,5},{5,4},{6,7},{7,6},{8,9},{9,8},{10,11... | collective-permute-start | bytes 786440 | tf_op jit(solution)/shard_map/ppermute | solution.py:351
  10.4 2.9 %copy-start.2 = (f32[4,64,1024]{2,1,0:T(8,128)S(1)}, f32[4,64,1024]{2,1,0:T(8,128)}, u32[]{:S(2)}) copy-start(f32[4,64,1024]{2,1,0:T(8,128)} %r_ref.1) | copy-start | bytes 3145732
  13.3 5.9 %collective-permute-start.4 = (f32[4,16,1024]{2,1,0:T(8,128)S(1)}, f32[4,16,1024]{2,1,0:T(8,128)S(1)}, u32[]{:S(2)}, u32[]{:S(2)}) collective-permute-start(f32[4,16,1024]{2,1,0:T(8,128)S(1)} %constant_dynamic-slice_fusion), channel_id=1, source_target_pairs={{0,1},{1,0},{2,3},{3,2},{4,5},{5,4},{6,7},{7,6},{8,9},{9,8},{10,11... | collective-permute-start | bytes 786440 | tf_op jit(solution)/shard_map/ppermute | solution.py:351
  13.4 3.7 %copy-start.3 = (f32[4,64,1024]{2,1,0:T(8,128)S(1)}, f32[4,64,1024]{2,1,0:T(8,128)}, u32[]{:S(2)}) copy-start(f32[4,64,1024]{2,1,0:T(8,128)} %grad_ref.1) | copy-start | bytes 3145732
  16.2 5.8 %collective-permute-start.2 = (f32[4,16,1024]{2,1,0:T(8,128)S(1)}, f32[4,16,1024]{2,1,0:T(8,128)S(1)}, u32[]{:S(2)}, u32[]{:S(2)}) collective-permute-start(f32[4,16,1024]{2,1,0:T(8,128)S(1)} %get-tuple-element.27), channel_id=1, source_target_pairs={{1,2},{2,1},{3,4},{4,3},{5,6},{6,5},{7,8},{8,7},{9,10},{10,9},{11,... | collective-permute-start | bytes 786440 | tf_op jit(solution)/shard_map/ppermute | solution.py:367
  19.2 2.8 %copy-start.4 = (f32[4,64,1024]{2,1,0:T(8,128)S(1)}, f32[4,64,1024]{2,1,0:T(8,128)}, u32[]{:S(2)}) copy-start(f32[4,64,1024]{2,1,0:T(8,128)} %x_ref.3) | copy-start | bytes 3145732
  24.8 4.7 %collective-permute-start.5 = (f32[8,128]{1,0:T(8,128)S(1)}, f32[8,128]{1,0:T(8,128)S(1)}, u32[]{:S(2)}, u32[]{:S(2)}) collective-permute-start(f32[8,128]{1,0:T(8,128)S(1)} %get-tuple-element.39), channel_id=1, source_target_pairs={{0,1},{1,0},{2,3},{3,2},{4,5},{5,4},{6,7},{7,6},{8,9},{9,8},{10,11... | collective-permute-start | bytes 12296 | tf_op jit(solution)/shard_map/ppermute | solution.py:351
  29.5 4.3 %collective-permute-start.6 = (f32[8,128]{1,0:T(8,128)S(1)}, f32[8,128]{1,0:T(8,128)S(1)}, u32[]{:S(2)}, u32[]{:S(2)}) collective-permute-start(f32[8,128]{1,0:T(8,128)S(1)} %add.26), channel_id=1, source_target_pairs={{0,2},{1,3},{2,0},{3,1},{4,6},{5,7},{6,4},{7,5},{8,10},{9,11},{10,... | collective-permute-start | bytes 12296 | tf_op jit(solution)/shard_map/ppermute | solution.py:351
  33.8 3.8 %collective-permute-start.7 = (f32[8,128]{1,0:T(8,128)S(1)}, f32[8,128]{1,0:T(8,128)S(1)}, u32[]{:S(2)}, u32[]{:S(2)}) collective-permute-start(f32[8,128]{1,0:T(8,128)S(1)} %add.27), channel_id=1, source_target_pairs={{0,4},{1,5},{2,6},{3,7},{4,0},{5,1},{6,2},{7,3},{8,12},{9,13},{10,... | collective-permute-start | bytes 12296 | tf_op jit(solution)/shard_map/ppermute | solution.py:351
  37.6 4.6 %collective-permute-start.8 = (f32[8,128]{1,0:T(8,128)S(1)}, f32[8,128]{1,0:T(8,128)S(1)}, u32[]{:S(2)}, u32[]{:S(2)}) collective-permute-start(f32[8,128]{1,0:T(8,128)S(1)} %add.28.mine_ref), channel_id=1, source_target_pairs={{0,8},{1,9},{2,10},{3,11},{4,12},{5,13},{6,14},{7,15},{8,0},{9,1},... | collective-permute-start | bytes 12296 | tf_op jit(solution)/shard_map/ppermute | solution.py:351

commit v5 on v4

--- a/solution.py
+++ b/solution.py
@@ -388,8 +388,10 @@
 
     step = 1
     while 2 * step < peers:
+        step *= 2
+    while step > 1:
         sums = sums + swap(sums, "lat", step)
-        step *= 2
+        step //= 2
     other = swap(sums, "lat", step)
     return final(damping, sums, other, solution, residual, direction, image, g, h)
 

time: 44.8 us -> 44.5 us (level)
  starting transfers between devices: 18 us -> 17.3 us
  waiting for transfers between devices: 5.59 us -> 6.05 us
    ppermute x7, starting transfers between devices: 16.5 us -> 15.7 us  [swap(): lax.ppermute(values, axis, [(i, i ^ step) for i in range(lax.axis_size(ax...]
    ppermute x7, waiting for transfers between devices: 5.58 us -> 6.05 us  [swap(): lax.ppermute(values, axis, [(i, i ^ step) for i in range(lax.axis_size(ax...]
where the time goes in v5:
time: 44.5 us; the launch traced here: 44.4 us
  starting transfers between devices  17.3 us (39%)
  Pallas kernels  17 us (38%)
  waiting for transfers between devices  6.05 us (14%)
  local copies, waits for them, and re-layouts  2.35 us (5%)
  between operations  1.68 us (4%)
    ppermute x7, starting transfers between devices, swap(): lax.ppermute(values, axis, [(i, i ^ step) for i in range(lax.axis_size(ax...  15.7 us
    pallas_call x3, Pallas kernels, early(): pl.pallas_call(functools.partial(early_kernel, border), out_shape=f32(dep...  8.41 us
    ppermute x7, waiting for transfers between devices, swap(): lax.ppermute(values, axis, [(i, i ^ step) for i in range(lax.axis_size(ax...  6.05 us
    pallas_call x1, Pallas kernels, last_late(): pl.pallas_call(functools.partial(last_kernel, border), out_shape=(f32(dep...  2.75 us
    pallas_call x1, Pallas kernels, final(): pl.pallas_call(final_kernel, out_shape=(f32(*shape),) * 4, in_specs=[SM]...  2.29 us
    pallas_call x1, Pallas kernels, image_late(): pl.pallas_call(functools.partial(image_kernel, border), out_shape=(f32(de...  2.1 us
    ppermute x2, starting transfers between devices, far_swap(): return lax.ppermute(v, 'lat', far_pairs)  1.54 us
    pallas_call x1, Pallas kernels, prep(): pl.pallas_call(functools.partial(prep_kernel, depth, inner), out_shape=ba...  1.36 us
  transfers between devices with their start and end apart: 9, of which 4 were waited for; matrix products, arithmetic and copies ran while one was open for 2% of the time, Pallas kernels for 27%

profile of v5, /device:TPU:0, one launch (start us, length us, event | category | flops | bytes accessed | tf_op | source)
XLA Modules:
  0.0 44.4 jit_solution(12252128384821805422)
XLA Ops:
  0.6 0.0 copy-start.5
  0.6 0.0 copy-start.6
  0.7 0.0 copy-start
  0.7 1.2 %copy-done = f32[4,64,1024]{2,1,0:T(8,128)S(1)} copy-done((f32[4,64,1024]{2,1,0:T(8,128)S(1)}, f32[4,64,1024]{2,1,0:T(8,128)}, u32[]{:S(2)}) %copy-start) | copy-done | bytes 1048600
  1.9 0.1 edges.1
  2.0 0.5 %collective-permute-start = (f32[4,16,1024]{2,1,0:T(8,128)S(1)}, f32[4,16,1024]{2,1,0:T(8,128)S(1)}, u32[]{:S(2)}, u32[]{:S(2)}) collective-permute-start(f32[4,16,1024]{2,1,0:T(8,128)S(1)} %get-tuple-element.23), channel_id=1, source_target_pairs={{0,1},{1,0},{2,3},{3,2},{4,5},{5,4},{6,7},{7,6},{8,9},{9,8},{10,11... | collective-permute-start | bytes 786440 | tf_op jit(solution)/shard_map/ppermute | solution.py:351
  2.5 0.7 %collective-permute-start.3 = (f32[4,32,1024]{2,1,0:T(8,128)S(1)}, f32[4,32,1024]{2,1,0:T(8,128)S(1)}, u32[]{:S(2)}, u32[]{:S(2)}) collective-permute-start(f32[4,32,1024]{2,1,0:T(8,128)S(1)} %get-tuple-element.29), channel_id=1, source_target_pairs={{1,2},{2,1},{3,4},{4,3},{5,6},{6,5},{7,8},{8,7},{9,10},{10,9},{11,... | collective-permute-start | bytes 1572872 | tf_op jit(solution)/shard_map/ppermute | solution.py:367
  3.9 1.1 %constant_dynamic-slice_fusion.1 = (f32[4,16,1024]{2,1,0:T(8,128)S(1)}, f32[4,16,1024]{2,1,0:T(8,128)S(1)}) fusion(f32[4,64,1024]{2,1,0:T(8,128)} %r_ref.1, s32[]{:T(128)S(6)} %select_n.22, s32[]{:T(128)S(6)} %select_n.21), kind=kLoop, calls=%fused_computation.1 | loop fusion | bytes 1048584 | tf_op jit(solution)/shard_map/dynamic_slice | solution.py:376
  5.0 1.4 %prep.1 = (bf16[4,192,256]{2,1,0:T(8,128)(2,1)S(1)}, bf16[4,128,256]{2,1,0:T(8,128)(2,1)S(1)}, bf16[4,1024,256]{2,1,0:T(8,128)(2,1)S(1)}, bf16[4,192,256]{2,1,0:...) custom-call(f32[16,31]{1,0:T(8,128)S(1)} %bitcast.4, ...), custom_call_target="tpu_custom_call" | custom-call | flops 1500000000 | bytes 1048576 | tf_op jit(solution)/shard_map/prep/pallas_call | solution.py:130
  6.3 0.0 collective-permute-done.near_ref
  6.3 4.1 %collective-permute-start.1 = (f32[4,16,1024]{2,1,0:T(8,128)S(1)}, f32[4,16,1024]{2,1,0:T(8,128)S(1)}, u32[]{:S(2)}, u32[]{:S(2)}) collective-permute-start(f32[4,16,1024]{2,1,0:T(8,128)S(1)} %get-tuple-element.24), channel_id=1, source_target_pairs={{0,1},{1,0},{2,3},{3,2},{4,5},{5,4},{6,7},{7,6},{8,9},{9,8},{10,11... | collective-permute-start | bytes 786440 | tf_op jit(solution)/shard_map/ppermute | solution.py:351
  10.4 2.8 %early.4.in_ref = f32[4,48,1024]{2,1,0:T(8,128)S(1)} custom-call(s32[1]{0:T(128)} %bitcast.odd_ref.after_ref, f32[4,64,1024]{2,1,0:T(8,128)S(1)} %copy-done.1, f32[4,16,1024]{2,1,0:T(8,128)S(1)} %collective-permute-done.near_ref, bf16[4,192,256]{2,1,0:T(8,128)(2,1)S(1)} %get-tuple-element.33.r_ref, bf16[4,1024,256]{2,1,0:T(8,128)(2,1)S(1)} %get-tuple-element.31.c_ref), custom_call_target="tpu_custom_call" | custom-call | flops 2800000000 | bytes 1048576 | tf_op jit(solution)/shard_map/early/pallas_call | solution.py:203
  13.3 0.1 collective-permute-start.4
  13.4 0.0 collective-permute-done.1.near_ref
  13.4 2.8 %early.3.after_ref.g_in_ref = f32[4,48,1024]{2,1,0:T(8,128)S(1)} custom-call(s32[1]{0:T(128)} %bitcast.odd_ref.after_ref, f32[4,64,1024]{2,1,0:T(8,128)S(1)} %copy-done.2, f32[4,16,1024]{2,1,0:T(8,128)S(1)} %collective-permute-done.1.near_ref, bf16[4,192,256]{2,1,0:T(8,128)(2,1)S(1)} %get-tuple-element.25.r_ref, ...), custom_call_target="tpu_custom_call" | custom-call | flops 2800000000 | bytes 1048576 | tf_op jit(solution)/shard_map/early/pallas_call | solution.py:203
  16.2 0.9 %collective-permute-start.2 = (f32[4,16,1024]{2,1,0:T(8,128)S(1)}, f32[4,16,1024]{2,1,0:T(8,128)S(1)}, u32[]{:S(2)}, u32[]{:S(2)}) collective-permute-start(f32[4,16,1024]{2,1,0:T(8,128)S(1)} %get-tuple-element.27), channel_id=1, source_target_pairs={{1,2},{2,1},{3,4},{4,3},{5,6},{6,5},{7,8},{8,7},{9,10},{10,9},{11,... | collective-permute-start | bytes 786440 | tf_op jit(solution)/shard_map/ppermute | solution.py:367
  17.1 0.0 collective-permute-done.3.far_ref
  17.1 2.1 %image_late.1 = (f32[4,64,1024]{2,1,0:T(8,128)S(1)}, f32[4,16,1024]{2,1,0:T(8,128)S(1)}, f32[8,128]{1,0:T(8,128)S(1)}) custom-call(s32[1]{0:T(128)} %bitcast.odd_ref.after_ref, s32[1]{0:T(128)} %bitcast.3.more_ref, f32[4,64,1024]{2,1,0:T(8,128)S(1)} %copy-done.1, f32[4,32,1024]{2,1,0:T(8,128)S(1)} %collective-permute-done.3.far_ref, ...), custom_call_target="tpu_custom_call" | custom-call | flops 2000000000 | bytes 1048576 | tf_op jit(solution)/shard_map/image_late/pallas_call | solution.py:259
  19.2 0.0 collective-permute-done.4.near_ref
  19.2 0.0 copy-start.4
  19.2 2.8 %early.5.h_in_ref = f32[4,48,1024]{2,1,0:T(8,128)S(1)} custom-call(s32[1]{0:T(128)} %bitcast.odd_ref.after_ref, f32[4,64,1024]{2,1,0:T(8,128)S(1)} %get-tuple-element.35.v_ref.f_ref, f32[4,16,1024]{2,1,0:T(8,128)S(1)} %collective-permute-done.4.near_ref, bf16[4,192,256]{2,1,0:T(8,128)(2,1)S(1)} %get-tuple-element.25.r_ref, ...), custom_call_target="tpu_custom_call" | custom-call | flops 2800000000 | bytes 1048576 | tf_op jit(solution)/shard_map/early/pallas_call | solution.py:203
  22.0 0.0 collective-permute-done.2.res_far_ref
  22.0 2.7 %last_late.1 = (f32[4,64,1024]{2,1,0:T(8,128)S(1)}, f32[4,64,1024]{2,1,0:T(8,128)S(1)}, f32[8,128]{1,0:T(8,128)S(1)}) custom-call(s32[1]{0:T(128)} %bitcast.odd_ref.after_ref, f32[1]{0:T(128)S(6)} %copy.11.damp_ref, f32[4,64,1024]{2,1,0:T(8,128)S(1)} %copy-done.2, f32[4,16,1024]{2,1,0:T(8,128)S(1)} %collective-permute-done.2.res_far_ref, ...), custom_call_target="tpu_custom_call" | custom-call | flops 2600000000 | bytes 1048576 | tf_op jit(solution)/shard_map/last_late/pallas_call | solution.py:298
  24.8 5.7 %collective-permute-start.5 = (f32[8,128]{1,0:T(8,128)S(1)}, f32[8,128]{1,0:T(8,128)S(1)}, u32[]{:S(2)}, u32[]{:S(2)}) collective-permute-start(f32[8,128]{1,0:T(8,128)S(1)} %get-tuple-element.39), channel_id=1, source_target_pairs={{0,8},{1,9},{2,10},{3,11},{4,12},{5,13},{6,14},{7,15},{8,0},{9,1},... | collective-permute-start | bytes 12296 | tf_op jit(solution)/shard_map/ppermute | solution.py:351
  30.5 1.6 %collective-permute-done.5 = f32[8,128]{1,0:T(8,128)S(1)} collective-permute-done((f32[8,128]{1,0:T(8,128)S(1)}, f32[8,128]{1,0:T(8,128)S(1)}, u32[]{:S(2)}, u32[]{:S(2)}) %collective-permute-start.5) | collective-permute-done | bytes 4128 | tf_op jit(solution)/shard_map/ppermute | solution.py:351
  32.1 1.9 %collective-permute-start.6 = (f32[8,128]{1,0:T(8,128)S(1)}, f32[8,128]{1,0:T(8,128)S(1)}, u32[]{:S(2)}, u32[]{:S(2)}) collective-permute-start(f32[8,128]{1,0:T(8,128)S(1)} %add.26), channel_id=1, source_target_pairs={{0,4},{1,5},{2,6},{3,7},{4,0},{5,1},{6,2},{7,3},{8,12},{9,13},{10,... | collective-permute-start | bytes 12296 | tf_op jit(solution)/shard_map/ppermute | solution.py:351
  34.0 1.7 %collective-permute-done.6 = f32[8,128]{1,0:T(8,128)S(1)} collective-permute-done((f32[8,128]{1,0:T(8,128)S(1)}, f32[8,128]{1,0:T(8,128)S(1)}, u32[]{:S(2)}, u32[]{:S(2)}) %collective-permute-start.6) | collective-permute-done | bytes 4128 | tf_op jit(solution)/shard_map/ppermute | solution.py:351
  35.7 3.5 %collective-permute-start.7 = (f32[8,128]{1,0:T(8,128)S(1)}, f32[8,128]{1,0:T(8,128)S(1)}, u32[]{:S(2)}, u32[]{:S(2)}) collective-permute-start(f32[8,128]{1,0:T(8,128)S(1)} %add.27), channel_id=1, source_target_pairs={{0,2},{1,3},{2,0},{3,1},{4,6},{5,7},{6,4},{7,5},{8,10},{9,11},{10,... | collective-permute-start | bytes 12296 | tf_op jit(solution)/shard_map/ppermute | solution.py:351
  39.1 1.6 %collective-permute-done.7 = f32[8,128]{1,0:T(8,128)S(1)} collective-permute-done((f32[8,128]{1,0:T(8,128)S(1)}, f32[8,128]{1,0:T(8,128)S(1)}, u32[]{:S(2)}, u32[]{:S(2)}) %collective-permute-start.7) | collective-permute-done | bytes 4128 | tf_op jit(solution)/shard_map/ppermute | solution.py:351
  40.7 0.0 collective-permute-start.8
  40.7 1.2 %collective-permute-done.8.other_ref = f32[8,128]{1,0:T(8,128)S(1)} collective-permute-done((f32[8,128]{1,0:T(8,128)S(1)}, f32[8,128]{1,0:T(8,128)S(1)}, u32[]{:S(2)}, u32[]{:S(2)}) %collective-permute-start.8) | collective-permute-done | bytes 4128 | tf_op jit(solution)/shard_map/ppermute | solution.py:351
  41.9 2.3 %final.1 = (f32[4,64,1024]{2,1,0:T(8,128)}, f32[4,64,1024]{2,1,0:T(8,128)}, f32[4,64,1024]{2,1,0:T(8,128)}, f32[4,64,1024]{2,1,0:T(8,128)}) custom-call(f32[1]{0:T(128)S(6)} %copy.11.damp_ref, f32[8,128]{1,0:T(8,128)S(1)} %add.28.mine_ref, f32[8,128]{1,0:T(8,128)S(1)} %collective-permute-done.8.other_ref, f32[4,64,1024]{2,1,0:T(8,128)S(1)} %copy-done.4, ...), custom_call_target="tpu_custom_call" | custom-call | flops 2000000000 | bytes 1048576 | tf_op jit(solution)/shard_map/final/pallas_call | solution.py:338
  (13 shorter events, 0.1 us)
Async XLA Ops:
  0.6 4.3 %copy-start.5 = (f32[4,4,31]{2,1,0:T(4,128)S(1)}, f32[4,4,31]{2,1,0:T(4,128)}, u32[]{:S(2)}) copy-start(f32[4,4,31]{2,1,0:T(4,128)} %param.11) | copy-start | bytes 5956
  0.6 4.3 %copy-start.6 = (f32[4,4,31]{2,1,0:T(4,128)S(1)}, f32[4,4,31]{2,1,0:T(4,128)}, u32[]{:S(2)}) copy-start(f32[4,4,31]{2,1,0:T(4,128)} %param.12) | copy-start | bytes 5956
  0.7 1.2 %copy-start = (f32[4,64,1024]{2,1,0:T(8,128)S(1)}, f32[4,64,1024]{2,1,0:T(8,128)}, u32[]{:S(2)}) copy-start(f32[4,64,1024]{2,1,0:T(8,128)} %p_ref.5) | copy-start | bytes 3145732
  1.9 3.1 %copy-start.1 = (f32[4,64,1024]{2,1,0:T(8,128)S(1)}, f32[4,64,1024]{2,1,0:T(8,128)}, u32[]{:S(2)}) copy-start(f32[4,64,1024]{2,1,0:T(8,128)} %p_ref.5) | copy-start | bytes 3145732
  2.0 4.4 %collective-permute-start = (f32[4,16,1024]{2,1,0:T(8,128)S(1)}, f32[4,16,1024]{2,1,0:T(8,128)S(1)}, u32[]{:S(2)}, u32[]{:S(2)}) collective-permute-start(f32[4,16,1024]{2,1,0:T(8,128)S(1)} %get-tuple-element.23), channel_id=1, source_target_pairs={{0,1},{1,0},{2,3},{3,2},{4,5},{5,4},{6,7},{7,6},{8,9},{9,8},{10,11... | collective-permute-start | bytes 786440 | tf_op jit(solution)/shard_map/ppermute | solution.py:351
  2.5 14.6 %collective-permute-start.3 = (f32[4,32,1024]{2,1,0:T(8,128)S(1)}, f32[4,32,1024]{2,1,0:T(8,128)S(1)}, u32[]{:S(2)}, u32[]{:S(2)}) collective-permute-start(f32[4,32,1024]{2,1,0:T(8,128)S(1)} %get-tuple-element.29), channel_id=1, source_target_pairs={{1,2},{2,1},{3,4},{4,3},{5,6},{6,5},{7,8},{8,7},{9,10},{10,9},{11,... | collective-permute-start | bytes 1572872 | tf_op jit(solution)/shard_map/ppermute | solution.py:367
  6.3 7.0 %collective-permute-start.1 = (f32[4,16,1024]{2,1,0:T(8,128)S(1)}, f32[4,16,1024]{2,1,0:T(8,128)S(1)}, u32[]{:S(2)}, u32[]{:S(2)}) collective-permute-start(f32[4,16,1024]{2,1,0:T(8,128)S(1)} %get-tuple-element.24), channel_id=1, source_target_pairs={{0,1},{1,0},{2,3},{3,2},{4,5},{5,4},{6,7},{7,6},{8,9},{9,8},{10,11... | collective-permute-start | bytes 786440 | tf_op jit(solution)/shard_map/ppermute | solution.py:351
  10.4 2.9 %copy-start.2 = (f32[4,64,1024]{2,1,0:T(8,128)S(1)}, f32[4,64,1024]{2,1,0:T(8,128)}, u32[]{:S(2)}) copy-start(f32[4,64,1024]{2,1,0:T(8,128)} %r_ref.1) | copy-start | bytes 3145732
  13.3 5.9 %collective-permute-start.4 = (f32[4,16,1024]{2,1,0:T(8,128)S(1)}, f32[4,16,1024]{2,1,0:T(8,128)S(1)}, u32[]{:S(2)}, u32[]{:S(2)}) collective-permute-start(f32[4,16,1024]{2,1,0:T(8,128)S(1)} %constant_dynamic-slice_fusion), channel_id=1, source_target_pairs={{0,1},{1,0},{2,3},{3,2},{4,5},{5,4},{6,7},{7,6},{8,9},{9,8},{10,11... | collective-permute-start | bytes 786440 | tf_op jit(solution)/shard_map/ppermute | solution.py:351
  13.4 3.7 %copy-start.3 = (f32[4,64,1024]{2,1,0:T(8,128)S(1)}, f32[4,64,1024]{2,1,0:T(8,128)}, u32[]{:S(2)}) copy-start(f32[4,64,1024]{2,1,0:T(8,128)} %grad_ref.1) | copy-start | bytes 3145732
  16.2 5.8 %collective-permute-start.2 = (f32[4,16,1024]{2,1,0:T(8,128)S(1)}, f32[4,16,1024]{2,1,0:T(8,128)S(1)}, u32[]{:S(2)}, u32[]{:S(2)}) collective-permute-start(f32[4,16,1024]{2,1,0:T(8,128)S(1)} %get-tuple-element.27), channel_id=1, source_target_pairs={{1,2},{2,1},{3,4},{4,3},{5,6},{6,5},{7,8},{8,7},{9,10},{10,9},{11,... | collective-permute-start | bytes 786440 | tf_op jit(solution)/shard_map/ppermute | solution.py:367
  19.2 2.8 %copy-start.4 = (f32[4,64,1024]{2,1,0:T(8,128)S(1)}, f32[4,64,1024]{2,1,0:T(8,128)}, u32[]{:S(2)}) copy-start(f32[4,64,1024]{2,1,0:T(8,128)} %x_ref.3) | copy-start | bytes 3145732
  24.8 7.3 %collective-permute-start.5 = (f32[8,128]{1,0:T(8,128)S(1)}, f32[8,128]{1,0:T(8,128)S(1)}, u32[]{:S(2)}, u32[]{:S(2)}) collective-permute-start(f32[8,128]{1,0:T(8,128)S(1)} %get-tuple-element.39), channel_id=1, source_target_pairs={{0,8},{1,9},{2,10},{3,11},{4,12},{5,13},{6,14},{7,15},{8,0},{9,1},... | collective-permute-start | bytes 12296 | tf_op jit(solution)/shard_map/ppermute | solution.py:351
  32.1 3.6 %collective-permute-start.6 = (f32[8,128]{1,0:T(8,128)S(1)}, f32[8,128]{1,0:T(8,128)S(1)}, u32[]{:S(2)}, u32[]{:S(2)}) collective-permute-start(f32[8,128]{1,0:T(8,128)S(1)} %add.26), channel_id=1, source_target_pairs={{0,4},{1,5},{2,6},{3,7},{4,0},{5,1},{6,2},{7,3},{8,12},{9,13},{10,... | collective-permute-start | bytes 12296 | tf_op jit(solution)/shard_map/ppermute | solution.py:351
  35.7 5.1 %collective-permute-start.7 = (f32[8,128]{1,0:T(8,128)S(1)}, f32[8,128]{1,0:T(8,128)S(1)}, u32[]{:S(2)}, u32[]{:S(2)}) collective-permute-start(f32[8,128]{1,0:T(8,128)S(1)} %add.27), channel_id=1, source_target_pairs={{0,2},{1,3},{2,0},{3,1},{4,6},{5,7},{6,4},{7,5},{8,10},{9,11},{10,... | collective-permute-start | bytes 12296 | tf_op jit(solution)/shard_map/ppermute | solution.py:351
  40.7 1.2 %collective-permute-start.8 = (f32[8,128]{1,0:T(8,128)S(1)}, f32[8,128]{1,0:T(8,128)S(1)}, u32[]{:S(2)}, u32[]{:S(2)}) collective-permute-start(f32[8,128]{1,0:T(8,128)S(1)} %add.28.mine_ref), channel_id=1, source_target_pairs={{0,1},{1,0},{2,3},{3,2},{4,5},{5,4},{6,7},{7,6},{8,9},{9,8},{10,11... | collective-permute-start | bytes 12296 | tf_op jit(solution)/shard_map/ppermute | solution.py:351

commit v6 on v5

--- a/solution.py
+++ b/solution.py
@@ -389,10 +389,11 @@
     step = 1
     while 2 * step < peers:
         step *= 2
-    while step > 1:
+    rounds = [step >> k for k in range(step.bit_length())]
+    rounds[:2] = rounds[1::-1]
+    for step in rounds[:-1]:
         sums = sums + swap(sums, "lat", step)
-        step //= 2
-    other = swap(sums, "lat", step)
+    other = swap(sums, "lat", rounds[-1])
     return final(damping, sums, other, solution, residual, direction, image, g, h)
 
 

time: 44.5 us -> 44.5 us (level)
  no operation moved by 1% of the time
where the time goes in v6:
time: 44.5 us; the launch traced here: 44.4 us
  starting transfers between devices  17.4 us (39%)
  Pallas kernels  17 us (38%)
  waiting for transfers between devices  5.93 us (13%)
  local copies, waits for them, and re-layouts  2.35 us (5%)
  between operations  1.68 us (4%)
    ppermute x7, starting transfers between devices, swap(): lax.ppermute(values, axis, [(i, i ^ step) for i in range(lax.axis_size(ax...  15.9 us
    pallas_call x3, Pallas kernels, early(): pl.pallas_call(functools.partial(early_kernel, border), out_shape=f32(dep...  8.41 us
    ppermute x7, waiting for transfers between devices, swap(): lax.ppermute(values, axis, [(i, i ^ step) for i in range(lax.axis_size(ax...  5.93 us
    pallas_call x1, Pallas kernels, last_late(): pl.pallas_call(functools.partial(last_kernel, border), out_shape=(f32(dep...  2.75 us
    pallas_call x1, Pallas kernels, final(): pl.pallas_call(final_kernel, out_shape=(f32(*shape),) * 4, in_specs=[SM]...  2.29 us
    pallas_call x1, Pallas kernels, image_late(): pl.pallas_call(functools.partial(image_kernel, border), out_shape=(f32(de...  2.1 us
    ppermute x2, starting transfers between devices, far_swap(): return lax.ppermute(v, 'lat', far_pairs)  1.54 us
    pallas_call x1, Pallas kernels, prep(): pl.pallas_call(functools.partial(prep_kernel, depth, inner), out_shape=ba...  1.36 us
  transfers between devices with their start and end apart: 9, of which 4 were waited for; matrix products, arithmetic and copies ran while one was open for 2% of the time, Pallas kernels for 27%

profile of v6, /device:TPU:0, one launch (start us, length us, event | category | flops | bytes accessed | tf_op | source)
XLA Modules:
  0.0 44.4 jit_solution(5934313087992239653)
XLA Ops:
  0.6 0.0 copy-start.5
  0.6 0.0 copy-start.6
  0.7 0.0 copy-start
  0.7 1.2 %copy-done = f32[4,64,1024]{2,1,0:T(8,128)S(1)} copy-done((f32[4,64,1024]{2,1,0:T(8,128)S(1)}, f32[4,64,1024]{2,1,0:T(8,128)}, u32[]{:S(2)}) %copy-start) | copy-done | bytes 1048600
  1.9 0.1 edges.1
  2.0 0.5 %collective-permute-start = (f32[4,16,1024]{2,1,0:T(8,128)S(1)}, f32[4,16,1024]{2,1,0:T(8,128)S(1)}, u32[]{:S(2)}, u32[]{:S(2)}) collective-permute-start(f32[4,16,1024]{2,1,0:T(8,128)S(1)} %get-tuple-element.23), channel_id=1, source_target_pairs={{0,1},{1,0},{2,3},{3,2},{4,5},{5,4},{6,7},{7,6},{8,9},{9,8},{10,11... | collective-permute-start | bytes 786440 | tf_op jit(solution)/shard_map/ppermute | solution.py:351
  2.5 0.7 %collective-permute-start.3 = (f32[4,32,1024]{2,1,0:T(8,128)S(1)}, f32[4,32,1024]{2,1,0:T(8,128)S(1)}, u32[]{:S(2)}, u32[]{:S(2)}) collective-permute-start(f32[4,32,1024]{2,1,0:T(8,128)S(1)} %get-tuple-element.29), channel_id=1, source_target_pairs={{1,2},{2,1},{3,4},{4,3},{5,6},{6,5},{7,8},{8,7},{9,10},{10,9},{11,... | collective-permute-start | bytes 1572872 | tf_op jit(solution)/shard_map/ppermute | solution.py:367
  3.9 1.1 %constant_dynamic-slice_fusion.1 = (f32[4,16,1024]{2,1,0:T(8,128)S(1)}, f32[4,16,1024]{2,1,0:T(8,128)S(1)}) fusion(f32[4,64,1024]{2,1,0:T(8,128)} %r_ref.1, s32[]{:T(128)S(6)} %select_n.22, s32[]{:T(128)S(6)} %select_n.21), kind=kLoop, calls=%fused_computation.1 | loop fusion | bytes 1048584 | tf_op jit(solution)/shard_map/dynamic_slice | solution.py:376
  5.0 1.4 %prep.1 = (bf16[4,192,256]{2,1,0:T(8,128)(2,1)S(1)}, bf16[4,128,256]{2,1,0:T(8,128)(2,1)S(1)}, bf16[4,1024,256]{2,1,0:T(8,128)(2,1)S(1)}, bf16[4,192,256]{2,1,0:...) custom-call(f32[16,31]{1,0:T(8,128)S(1)} %bitcast.4, ...), custom_call_target="tpu_custom_call" | custom-call | flops 1500000000 | bytes 1048576 | tf_op jit(solution)/shard_map/prep/pallas_call | solution.py:130
  6.3 0.0 collective-permute-done.near_ref
  6.3 4.1 %collective-permute-start.1 = (f32[4,16,1024]{2,1,0:T(8,128)S(1)}, f32[4,16,1024]{2,1,0:T(8,128)S(1)}, u32[]{:S(2)}, u32[]{:S(2)}) collective-permute-start(f32[4,16,1024]{2,1,0:T(8,128)S(1)} %get-tuple-element.24), channel_id=1, source_target_pairs={{0,1},{1,0},{2,3},{3,2},{4,5},{5,4},{6,7},{7,6},{8,9},{9,8},{10,11... | collective-permute-start | bytes 786440 | tf_op jit(solution)/shard_map/ppermute | solution.py:351
  10.4 2.8 %early.4.in_ref = f32[4,48,1024]{2,1,0:T(8,128)S(1)} custom-call(s32[1]{0:T(128)} %bitcast.odd_ref.after_ref, f32[4,64,1024]{2,1,0:T(8,128)S(1)} %copy-done.1, f32[4,16,1024]{2,1,0:T(8,128)S(1)} %collective-permute-done.near_ref, bf16[4,192,256]{2,1,0:T(8,128)(2,1)S(1)} %get-tuple-element.33.r_ref, bf16[4,1024,256]{2,1,0:T(8,128)(2,1)S(1)} %get-tuple-element.31.c_ref), custom_call_target="tpu_custom_call" | custom-call | flops 2800000000 | bytes 1048576 | tf_op jit(solution)/shard_map/early/pallas_call | solution.py:203
  13.3 0.1 collective-permute-start.4
  13.4 0.0 collective-permute-done.1.near_ref
  13.4 2.8 %early.3.after_ref.g_in_ref = f32[4,48,1024]{2,1,0:T(8,128)S(1)} custom-call(s32[1]{0:T(128)} %bitcast.odd_ref.after_ref, f32[4,64,1024]{2,1,0:T(8,128)S(1)} %copy-done.2, f32[4,16,1024]{2,1,0:T(8,128)S(1)} %collective-permute-done.1.near_ref, bf16[4,192,256]{2,1,0:T(8,128)(2,1)S(1)} %get-tuple-element.25.r_ref, ...), custom_call_target="tpu_custom_call" | custom-call | flops 2800000000 | bytes 1048576 | tf_op jit(solution)/shard_map/early/pallas_call | solution.py:203
  16.2 0.9 %collective-permute-start.2 = (f32[4,16,1024]{2,1,0:T(8,128)S(1)}, f32[4,16,1024]{2,1,0:T(8,128)S(1)}, u32[]{:S(2)}, u32[]{:S(2)}) collective-permute-start(f32[4,16,1024]{2,1,0:T(8,128)S(1)} %get-tuple-element.27), channel_id=1, source_target_pairs={{1,2},{2,1},{3,4},{4,3},{5,6},{6,5},{7,8},{8,7},{9,10},{10,9},{11,... | collective-permute-start | bytes 786440 | tf_op jit(solution)/shard_map/ppermute | solution.py:367
  17.1 0.0 collective-permute-done.3.far_ref
  17.1 2.1 %image_late.1 = (f32[4,64,1024]{2,1,0:T(8,128)S(1)}, f32[4,16,1024]{2,1,0:T(8,128)S(1)}, f32[8,128]{1,0:T(8,128)S(1)}) custom-call(s32[1]{0:T(128)} %bitcast.odd_ref.after_ref, s32[1]{0:T(128)} %bitcast.3.more_ref, f32[4,64,1024]{2,1,0:T(8,128)S(1)} %copy-done.1, f32[4,32,1024]{2,1,0:T(8,128)S(1)} %collective-permute-done.3.far_ref, ...), custom_call_target="tpu_custom_call" | custom-call | flops 2000000000 | bytes 1048576 | tf_op jit(solution)/shard_map/image_late/pallas_call | solution.py:259
  19.2 0.0 collective-permute-done.4.near_ref
  19.2 0.0 copy-start.4
  19.2 2.8 %early.5.h_in_ref = f32[4,48,1024]{2,1,0:T(8,128)S(1)} custom-call(s32[1]{0:T(128)} %bitcast.odd_ref.after_ref, f32[4,64,1024]{2,1,0:T(8,128)S(1)} %get-tuple-element.35.v_ref.f_ref, f32[4,16,1024]{2,1,0:T(8,128)S(1)} %collective-permute-done.4.near_ref, bf16[4,192,256]{2,1,0:T(8,128)(2,1)S(1)} %get-tuple-element.25.r_ref, ...), custom_call_target="tpu_custom_call" | custom-call | flops 2800000000 | bytes 1048576 | tf_op jit(solution)/shard_map/early/pallas_call | solution.py:203
  22.0 0.0 collective-permute-done.2.res_far_ref
  22.0 2.7 %last_late.1 = (f32[4,64,1024]{2,1,0:T(8,128)S(1)}, f32[4,64,1024]{2,1,0:T(8,128)S(1)}, f32[8,128]{1,0:T(8,128)S(1)}) custom-call(s32[1]{0:T(128)} %bitcast.odd_ref.after_ref, f32[1]{0:T(128)S(6)} %copy.11.damp_ref, f32[4,64,1024]{2,1,0:T(8,128)S(1)} %copy-done.2, f32[4,16,1024]{2,1,0:T(8,128)S(1)} %collective-permute-done.2.res_far_ref, ...), custom_call_target="tpu_custom_call" | custom-call | flops 2600000000 | bytes 1048576 | tf_op jit(solution)/shard_map/last_late/pallas_call | solution.py:298
  24.8 4.7 %collective-permute-start.5 = (f32[8,128]{1,0:T(8,128)S(1)}, f32[8,128]{1,0:T(8,128)S(1)}, u32[]{:S(2)}, u32[]{:S(2)}) collective-permute-start(f32[8,128]{1,0:T(8,128)S(1)} %get-tuple-element.39), channel_id=1, source_target_pairs={{0,4},{1,5},{2,6},{3,7},{4,0},{5,1},{6,2},{7,3},{8,12},{9,13},{10,... | collective-permute-start | bytes 12296 | tf_op jit(solution)/shard_map/ppermute | solution.py:351
  29.5 1.6 %collective-permute-done.5 = f32[8,128]{1,0:T(8,128)S(1)} collective-permute-done((f32[8,128]{1,0:T(8,128)S(1)}, f32[8,128]{1,0:T(8,128)S(1)}, u32[]{:S(2)}, u32[]{:S(2)}) %collective-permute-start.5) | collective-permute-done | bytes 4128 | tf_op jit(solution)/shard_map/ppermute | solution.py:351
  31.0 3.0 %collective-permute-start.6 = (f32[8,128]{1,0:T(8,128)S(1)}, f32[8,128]{1,0:T(8,128)S(1)}, u32[]{:S(2)}, u32[]{:S(2)}) collective-permute-start(f32[8,128]{1,0:T(8,128)S(1)} %add.26), channel_id=1, source_target_pairs={{0,8},{1,9},{2,10},{3,11},{4,12},{5,13},{6,14},{7,15},{8,0},{9,1},... | collective-permute-start | bytes 12296 | tf_op jit(solution)/shard_map/ppermute | solution.py:351
  34.1 1.6 %collective-permute-done.6 = f32[8,128]{1,0:T(8,128)S(1)} collective-permute-done((f32[8,128]{1,0:T(8,128)S(1)}, f32[8,128]{1,0:T(8,128)S(1)}, u32[]{:S(2)}, u32[]{:S(2)}) %collective-permute-start.6) | collective-permute-done | bytes 4128 | tf_op jit(solution)/shard_map/ppermute | solution.py:351
  35.7 3.5 %collective-permute-start.7 = (f32[8,128]{1,0:T(8,128)S(1)}, f32[8,128]{1,0:T(8,128)S(1)}, u32[]{:S(2)}, u32[]{:S(2)}) collective-permute-start(f32[8,128]{1,0:T(8,128)S(1)} %add.27), channel_id=1, source_target_pairs={{0,2},{1,3},{2,0},{3,1},{4,6},{5,7},{6,4},{7,5},{8,10},{9,11},{10,... | collective-permute-start | bytes 12296 | tf_op jit(solution)/shard_map/ppermute | solution.py:351
  39.1 1.6 %collective-permute-done.7 = f32[8,128]{1,0:T(8,128)S(1)} collective-permute-done((f32[8,128]{1,0:T(8,128)S(1)}, f32[8,128]{1,0:T(8,128)S(1)}, u32[]{:S(2)}, u32[]{:S(2)}) %collective-permute-start.7) | collective-permute-done | bytes 4128 | tf_op jit(solution)/shard_map/ppermute | solution.py:351
  40.7 0.0 collective-permute-start.8
  40.7 1.2 %collective-permute-done.8.other_ref = f32[8,128]{1,0:T(8,128)S(1)} collective-permute-done((f32[8,128]{1,0:T(8,128)S(1)}, f32[8,128]{1,0:T(8,128)S(1)}, u32[]{:S(2)}, u32[]{:S(2)}) %collective-permute-start.8) | collective-permute-done | bytes 4128 | tf_op jit(solution)/shard_map/ppermute | solution.py:351
  41.9 2.3 %final.1 = (f32[4,64,1024]{2,1,0:T(8,128)}, f32[4,64,1024]{2,1,0:T(8,128)}, f32[4,64,1024]{2,1,0:T(8,128)}, f32[4,64,1024]{2,1,0:T(8,128)}) custom-call(f32[1]{0:T(128)S(6)} %copy.11.damp_ref, f32[8,128]{1,0:T(8,128)S(1)} %add.28.mine_ref, f32[8,128]{1,0:T(8,128)S(1)} %collective-permute-done.8.other_ref, f32[4,64,1024]{2,1,0:T(8,128)S(1)} %copy-done.4, ...), custom_call_target="tpu_custom_call" | custom-call | flops 2000000000 | bytes 1048576 | tf_op jit(solution)/shard_map/final/pallas_call | solution.py:338
  (13 shorter events, 0.1 us)
Async XLA Ops:
  0.6 4.3 %copy-start.5 = (f32[4,4,31]{2,1,0:T(4,128)S(1)}, f32[4,4,31]{2,1,0:T(4,128)}, u32[]{:S(2)}) copy-start(f32[4,4,31]{2,1,0:T(4,128)} %param.11) | copy-start | bytes 5956
  0.6 4.3 %copy-start.6 = (f32[4,4,31]{2,1,0:T(4,128)S(1)}, f32[4,4,31]{2,1,0:T(4,128)}, u32[]{:S(2)}) copy-start(f32[4,4,31]{2,1,0:T(4,128)} %param.12) | copy-start | bytes 5956
  0.7 1.2 %copy-start = (f32[4,64,1024]{2,1,0:T(8,128)S(1)}, f32[4,64,1024]{2,1,0:T(8,128)}, u32[]{:S(2)}) copy-start(f32[4,64,1024]{2,1,0:T(8,128)} %p_ref.5) | copy-start | bytes 3145732
  1.9 3.1 %copy-start.1 = (f32[4,64,1024]{2,1,0:T(8,128)S(1)}, f32[4,64,1024]{2,1,0:T(8,128)}, u32[]{:S(2)}) copy-start(f32[4,64,1024]{2,1,0:T(8,128)} %p_ref.5) | copy-start | bytes 3145732
  2.0 4.4 %collective-permute-start = (f32[4,16,1024]{2,1,0:T(8,128)S(1)}, f32[4,16,1024]{2,1,0:T(8,128)S(1)}, u32[]{:S(2)}, u32[]{:S(2)}) collective-permute-start(f32[4,16,1024]{2,1,0:T(8,128)S(1)} %get-tuple-element.23), channel_id=1, source_target_pairs={{0,1},{1,0},{2,3},{3,2},{4,5},{5,4},{6,7},{7,6},{8,9},{9,8},{10,11... | collective-permute-start | bytes 786440 | tf_op jit(solution)/shard_map/ppermute | solution.py:351
  2.5 14.6 %collective-permute-start.3 = (f32[4,32,1024]{2,1,0:T(8,128)S(1)}, f32[4,32,1024]{2,1,0:T(8,128)S(1)}, u32[]{:S(2)}, u32[]{:S(2)}) collective-permute-start(f32[4,32,1024]{2,1,0:T(8,128)S(1)} %get-tuple-element.29), channel_id=1, source_target_pairs={{1,2},{2,1},{3,4},{4,3},{5,6},{6,5},{7,8},{8,7},{9,10},{10,9},{11,... | collective-permute-start | bytes 1572872 | tf_op jit(solution)/shard_map/ppermute | solution.py:367
  6.3 7.0 %collective-permute-start.1 = (f32[4,16,1024]{2,1,0:T(8,128)S(1)}, f32[4,16,1024]{2,1,0:T(8,128)S(1)}, u32[]{:S(2)}, u32[]{:S(2)}) collective-permute-start(f32[4,16,1024]{2,1,0:T(8,128)S(1)} %get-tuple-element.24), channel_id=1, source_target_pairs={{0,1},{1,0},{2,3},{3,2},{4,5},{5,4},{6,7},{7,6},{8,9},{9,8},{10,11... | collective-permute-start | bytes 786440 | tf_op jit(solution)/shard_map/ppermute | solution.py:351
  10.4 2.9 %copy-start.2 = (f32[4,64,1024]{2,1,0:T(8,128)S(1)}, f32[4,64,1024]{2,1,0:T(8,128)}, u32[]{:S(2)}) copy-start(f32[4,64,1024]{2,1,0:T(8,128)} %r_ref.1) | copy-start | bytes 3145732
  13.3 5.9 %collective-permute-start.4 = (f32[4,16,1024]{2,1,0:T(8,128)S(1)}, f32[4,16,1024]{2,1,0:T(8,128)S(1)}, u32[]{:S(2)}, u32[]{:S(2)}) collective-permute-start(f32[4,16,1024]{2,1,0:T(8,128)S(1)} %constant_dynamic-slice_fusion), channel_id=1, source_target_pairs={{0,1},{1,0},{2,3},{3,2},{4,5},{5,4},{6,7},{7,6},{8,9},{9,8},{10,11... | collective-permute-start | bytes 786440 | tf_op jit(solution)/shard_map/ppermute | solution.py:351
  13.4 3.7 %copy-start.3 = (f32[4,64,1024]{2,1,0:T(8,128)S(1)}, f32[4,64,1024]{2,1,0:T(8,128)}, u32[]{:S(2)}) copy-start(f32[4,64,1024]{2,1,0:T(8,128)} %grad_ref.1) | copy-start | bytes 3145732
  16.2 5.8 %collective-permute-start.2 = (f32[4,16,1024]{2,1,0:T(8,128)S(1)}, f32[4,16,1024]{2,1,0:T(8,128)S(1)}, u32[]{:S(2)}, u32[]{:S(2)}) collective-permute-start(f32[4,16,1024]{2,1,0:T(8,128)S(1)} %get-tuple-element.27), channel_id=1, source_target_pairs={{1,2},{2,1},{3,4},{4,3},{5,6},{6,5},{7,8},{8,7},{9,10},{10,9},{11,... | collective-permute-start | bytes 786440 | tf_op jit(solution)/shard_map/ppermute | solution.py:367
  19.2 2.8 %copy-start.4 = (f32[4,64,1024]{2,1,0:T(8,128)S(1)}, f32[4,64,1024]{2,1,0:T(8,128)}, u32[]{:S(2)}) copy-start(f32[4,64,1024]{2,1,0:T(8,128)} %x_ref.3) | copy-start | bytes 3145732
  24.8 6.3 %collective-permute-start.5 = (f32[8,128]{1,0:T(8,128)S(1)}, f32[8,128]{1,0:T(8,128)S(1)}, u32[]{:S(2)}, u32[]{:S(2)}) collective-permute-start(f32[8,128]{1,0:T(8,128)S(1)} %get-tuple-element.39), channel_id=1, source_target_pairs={{0,4},{1,5},{2,6},{3,7},{4,0},{5,1},{6,2},{7,3},{8,12},{9,13},{10,... | collective-permute-start | bytes 12296 | tf_op jit(solution)/shard_map/ppermute | solution.py:351
  31.0 4.6 %collective-permute-start.6 = (f32[8,128]{1,0:T(8,128)S(1)}, f32[8,128]{1,0:T(8,128)S(1)}, u32[]{:S(2)}, u32[]{:S(2)}) collective-permute-start(f32[8,128]{1,0:T(8,128)S(1)} %add.26), channel_id=1, source_target_pairs={{0,8},{1,9},{2,10},{3,11},{4,12},{5,13},{6,14},{7,15},{8,0},{9,1},... | collective-permute-start | bytes 12296 | tf_op jit(solution)/shard_map/ppermute | solution.py:351
  35.7 5.1 %collective-permute-start.7 = (f32[8,128]{1,0:T(8,128)S(1)}, f32[8,128]{1,0:T(8,128)S(1)}, u32[]{:S(2)}, u32[]{:S(2)}) collective-permute-start(f32[8,128]{1,0:T(8,128)S(1)} %add.27), channel_id=1, source_target_pairs={{0,2},{1,3},{2,0},{3,1},{4,6},{5,7},{6,4},{7,5},{8,10},{9,11},{10,... | collective-permute-start | bytes 12296 | tf_op jit(solution)/shard_map/ppermute | solution.py:351
  40.7 1.2 %collective-permute-start.8 = (f32[8,128]{1,0:T(8,128)S(1)}, f32[8,128]{1,0:T(8,128)S(1)}, u32[]{:S(2)}, u32[]{:S(2)}) collective-permute-start(f32[8,128]{1,0:T(8,128)S(1)} %add.28.mine_ref), channel_id=1, source_target_pairs={{0,1},{1,0},{2,3},{3,2},{4,5},{5,4},{6,7},{7,6},{8,9},{9,8},{10,11... | collective-permute-start | bytes 12296 | tf_op jit(solution)/shard_map/ppermute | solution.py:351
